TPU v7x, 32 devices: a whole 2x2x4 slice. The times are simulated.
32 devices in a mesh: section: 2 (over x), fsdp: 4 (over y, core), rep: 4 (over z).
Axes of the slice: x: 2, y: 2, z: 4, core: 2. Of those that a mesh axis runs over, the one named last changes fastest.
Arguments:
- inputs: bfloat16 [2, 16, 640, 768], P(None, ('fsdp', 'rep')), may hold values from -6 to 6
- cotangent: bfloat16 [2, 16, 640, 768], P(None, ('fsdp', 'rep')), may hold values from -6 to 6
- live_slots: int32 [2, 16], P(None, ('fsdp', 'rep')), may hold values from 0 to 1, as said below
- gain_one: bfloat16 [2, 768], P('section', 'fsdp'), may hold values from 0.5 to 1.5
- shift_one: bfloat16 [2, 768], P('section', 'fsdp'), may hold values from -2 to 2
- project: bfloat16 [2, 768, 2304], P('section', 'fsdp'), may hold values from -0.21875 to 0.21875
- bias_query: bfloat16 [2, 768], P('section', 'fsdp'), may hold values from -3 to 3
- bias_value: bfloat16 [2, 768], P('section', 'fsdp'), may hold values from -2 to 2
- output: bfloat16 [2, 768, 768], P('section', 'fsdp'), may hold values from -3.5 to 3.5
- bias_output: bfloat16 [2, 768], P('section', 'fsdp'), may hold values from -2 to 2
- gain_two: bfloat16 [2, 768], P('section', 'fsdp'), may hold values from 0.5 to 1.5
- shift_two: bfloat16 [2, 768], P('section', 'fsdp'), may hold values from -2 to 2
- expand: bfloat16 [2, 768, 3072], P('section', 'fsdp'), may hold values from -0.21875 to 0.21875
- bias_expand: bfloat16 [2, 3072], P('section', 'fsdp'), may hold values from -3 to 3
- contract: bfloat16 [2, 3072, 768], P('section', 'fsdp'), may hold values from -0.15625 to 0.15625
- bias_contract: bfloat16 [2, 768], P('section', 'fsdp'), may hold values from -2 to 2
Outputs:
- section_outputs: bfloat16 [2, 2, 16, 640, 768], P('section', None, ('fsdp', 'rep'))
- section_input_grads: bfloat16 [2, 2, 16, 640, 768], P('section', None, ('fsdp', 'rep'))
- gain_one_grad: float32 [2, 768], P('section', 'fsdp')
- shift_one_grad: float32 [2, 768], P('section', 'fsdp')
- project_grad: float32 [2, 768, 2304], P('section', 'fsdp')
- bias_query_grad: float32 [2, 768], P('section', 'fsdp')
- bias_value_grad: float32 [2, 768], P('section', 'fsdp')
- output_grad: float32 [2, 768, 768], P('section', 'fsdp')
- bias_output_grad: float32 [2, 768], P('section', 'fsdp')
- gain_two_grad: float32 [2, 768], P('section', 'fsdp')
- shift_two_grad: float32 [2, 768], P('section', 'fsdp')
- expand_grad: float32 [2, 768, 3072], P('section', 'fsdp')
- bias_expand_grad: float32 [2, 3072], P('section', 'fsdp')
- contract_grad: float32 [2, 3072, 768], P('section', 'fsdp')
- bias_contract_grad: float32 [2, 768], P('section', 'fsdp')
Inputs may be any that keep to these rules, and one draw needn't show every extreme that they name: `live_slots`: some micro-batch has all 16 slots live.
All inputs are finite; a program needn't handle non-finite values.
Results may differ from a plain program's by a relative error of at most 0.018.
Values may be sent and summed in bfloat16 or wider, within the bound.
No kernel may reach another device: no remote copies, remote signals or barrier semaphores. Data moves between devices by JAX's collectives and lax.ppermute only.
A program may use at most 448 MiB of HBM per device.

v0:
```python
import math

import jax
import jax.numpy as jnp
from jax import lax
from jax.sharding import PartitionSpec as P

HEADS = 12
HD = 64


epsilon = 1e-05


def shifted(block, axis, distance):
    devices = range(lax.axis_size(axis))
    route = [(i - distance, i) for i in devices if i - distance in devices]
    return lax.ppermute(block, axis, route)


def shortened(shard):

    def short(part):
        return part.astype(jnp.bfloat16) if part.dtype == jnp.float32 else part

    return jax.tree.map(short, shard)


def row_stats(values_in):
    mean_row = jnp.mean(values_in, axis=-1, keepdims=True)
    centered = values_in - mean_row
    factor = lax.rsqrt(jnp.mean(centered * centered, axis=-1, keepdims=True) + epsilon)
    return (centered * factor, factor)


def norm_back(grad_norm, normal, factor):
    first_mean = jnp.mean(grad_norm, axis=-1, keepdims=True)
    second_mean = jnp.mean(grad_norm * normal, axis=-1, keepdims=True)
    return factor * (grad_norm - first_mean - normal * second_mean)


def matmul(left, right):
    return jnp.dot(left, right, preferred_element_type=jnp.float32)


def matmul_left(left, right):
    return lax.dot_general(
        left, right, (((0,), (0,)), ((), ())), preferred_element_type=jnp.float32
    )


def matmul_right(left, right):
    return lax.dot_general(
        left, right, (((1,), (1,)), ((), ())), preferred_element_type=jnp.float32
    )


def row_total(values_in):
    return jnp.sum(values_in.astype(jnp.float32), axis=0)


def attend_forward(items):
    queries, key_rows, value_rows = items
    length, model_width = queries.shape
    query_heads = queries.reshape(length, HEADS, HD)
    key_heads = key_rows.reshape(length, HEADS, HD)
    value_heads = value_rows.reshape(length, HEADS, HD)
    factor = HD ** (-0.5)
    scores = (
        jnp.einsum("qhd,khd->hqk", query_heads, key_heads, preferred_element_type=jnp.float32)
        * factor
    )
    row_max = jnp.max(scores, axis=-1, keepdims=True)
    exponent = jnp.exp(scores - row_max)
    row_sum = jnp.sum(exponent, axis=-1, keepdims=True)
    probs_low = (exponent / row_sum).astype(jnp.bfloat16)
    context = jnp.einsum("hqk,khd->qhd", probs_low, value_heads, preferred_element_type=jnp.float32)
    pieces = [context.reshape(-1, model_width).astype(jnp.bfloat16)]
    log_pieces = [(row_max + jnp.log(row_sum))[..., 0]]
    return (jnp.concatenate(pieces, 0), jnp.concatenate(log_pieces, 1))


def attend_backward(items):
    queries, key_rows, value_rows, log_totals, grad_context = items
    length, model_width = queries.shape
    query_heads = queries.reshape(length, HEADS, HD)
    key_heads = key_rows.reshape(length, HEADS, HD)
    value_heads = value_rows.reshape(length, HEADS, HD)
    grad_heads = grad_context.reshape(length, HEADS, HD)
    factor = HD ** (-0.5)
    scores = (
        jnp.einsum("qhd,khd->hqk", query_heads, key_heads, preferred_element_type=jnp.float32)
        * factor
    )
    probs = jnp.exp(scores - log_totals[..., None])
    grad_values = jnp.einsum(
        "hqk,qhd->khd", probs.astype(jnp.bfloat16), grad_heads, preferred_element_type=jnp.float32
    )
    grad_probs = jnp.einsum(
        "qhd,khd->hqk", grad_heads, value_heads, preferred_element_type=jnp.float32
    )
    inner_sum = jnp.sum(grad_probs * probs, axis=-1, keepdims=True)
    grad_scores = (probs * (grad_probs - inner_sum)).astype(jnp.bfloat16)
    query_pieces = [
        jnp.einsum("hqk,khd->qhd", grad_scores, key_heads, preferred_element_type=jnp.float32)
        * factor
    ]
    grad_keys = (
        jnp.einsum("hqk,qhd->khd", grad_scores, query_heads, preferred_element_type=jnp.float32)
        * factor
    )
    grad_queries = jnp.concatenate(query_pieces, 0)
    return (
        grad_queries.reshape(length, model_width),
        grad_keys.reshape(length, model_width),
        grad_values.reshape(length, model_width),
    )


def layer_forward(layer_weights, block_in):
    (
        gain_one,
        shift_one,
        project,
        bias_query,
        bias_value,
        output,
        bias_output,
        gain_two,
        shift_two,
        expand,
        bias_expand,
        contract,
        bias_contract,
    ) = layer_weights
    clip_count, length, model_width = block_in.shape
    token_rows = block_in.reshape(clip_count * length, model_width).astype(jnp.float32)
    normal_one, factor_one = row_stats(token_rows)
    normed = (normal_one * gain_one + shift_one).astype(jnp.bfloat16)
    projected = matmul(normed, project)
    queries = (projected[:, :model_width] + bias_query).astype(jnp.bfloat16)
    key_rows = projected[:, model_width : 2 * model_width].astype(jnp.bfloat16)
    value_rows = (projected[:, 2 * model_width :] + bias_value).astype(jnp.bfloat16)
    shaped = (
        queries.reshape(clip_count, length, model_width),
        key_rows.reshape(clip_count, length, model_width),
        value_rows.reshape(clip_count, length, model_width),
    )
    context, log_totals = lax.map(attend_forward, shaped)
    context = context.reshape(clip_count * length, model_width)
    hidden = token_rows + (matmul(context, output) + bias_output)
    normal_two, factor_two = row_stats(hidden)
    mixed_rows = (normal_two * gain_two + shift_two).astype(jnp.bfloat16)
    upper_pre = matmul(mixed_rows, expand) + bias_expand
    active = jax.nn.gelu(upper_pre, approximate=False).astype(jnp.bfloat16)
    result = (hidden + (matmul(active, contract) + bias_contract)).astype(jnp.bfloat16)
    kept_items = (block_in, queries, key_rows, value_rows, log_totals, context, hidden, upper_pre)
    return (result.reshape(clip_count, length, model_width), kept_items)


def layer_backward(layer_weights, kept_items, grad_out):
    (
        gain_one,
        shift_one,
        project,
        bias_query,
        bias_value,
        output,
        bias_output,
        gain_two,
        shift_two,
        expand,
        bias_expand,
        contract,
        bias_contract,
    ) = layer_weights
    block_in, queries, key_rows, value_rows, log_totals, context, hidden, upper_pre = kept_items
    clip_count, length, model_width = block_in.shape
    grad_rows = grad_out.reshape(clip_count * length, model_width)
    token_rows = block_in.reshape(clip_count * length, model_width).astype(jnp.float32)
    normal_one, factor_one = row_stats(token_rows)
    normed = (normal_one * gain_one + shift_one).astype(jnp.bfloat16)
    normal_two, factor_two = row_stats(hidden)
    mixed_rows = (normal_two * gain_two + shift_two).astype(jnp.bfloat16)
    active = jax.nn.gelu(upper_pre, approximate=False).astype(jnp.bfloat16)
    grad_low = grad_rows.astype(jnp.bfloat16)
    contract_grad = matmul_left(active, grad_low)
    bias_contract_grad = row_total(grad_low)
    grad_active = matmul_right(grad_low, contract)
    slope = 0.5 * (1.0 + lax.erf(upper_pre / math.sqrt(2.0))) + upper_pre * jnp.exp(
        -0.5 * upper_pre * upper_pre
    ) / math.sqrt(2.0 * math.pi)
    grad_upper = (grad_active * slope).astype(jnp.bfloat16)
    expand_grad = matmul_left(mixed_rows, grad_upper)
    bias_expand_grad = row_total(grad_upper)
    grad_mixed = matmul_right(grad_upper, expand)
    gain_two_grad = jnp.sum(grad_mixed * normal_two, axis=0)
    shift_two_grad = jnp.sum(grad_mixed, axis=0)
    grad_hidden = grad_rows + norm_back(grad_mixed * gain_two, normal_two, factor_two)
    grad_attended = grad_hidden.astype(jnp.bfloat16)
    output_grad = matmul_left(context, grad_attended)
    bias_output_grad = row_total(grad_attended)
    grad_context = matmul_right(grad_attended, output).astype(jnp.bfloat16)
    shaped = (
        queries.reshape(clip_count, length, model_width),
        key_rows.reshape(clip_count, length, model_width),
        value_rows.reshape(clip_count, length, model_width),
        log_totals,
        grad_context.reshape(clip_count, length, model_width),
    )
    grad_queries, grad_keys, grad_values = lax.map(attend_backward, shaped)
    grad_queries = grad_queries.reshape(clip_count * length, model_width).astype(jnp.bfloat16)
    grad_keys = grad_keys.reshape(clip_count * length, model_width).astype(jnp.bfloat16)
    grad_values = grad_values.reshape(clip_count * length, model_width).astype(jnp.bfloat16)
    bias_query_grad = row_total(grad_queries)
    bias_value_grad = row_total(grad_values)
    grad_proj = jnp.concatenate([grad_queries, grad_keys, grad_values], 1)
    project_grad = matmul_left(normed, grad_proj)
    grad_normed = matmul_right(grad_proj, project)
    gain_one_grad = jnp.sum(grad_normed * normal_one, axis=0)
    shift_one_grad = jnp.sum(grad_normed, axis=0)
    grad_in = grad_hidden + norm_back(grad_normed * gain_one, normal_one, factor_one)
    weight_grads = (
        gain_one_grad,
        shift_one_grad,
        project_grad,
        bias_query_grad,
        bias_value_grad,
        output_grad,
        bias_output_grad,
        gain_two_grad,
        shift_two_grad,
        expand_grad,
        bias_expand_grad,
        contract_grad,
        bias_contract_grad,
    )
    return (grad_in.reshape(clip_count, length, model_width).astype(jnp.bfloat16), weight_grads)


def blank_kept(clip_count, length, model_width, hidden_units):
    token_count = clip_count * length
    return (
        jnp.zeros((clip_count, length, model_width), jnp.bfloat16),
        jnp.zeros((token_count, model_width), jnp.bfloat16),
        jnp.zeros((token_count, model_width), jnp.bfloat16),
        jnp.zeros((token_count, model_width), jnp.bfloat16),
        jnp.zeros((clip_count, HEADS, length), jnp.float32),
        jnp.zeros((token_count, model_width), jnp.bfloat16),
        jnp.zeros((token_count, model_width), jnp.float32),
        jnp.zeros((token_count, hidden_units), jnp.float32),
    )


def local(
    inputs,
    cotangent,
    live_slots,
    gain_one,
    shift_one,
    project,
    bias_query,
    bias_value,
    output,
    bias_output,
    gain_two,
    shift_two,
    expand,
    bias_expand,
    contract,
    bias_contract,
):
    shards = (
        gain_one,
        shift_one,
        project,
        bias_query,
        bias_value,
        output,
        bias_output,
        gain_two,
        shift_two,
        expand,
        bias_expand,
        contract,
        bias_contract,
    )
    section_index = lax.axis_index("section")
    micro_count, clip_count, length, model_width = inputs.shape
    hidden_units = bias_expand.shape[1] * lax.axis_size("fsdp")
    live_mask = live_slots.astype(jnp.float32)
    clip_shape = (clip_count, length, model_width)
    stored = tuple(
        (
            jnp.zeros((micro_count + 1,) + item.shape, item.dtype)
            for item in blank_kept(clip_count, length, model_width, hidden_units)
        )
    )
    out_store = jnp.zeros((micro_count + 1,) + clip_shape, jnp.bfloat16)
    back_store = jnp.zeros((micro_count + 1,) + clip_shape, jnp.bfloat16)
    act_in = jnp.zeros(clip_shape, jnp.bfloat16)
    grad_in = jnp.zeros(clip_shape, jnp.bfloat16)
    shares = None
    for moment in range(micro_count + 2):
        gathered = (
            lax.all_gather(shards[0], "fsdp", axis=1, tiled=True),
            lax.all_gather(shards[1], "fsdp", axis=1, tiled=True),
            lax.all_gather(shards[2], "fsdp", axis=1, tiled=True),
            lax.all_gather(shards[3], "fsdp", axis=1, tiled=True),
            lax.all_gather(shards[4], "fsdp", axis=1, tiled=True),
            lax.all_gather(shards[5], "fsdp", axis=1, tiled=True),
            lax.all_gather(shards[6], "fsdp", axis=1, tiled=True),
            lax.all_gather(shards[7], "fsdp", axis=1, tiled=True),
            lax.all_gather(shards[8], "fsdp", axis=1, tiled=True),
            lax.all_gather(shards[9], "fsdp", axis=1, tiled=True),
            lax.all_gather(shards[10], "fsdp", axis=1, tiled=True),
            lax.all_gather(shards[11], "fsdp", axis=1, tiled=True),
            lax.all_gather(shards[12], "fsdp", axis=1, tiled=True),
        )
        layer_weights = tuple((item[0] for item in gathered))
        if moment <= micro_count:
            forward_index = moment - section_index
            forward_live = (forward_index >= 0) & (forward_index < micro_count)
            forward_clip = jnp.clip(forward_index, 0, micro_count - 1)
            fresh_clip = lax.dynamic_index_in_dim(inputs, forward_clip, 0, keepdims=False)
            entering = jnp.where(section_index == 0, fresh_clip, act_in)
            result, kept_items = lax.cond(
                forward_live,
                lambda block_in: layer_forward(layer_weights, block_in),
                lambda block_in: (
                    jnp.zeros_like(block_in),
                    blank_kept(clip_count, length, model_width, hidden_units),
                ),
                entering,
            )
            slot_now = jnp.where(forward_live, forward_clip, micro_count)
            stored = tuple(
                (
                    lax.dynamic_update_index_in_dim(buffer, item, slot_now, 0)
                    for buffer, item in zip(stored, kept_items)
                )
            )
            out_store = lax.dynamic_update_index_in_dim(out_store, result, slot_now, 0)
            if moment < micro_count:
                act_in = shifted(result, "section", 1)
        if moment >= 1:
            back_index = moment - 2 + section_index
            back_live = (back_index >= 0) & (back_index < micro_count)
            back_clip = jnp.clip(back_index, 0, micro_count - 1)
            clip_live = lax.dynamic_index_in_dim(live_mask, back_clip, 0, keepdims=False)
            outer_grad = lax.dynamic_index_in_dim(cotangent, back_clip, 0, keepdims=False).astype(
                jnp.float32
            )
            outer_grad = outer_grad * clip_live[:, None, None]
            grad_out = jnp.where(section_index == 1, outer_grad, grad_in.astype(jnp.float32))
            saved_items = tuple(
                (
                    lax.dynamic_index_in_dim(buffer, back_clip, 0, keepdims=False)
                    for buffer in stored
                )
            )
            grad_back, weight_grads = lax.cond(
                back_live,
                lambda packed: layer_backward(layer_weights, packed[0], packed[1]),
                lambda packed: (
                    jnp.zeros(clip_shape, jnp.bfloat16),
                    tuple((jnp.zeros(item.shape, jnp.float32) for item in layer_weights)),
                ),
                (saved_items, grad_out),
            )
            back_slot = jnp.where(back_live, back_clip, micro_count)
            back_store = lax.dynamic_update_index_in_dim(back_store, grad_back, back_slot, 0)
            if moment <= micro_count:
                grad_in = shifted(grad_back, "section", -1)
            owned = jax.tree.map(
                lambda part: part.astype(jnp.float32),
                lax.psum_scatter(shortened(weight_grads), "fsdp", scatter_dimension=0, tiled=True),
            )
            shares = (
                owned
                if shares is None
                else tuple((left + right for left, right in zip(shares, owned)))
            )
    summed = jax.tree.map(lambda part: part.astype(jnp.float32), lax.psum(shortened(shares), "rep"))
    section_outputs = out_store[:micro_count][None]
    section_input_grads = back_store[:micro_count][None]
    return (
        section_outputs,
        section_input_grads,
        summed[0][None],
        summed[1][None],
        summed[2][None],
        summed[3][None],
        summed[4][None],
        summed[5][None],
        summed[6][None],
        summed[7][None],
        summed[8][None],
        summed[9][None],
        summed[10][None],
        summed[11][None],
        summed[12][None],
    )


def solution(mesh):
    in_specs = (
        P(None, ("fsdp", "rep"), None, None),
        P(None, ("fsdp", "rep"), None, None),
        P(None, ("fsdp", "rep")),
        P("section", "fsdp"),
        P("section", "fsdp"),
        P("section", "fsdp", None),
        P("section", "fsdp"),
        P("section", "fsdp"),
        P("section", "fsdp", None),
        P("section", "fsdp"),
        P("section", "fsdp"),
        P("section", "fsdp"),
        P("section", "fsdp", None),
        P("section", "fsdp"),
        P("section", "fsdp", None),
        P("section", "fsdp"),
    )
    out_specs = (
        P("section", None, ("fsdp", "rep"), None, None),
        P("section", None, ("fsdp", "rep"), None, None),
        P("section", "fsdp"),
        P("section", "fsdp"),
        P("section", "fsdp", None),
        P("section", "fsdp"),
        P("section", "fsdp"),
        P("section", "fsdp", None),
        P("section", "fsdp"),
        P("section", "fsdp"),
        P("section", "fsdp"),
        P("section", "fsdp", None),
        P("section", "fsdp"),
        P("section", "fsdp", None),
        P("section", "fsdp"),
    )
    return jax.shard_map(local, mesh=mesh, in_specs=in_specs, out_specs=out_specs, check_vma=False)
```

profile of v0, /device:TPU:0, one launch (start us, length us, event | category | flops | bytes accessed | tf_op | source)
XLA Modules:
  0.0 1616.5 jit_solution(1423898724580367199)
XLA Ops:
  16.8 6.3 all_gather.36
  26.9 11.9 all-reduce.38
  38.8 23.4 %all-gather.5.cloned.1.call-done = bf16[1,768,2304]{2,1,0:T(8,128)(2,1)} async-done(((bf16[1,192,2304]{2,1,0:T(8,128)(2,1)}), bf16[1,768,2304]{2,1,0:T(8,128)(2,1)}) %all-gather.5.cloned.1.call-update) | async-done | bytes 3538960 | tf_op jit(solution)/shard_map/all_gather | solution.py:308
  62.2 39.1 %all-gather.9.cloned.1.call-done = bf16[1,768,3072]{2,1,0:T(8,128)(2,1)} async-done(((bf16[1,192,3072]{2,1,0:T(8,128)(2,1)}), bf16[1,768,3072]{2,1,0:T(8,128)(2,1)}) %all-gather.9.cloned.1.call-update) | async-done | bytes 4718608 | tf_op jit(solution)/shard_map/all_gather | solution.py:315
  101.3 38.9 %all-gather.11.cloned.1.call-done = bf16[1,3072,768]{2,1,0:T(8,128)(2,1)} async-done(((bf16[1,768,768]{2,1,0:T(8,128)(2,1)}), bf16[1,3072,768]{2,1,0:T(8,128)(2,1)}) %all-gather.11.cloned.1.call-update) | async-done | bytes 4718608 | tf_op jit(solution)/shard_map/all_gather | solution.py:317
  140.2 80.3 %conditional.6 = (bf16[1,640,768]{2,1,0:T(8,128)(2,1)}, bf16[1,1,640,768]{3,2,1,0:T(8,128)(2,1)S(1)}, bf16[1,1,640,768]{3,2,1,0:T(8,128)(2,1)}, bf16[1,640,768]{...) conditional(s32[]{:T(128)} %convert_element_type.1138, ...), branch_computations={%region_0.1_spmd, %region_1.8_spmd} | conditional | flops 10510176256 | bytes 181472528 | solution.py:327
  155.4 8.2 multiply_reduce_fusion
  163.6 9.9 fusion
  173.5 8.9 fusion.26
  191.8 23.4 %add_convert_fusion = bf16[640,768]{1,0:T(8,128)(2,1)} fusion(f32[640,768]{1,0:T(8,128)S(1)} %get-tuple-element.1593, bf16[3072,768]{1,0:T(8,128)(2,1)} %get-tuple-element.965, f32[640,3072]{1,0:T(8,128)S(1)} %fusion.27, f32[3072]{0:T(1024)S(1)} %convert_element_type.885, f32[768]{0:T(1024)S(1)} %convert_element_type.887), kind=kOutput, calls=%fused_computation.41 | convolution fusion | flops 3151134720 | bytes 15547392 | tf_op jit(solution)/shard_map/cond/branch_1_fun/dot_general | solution.py:43
  244.7 10.8 broadcast_in_dim.435
  255.5 7.4 constant_dynamic-update-slice_fusion.18
  263.0 77.8 %conditional.7 = (bf16[1,640,768]{2,1,0:T(8,128)(2,1)}, bf16[1,1,640,768]{3,2,1,0:T(8,128)(2,1)S(1)}, bf16[1,1,640,768]{3,2,1,0:T(8,128)(2,1)}, bf16[1,640,768]{...) conditional(s32[]{:T(128)} %convert_element_type.1139, ...), branch_computations={%region_8.9_spmd, %region_9.16_spmd} | conditional | flops 10510176256 | bytes 178523376 | solution.py:327
  276.0 8.2 multiply_reduce_fusion.2
  284.2 9.9 fusion.69
  294.1 8.9 fusion.95
  312.4 23.2 %add_convert_fusion.3 = bf16[640,768]{1,0:T(8,128)(2,1)} fusion(f32[640,768]{1,0:T(8,128)S(1)} %get-tuple-element.1599, bf16[3072,768]{1,0:T(8,128)(2,1)} %get-tuple-element.982, f32[640,3072]{1,0:T(8,128)S(1)} %fusion.96, f32[3072]{0:T(1024)S(1)} %convert_element_type.907, f32[768]{0:T(1024)S(1)} %convert_element_type.909), kind=kOutput, calls=%fused_computation.133 | convolution fusion | flops 3151134720 | bytes 15547392 | tf_op jit(solution)/shard_map/cond/branch_1_fun/dot_general | solution.py:43
  344.9 7.5 constant_dynamic-update-slice_fusion.17
  361.3 20.2 %conditional.9 = (bf16[1,640,768]{2,1,0:T(8,128)(2,1)}, bf16[768]{0:T(1024)(128)(2,1)}, bf16[768]{0:T(1024)(128)(2,1)}, bf16[768,2304]{1,0:T(8,128)(2,1)}, bf16[...) conditional(s32[]{:T(128)} %convert_element_type.1141, ...), branch_computations={%region_24.25_spmd, %region_25.0_spmd} | conditional | flops 21535936512 | bytes 344967680 | solution.py:362
  382.9 14.5 conditional.8
  397.4 141.8 %collective-permute-done.2 = bf16[1,640,768]{2,1,0:T(8,128)(2,1)} collective-permute-done((bf16[1,640,768]{2,1,0:T(8,128)(2,1)}, bf16[1,640,768]{2,1,0:T(8,128)(2,1)}, u32[]{:S(2)}, u32[]{:S(2)}) %collective-permute-start.2) | collective-permute-done | bytes 983072 | tf_op jit(solution)/shard_map/ppermute | solution.py:18
  554.1 8.0 constant_dynamic-update-slice_fusion.5
  562.3 165.5 %conditional.10 = (bf16[1,640,768]{2,1,0:T(8,128)(2,1)}, bf16[768]{0:T(1024)(128)(2,1)S(1)}, bf16[768]{0:T(1024)(128)(2,1)S(1)}, bf16[768,2304]{1,0:T(8,128)(2,1...) conditional(s32[]{:T(128)} %convert_element_type.1143, ...), branch_computations={%region_44.45_spmd, %region_45.64_spmd} | conditional | flops 21532495872 | bytes 327073728 | solution.py:362
  565.1 8.0 convert_reduce_fusion.9
  573.1 22.5 %fusion.371 = bf16[3072,768]{1,0:T(8,128)(2,1)} fusion(f32[3,640,3072]{2,1,0:T(8,128)} %get-tuple-element.1028, s32[]{:T(128)} %get-tuple-element.1023, f32[1,640,768]{2,1,0:T(8,128)S(1)} %get-tuple-element.1581), kind=kOutput, calls=%fused_computation.494 | convolution fusion | flops 3148185600 | bytes 14549504 | tf_op jit(solution)/shard_map/cond/branch_1_fun/dot_general | solution.py:47
  599.3 5.8 multiply_reduce_fusion.13
  608.0 8.4 fusion.425
  623.9 5.5 copy.180
  629.4 5.5 copy.179
  637.9 5.5 copy.178
  644.7 11.0 fusion.625
  655.7 11.2 convert_reduce_fusion.13
  667.6 18.3 %multiply_reduce_fusion.12 = (f32[12,640]{1,0:T(8,128)S(1)}, f32[12,640,640]{1,2,0:T(8,128)}) fusion(f32[12,640,640]{1,2,0:T(8,128)} %fusion.625, f32[12,640]{1,0:T(8,128)S(1)} %dynamic-slice_bitcast_fusion.1, bf16[640,12,64]{0,2,1:T(8,128)(2,1)} %bitcast.586, bf16[640,12,64]{0,2,1:T(8,128)(2,1)} %bitcast.601), kind=kOutput, calls=%fused_computation.457 | convolution fusion | flops 648798720 | bytes 41349120 | tf_op jit(solution)/shard_map/cond/branch_1_fun/while/body/eval_jaxpr/qhd,khd->hqk/dot_general | solution.py:99
  685.9 13.8 multiply_convert_fusion.3
  709.7 6.7 fusion.415
  718.4 7.1 fusion.423
  729.2 108.4 %collective-permute-done.3 = bf16[1,640,768]{2,1,0:T(8,128)(2,1)} collective-permute-done((bf16[1,640,768]{2,1,0:T(8,128)(2,1)}, bf16[1,640,768]{2,1,0:T(8,128)(2,1)}, u32[]{:S(2)}, u32[]{:S(2)}) %collective-permute-start.3) | collective-permute-done | bytes 983072 | tf_op jit(solution)/shard_map/ppermute | solution.py:18
  839.0 165.9 %conditional.11 = (bf16[768]{0:T(1024)(128)(2,1)}, bf16[768]{0:T(1024)(128)(2,1)}, bf16[768,2304]{1,0:T(8,128)(2,1)}, bf16[768]{0:T(1024)(128)(2,1)}, bf16[768]{...) conditional(s32[]{:T(128)} %convert_element_type.1145, ...), branch_computations={%region_64.65_spmd, %region_65.84_spmd} | conditional | flops 21532493824 | bytes 362844096 | solution.py:362
  844.0 8.1 convert_reduce_fusion.15
  852.1 22.6 %fusion.502 = bf16[3072,768]{1,0:T(8,128)(2,1)} fusion(f32[3,640,3072]{2,1,0:T(8,128)} %get-tuple-element.1052, s32[]{:T(128)} %get-tuple-element.1043, f32[1,640,768]{2,1,0:T(8,128)S(1)} %get-tuple-element.1585), kind=kOutput, calls=%fused_computation.668 | convolution fusion | flops 3148185600 | bytes 14549504 | tf_op jit(solution)/shard_map/cond/branch_1_fun/dot_general | solution.py:47
  878.4 5.8 multiply_reduce_fusion.19
  887.0 8.7 fusion.556
  903.3 5.4 copy.184
  908.7 5.4 copy.183
  917.1 5.4 copy.182
  923.9 11.0 fusion.626
  934.9 11.3 convert_reduce_fusion.19
  946.7 18.3 %multiply_reduce_fusion.18 = (f32[12,640]{1,0:T(8,128)S(1)}, f32[12,640,640]{1,2,0:T(8,128)}) fusion(f32[12,640,640]{1,2,0:T(8,128)} %fusion.626, f32[12,640]{1,0:T(8,128)S(1)} %dynamic-slice_bitcast_fusion.2, bf16[640,12,64]{0,2,1:T(8,128)(2,1)} %bitcast.588, bf16[640,12,64]{0,2,1:T(8,128)(2,1)} %bitcast.602), kind=kOutput, calls=%fused_computation.631 | convolution fusion | flops 648798720 | bytes 41349120 | tf_op jit(solution)/shard_map/cond/branch_1_fun/while/body/eval_jaxpr/qhd,khd->hqk/dot_general | solution.py:99
  965.0 13.8 multiply_convert_fusion.6
  988.8 6.7 fusion.544
  997.6 7.1 fusion.554
  1010.9 19.0 %reduce-scatter.23.cloned.1.call-done = bf16[192,768]{1,0:T(8,128)(2,1)} async-done(((bf16[768,768]{1,0:T(8,128)(2,1)}), bf16[192,768]{1,0:T(8,128)(2,1)}) %reduce-scatter.23.cloned.1.call-update) | async-done | bytes 294928 | tf_op jit(solution)/shard_map/reduce_scatter | solution.py:377
  1031.8 41.3 %reduce-scatter.13.cloned.1.call-done = bf16[192,2304]{1,0:T(8,128)(2,1)} async-done(((bf16[768,2304]{1,0:T(8,128)(2,1)}), bf16[192,2304]{1,0:T(8,128)(2,1)}) %reduce-scatter.13.cloned.1.call-update) | async-done | bytes 884752 | tf_op jit(solution)/shard_map/reduce_scatter | solution.py:377
  1073.1 43.1 %reduce-scatter.15.cloned.1.call-done = bf16[192,2304]{1,0:T(8,128)(2,1)} async-done(((bf16[768,2304]{1,0:T(8,128)(2,1)}), bf16[192,2304]{1,0:T(8,128)(2,1)}) %reduce-scatter.15.cloned.1.call-update) | async-done | bytes 884752 | tf_op jit(solution)/shard_map/reduce_scatter | solution.py:377
  1116.2 43.0 %reduce-scatter.17.cloned.1.call-done = bf16[192,2304]{1,0:T(8,128)(2,1)} async-done(((bf16[768,2304]{1,0:T(8,128)(2,1)}), bf16[192,2304]{1,0:T(8,128)(2,1)}) %reduce-scatter.17.cloned.1.call-update) | async-done | bytes 884752 | tf_op jit(solution)/shard_map/reduce_scatter | solution.py:377
  1162.1 47.5 %reduce-scatter.25.cloned.1.call-done = bf16[192,3072]{1,0:T(8,128)(2,1)} async-done(((bf16[768,3072]{1,0:T(8,128)(2,1)}), bf16[192,3072]{1,0:T(8,128)(2,1)}) %reduce-scatter.25.cloned.1.call-update) | async-done | bytes 1179664 | tf_op jit(solution)/shard_map/reduce_scatter | solution.py:377
  1209.6 50.4 %reduce-scatter.27.cloned.1.call-done = bf16[192,3072]{1,0:T(8,128)(2,1)} async-done(((bf16[768,3072]{1,0:T(8,128)(2,1)}), bf16[192,3072]{1,0:T(8,128)(2,1)}) %reduce-scatter.27.cloned.1.call-update) | async-done | bytes 1179664 | tf_op jit(solution)/shard_map/reduce_scatter | solution.py:377
  1260.1 50.4 %reduce-scatter.29.cloned.1.call-done = bf16[192,3072]{1,0:T(8,128)(2,1)} async-done(((bf16[768,3072]{1,0:T(8,128)(2,1)}), bf16[192,3072]{1,0:T(8,128)(2,1)}) %reduce-scatter.29.cloned.1.call-update) | async-done | bytes 1179664 | tf_op jit(solution)/shard_map/reduce_scatter | solution.py:377
  1314.0 46.9 %reduce-scatter.31.cloned.1.call-done = bf16[768,768]{1,0:T(8,128)(2,1)} async-done(((bf16[3072,768]{1,0:T(8,128)(2,1)}), bf16[768,768]{1,0:T(8,128)(2,1)}) %reduce-scatter.31.cloned.1.call-update) | async-done | bytes 1179664 | tf_op jit(solution)/shard_map/reduce_scatter | solution.py:377
  1360.9 50.3 %reduce-scatter.33.cloned.1.call-done = bf16[768,768]{1,0:T(8,128)(2,1)} async-done(((bf16[3072,768]{1,0:T(8,128)(2,1)}), bf16[768,768]{1,0:T(8,128)(2,1)}) %reduce-scatter.33.cloned.1.call-update) | async-done | bytes 1179664 | tf_op jit(solution)/shard_map/reduce_scatter | solution.py:377
  1411.2 50.4 %reduce-scatter.35.cloned.1.call-done = bf16[768,768]{1,0:T(8,128)(2,1)} async-done(((bf16[3072,768]{1,0:T(8,128)(2,1)}), bf16[768,768]{1,0:T(8,128)(2,1)}) %reduce-scatter.35.cloned.1.call-update) | async-done | bytes 1179664 | tf_op jit(solution)/shard_map/reduce_scatter | solution.py:377
  1474.8 12.5 all-reduce.37
  1488.1 20.6 %all-reduce.35 = (bf16[1,192]{1,0:T(2,128)(2,1)S(1)}, bf16[1,192]{1,0:T(2,128)(2,1)S(1)}, bf16[1,192]{1,0:T(2,128)(2,1)S(1)}, bf16[1,192]{1,0:T(2,128)(2,1)S(1)}...) all-reduce(bf16[1,192]{1,0:T(2,128)(2,1)S(1)} %broadcast_in_dim.438, ...), channel_id=1, replica_groups=mesh['section'=2,'fsdp'=4,'rep'=4] {'rep'}, use_global_device_ids=true, to_apply=%region_87.88 | all-reduce | flops 2304 | bytes 9216 | tf_op jit(solution)/shard_map/psum | solution.py:384
  1516.5 84.1 %all-reduce.41.cloned.1.call-done = (bf16[1,192,2304]{2,1,0:T(8,128)(2,1)}, bf16[1,192,768]{2,1,0:T(8,128)(2,1)}, bf16[1,192,3072]{2,1,0:T(8,128)(2,1)}, bf16[1,768,768]{2,1,0:T(8,128)(2,1)}) async-done(((bf16[1,192,2304]{2,1,0:T(8,128)(2,1)}, bf16[1,192,768]{2,1,0:T(8,128)(2,1)}, bf16[1,192,3072]{2,1,0:T(8,128)(2,1)}, bf16[1,768,768]{2,1,0:T(8,128)(2,1)}), (bf16[1,192,2304]{2,1,0:T(8,128)(2,1)}, ...) | async-done | bytes 3538960 | tf_op jit(solution)/shard_map/psum | solution.py:384
  (465 shorter events, 268.1 us)
Async XLA Ops:
  7.2 31.6 %all-gather.7.cloned.1.call-start = ((), (), s32[]{:S(2)}) async-start(), calls=%async_computation.13 | async-start | bytes 1474560 | tf_op jit(solution)/shard_map/all_gather | solution.py:311
  7.9 54.3 %all-gather.5.cloned.1.call-start = ((), (), s32[]{:S(2)}) async-start(), calls=%async_computation.12 | async-start | bytes 4423680 | tf_op jit(solution)/shard_map/all_gather | solution.py:308
  8.7 92.6 %all-gather.9.cloned.1.call-start = ((), (), s32[]{:S(2)}) async-start(), calls=%async_computation.14 | async-start | bytes 5898240 | tf_op jit(solution)/shard_map/all_gather | solution.py:315
  9.4 130.8 %all-gather.11.cloned.1.call-start = ((), (), s32[]{:S(2)}) async-start(), calls=%async_computation.15 | async-start | bytes 5898240 | tf_op jit(solution)/shard_map/all_gather | solution.py:317
  10.0 1000.9 %reduce-scatter.19.cloned.1.call-start = ((), (), s32[]{:S(2)}) async-start(), calls=%async_computation.19 | async-start | bytes 1474560 | tf_op jit(solution)/shard_map/reduce_scatter | solution.py:377
  23.2 239.7 %copy-start.43 = (bf16[3072]{0:T(1024)(128)(2,1)}, bf16[3072]{0:T(1024)(128)(2,1)S(1)}, u32[]{:S(2)}) copy-start(bf16[3072]{0:T(1024)(128)(2,1)S(1)} %reduce.40) | copy-start | bytes 18436
  38.7 224.2 %copy-start.59 = (bf16[768]{0:T(1024)(128)(2,1)}, bf16[768]{0:T(1024)(128)(2,1)S(1)}, u32[]{:S(2)}) copy-start(bf16[768]{0:T(1024)(128)(2,1)S(1)} %get-tuple-element.1566) | copy-start | bytes 4612
  38.7 224.2 %copy-start.61 = (bf16[768]{0:T(1024)(128)(2,1)}, bf16[768]{0:T(1024)(128)(2,1)S(1)}, u32[]{:S(2)}) copy-start(bf16[768]{0:T(1024)(128)(2,1)S(1)} %get-tuple-element.1567) | copy-start | bytes 4612
  38.8 224.2 %copy-start.63 = (bf16[768]{0:T(1024)(128)(2,1)}, bf16[768]{0:T(1024)(128)(2,1)S(1)}, u32[]{:S(2)}) copy-start(bf16[768]{0:T(1024)(128)(2,1)S(1)} %get-tuple-element.1568) | copy-start | bytes 4612
  38.8 224.2 %copy-start.65 = (bf16[768]{0:T(1024)(128)(2,1)}, bf16[768]{0:T(1024)(128)(2,1)S(1)}, u32[]{:S(2)}) copy-start(bf16[768]{0:T(1024)(128)(2,1)S(1)} %get-tuple-element.1571) | copy-start | bytes 4612
  38.8 322.5 %copy-start.45 = (bf16[768]{0:T(1024)(128)(2,1)}, bf16[768]{0:T(1024)(128)(2,1)S(1)}, u32[]{:S(2)}) copy-start(bf16[768]{0:T(1024)(128)(2,1)S(1)} %get-tuple-element.1564) | copy-start | bytes 4612
  38.8 322.5 %copy-start.48 = (bf16[768]{0:T(1024)(128)(2,1)}, bf16[768]{0:T(1024)(128)(2,1)S(1)}, u32[]{:S(2)}) copy-start(bf16[768]{0:T(1024)(128)(2,1)S(1)} %get-tuple-element.1565) | copy-start | bytes 4612
  38.8 322.5 %copy-start.51 = (bf16[768]{0:T(1024)(128)(2,1)}, bf16[768]{0:T(1024)(128)(2,1)S(1)}, u32[]{:S(2)}) copy-start(bf16[768]{0:T(1024)(128)(2,1)S(1)} %get-tuple-element.1569) | copy-start | bytes 4612
  38.8 322.5 %copy-start.54 = (bf16[768]{0:T(1024)(128)(2,1)}, bf16[768]{0:T(1024)(128)(2,1)S(1)}, u32[]{:S(2)}) copy-start(bf16[768]{0:T(1024)(128)(2,1)S(1)} %get-tuple-element.1570) | copy-start | bytes 4612
  151.7 11.9 copy-start.9
  163.6 9.9 copy-start.39
  173.5 8.9 copy-start.84
  220.5 10.1 copy-start.25
  220.5 42.4 %collective-permute-start = (bf16[1,640,768]{2,1,0:T(8,128)(2,1)}, bf16[1,640,768]{2,1,0:T(8,128)(2,1)S(1)}, u32[]{:S(2)}, u32[]{:S(2)}) collective-permute-start(bf16[1,640,768]{2,1,0:T(8,128)(2,1)} %get-tuple-element.1152), channel_id=1, source_target_pairs={{0,16},{1,17},{2,18},{3,19},{4,20},{5,21},{6,22},{7,23},{8,24},{9,... | collective-permute-start | bytes 2949128 | tf_op jit(solution)/shard_map/ppermute | solution.py:18
  262.9 80.5 %copy-start.42 = (f32[3,1,12,640]{3,2,1,0:T(8,128)S(1)}, f32[3,1,12,640]{3,2,1,0:T(8,128)}, u32[]{:S(2)}) copy-start(f32[3,1,12,640]{3,2,1,0:T(8,128)} %copy-done.41) | copy-start | bytes 276484
  272.3 11.9 copy-start.11
  284.2 9.9 copy-start.40
  294.1 8.9 copy-start.85
  340.8 42.1 %collective-permute-start.1 = (bf16[1,640,768]{2,1,0:T(8,128)(2,1)}, bf16[1,640,768]{2,1,0:T(8,128)(2,1)}, u32[]{:S(2)}, u32[]{:S(2)}) collective-permute-start(bf16[1,640,768]{2,1,0:T(8,128)(2,1)} %get-tuple-element.1154), channel_id=1, source_target_pairs={{0,16},{1,17},{2,18},{3,19},{4,20},{5,21},{6,22},{7,23},{8,24},{9,... | collective-permute-start | bytes 2949128 | tf_op jit(solution)/shard_map/ppermute | solution.py:18
  361.2 21.6 %copy-start.44 = (bf16[3072]{0:T(1024)(128)(2,1)S(1)}, bf16[3072]{0:T(1024)(128)(2,1)}, u32[]{:S(2)}) copy-start(bf16[3072]{0:T(1024)(128)(2,1)} %copy-done.43) | copy-start | bytes 18436
  361.2 21.6 %copy-start.60 = (bf16[768]{0:T(1024)(128)(2,1)S(1)}, bf16[768]{0:T(1024)(128)(2,1)}, u32[]{:S(2)}) copy-start(bf16[768]{0:T(1024)(128)(2,1)} %copy-done.59) | copy-start | bytes 4612
  361.2 21.7 %copy-start.62 = (bf16[768]{0:T(1024)(128)(2,1)S(1)}, bf16[768]{0:T(1024)(128)(2,1)}, u32[]{:S(2)}) copy-start(bf16[768]{0:T(1024)(128)(2,1)} %copy-done.61) | copy-start | bytes 4612
  361.2 21.7 %copy-start.64 = (bf16[768]{0:T(1024)(128)(2,1)S(1)}, bf16[768]{0:T(1024)(128)(2,1)}, u32[]{:S(2)}) copy-start(bf16[768]{0:T(1024)(128)(2,1)} %copy-done.63) | copy-start | bytes 4612
  361.2 21.7 %copy-start.66 = (bf16[768]{0:T(1024)(128)(2,1)S(1)}, bf16[768]{0:T(1024)(128)(2,1)}, u32[]{:S(2)}) copy-start(bf16[768]{0:T(1024)(128)(2,1)} %copy-done.65) | copy-start | bytes 4612
  381.5 157.7 %collective-permute-start.2 = (bf16[1,640,768]{2,1,0:T(8,128)(2,1)}, bf16[1,640,768]{2,1,0:T(8,128)(2,1)}, u32[]{:S(2)}, u32[]{:S(2)}) collective-permute-start(bf16[1,640,768]{2,1,0:T(8,128)(2,1)} %get-tuple-element.1173), channel_id=1, source_target_pairs={{16,0},{17,1},{18,2},{19,3},{20,4},{21,5},{22,6},{23,7},{24,8},{25... | collective-permute-start | bytes 2949128 | tf_op jit(solution)/shard_map/ppermute | solution.py:18
  382.8 628.1 %reduce-scatter.21.cloned.1.call-start = ((), (), s32[]{:S(2)}) async-start(), calls=%async_computation.20 | async-start | bytes 1474560 | tf_op jit(solution)/shard_map/reduce_scatter | solution.py:377
  552.6 9.6 slice-start
  552.6 9.6 slice-start.6
  562.2 276.7 %copy-start.47 = (bf16[768]{0:T(1024)(128)(2,1)S(1)}, bf16[768]{0:T(1024)(128)(2,1)}, u32[]{:S(2)}) copy-start(bf16[768]{0:T(1024)(128)(2,1)} %copy-done.45) | copy-start | bytes 4612
  562.2 276.7 %copy-start.50 = (bf16[768]{0:T(1024)(128)(2,1)S(1)}, bf16[768]{0:T(1024)(128)(2,1)}, u32[]{:S(2)}) copy-start(bf16[768]{0:T(1024)(128)(2,1)} %copy-done.48) | copy-start | bytes 4612
  562.3 276.7 %copy-start.53 = (bf16[768]{0:T(1024)(128)(2,1)S(1)}, bf16[768]{0:T(1024)(128)(2,1)}, u32[]{:S(2)}) copy-start(bf16[768]{0:T(1024)(128)(2,1)} %copy-done.51) | copy-start | bytes 4612
  562.3 276.7 %copy-start.56 = (bf16[768]{0:T(1024)(128)(2,1)S(1)}, bf16[768]{0:T(1024)(128)(2,1)}, u32[]{:S(2)}) copy-start(bf16[768]{0:T(1024)(128)(2,1)} %copy-done.54) | copy-start | bytes 4612
  562.3 276.7 %copy-start.94 = (f32[2,1]{0,1:T(1,128)S(1)}, f32[2,1]{0,1:T(1,128)}, u32[]{:S(2)}) copy-start(f32[2,1]{0,1:T(1,128)} %convert_element_type.1142) | copy-start | bytes 28
  608.0 11.8 copy-start.18
  644.7 11.0 copy-start.29
  644.7 11.0 copy-start.6
  718.4 9.4 copy-start.72
  718.4 9.4 copy-start.75
  727.8 111.2 %copy-start.73 = (bf16[768]{0:T(1024)(128)(2,1)}, bf16[768]{0:T(1024)(128)(2,1)S(1)}, u32[]{:S(2)}) copy-start(bf16[768]{0:T(1024)(128)(2,1)S(1)} %get-tuple-element.1195) | copy-start | bytes 4612
  727.8 111.2 %copy-start.76 = (bf16[768]{0:T(1024)(128)(2,1)}, bf16[768]{0:T(1024)(128)(2,1)S(1)}, u32[]{:S(2)}) copy-start(bf16[768]{0:T(1024)(128)(2,1)S(1)} %get-tuple-element.1189) | copy-start | bytes 4612
  727.8 111.2 %copy-start.78 = (bf16[768]{0:T(1024)(128)(2,1)}, bf16[768]{0:T(1024)(128)(2,1)S(1)}, u32[]{:S(2)}) copy-start(bf16[768]{0:T(1024)(128)(2,1)S(1)} %get-tuple-element.1186) | copy-start | bytes 4612
  727.8 302.1 %reduce-scatter.23.cloned.1.call-start = ((), (), s32[]{:S(2)}) async-start(), calls=%async_computation.21 | async-start | bytes 1474560 | tf_op jit(solution)/shard_map/reduce_scatter | solution.py:377
  727.9 109.7 %collective-permute-start.3 = (bf16[1,640,768]{2,1,0:T(8,128)(2,1)}, bf16[1,640,768]{2,1,0:T(8,128)(2,1)}, u32[]{:S(2)}, u32[]{:S(2)}) collective-permute-start(bf16[1,640,768]{2,1,0:T(8,128)(2,1)} %get-tuple-element.1183), channel_id=1, source_target_pairs={{16,0},{17,1},{18,2},{19,3},{20,4},{21,5},{22,6},{23,7},{24,8},{25... | collective-permute-start | bytes 2949128 | tf_op jit(solution)/shard_map/ppermute | solution.py:18
  844.0 34.4 %slice-start.4 = ((s8[4718592]{0:T(1024)(128)(4,1)}), s8[4194304]{0:T(1024)(128)(4,1)S(1)}, s32[]{:S(2)}) async-start(s8[4718592]{0:T(1024)(128)(4,1)} %bitcast.640), calls=%async_computation.33 | async-start | bytes 8388608 | tf_op jit(solution)/shard_map/cond
  852.1 26.3 %slice-start.5 = ((s8[4718592]{0:T(1024)(128)(4,1)}), s8[524288]{0:T(1024)(128)(4,1)S(1)}, s32[]{:S(2)}) async-start(s8[4718592]{0:T(1024)(128)(4,1)} %bitcast.640), calls=%async_computation.34 | async-start | bytes 1048576 | tf_op jit(solution)/shard_map/cond
  887.0 12.1 copy-start.20
  887.0 12.1 copy-start.88
  923.8 11.0 copy-start.30
  923.9 11.0 copy-start.7
  1004.9 68.2 %reduce-scatter.13.cloned.1.call-start = ((), (), s32[]{:S(2)}) async-start(), calls=%async_computation.16 | async-start | bytes 4423680 | tf_op jit(solution)/shard_map/reduce_scatter | solution.py:377
  1005.7 110.5 %reduce-scatter.15.cloned.1.call-start = ((), (), s32[]{:S(2)}) async-start(), calls=%async_computation.17 | async-start | bytes 4423680 | tf_op jit(solution)/shard_map/reduce_scatter | solution.py:377
  1006.4 152.8 %reduce-scatter.17.cloned.1.call-start = ((), (), s32[]{:S(2)}) async-start(), calls=%async_computation.18 | async-start | bytes 4423680 | tf_op jit(solution)/shard_map/reduce_scatter | solution.py:377
  1007.0 202.6 %reduce-scatter.25.cloned.1.call-start = ((), (), s32[]{:S(2)}) async-start(), calls=%async_computation.22 | async-start | bytes 5898240 | tf_op jit(solution)/shard_map/reduce_scatter | solution.py:377
  1007.7 252.3 %reduce-scatter.27.cloned.1.call-start = ((), (), s32[]{:S(2)}) async-start(), calls=%async_computation.23 | async-start | bytes 5898240 | tf_op jit(solution)/shard_map/reduce_scatter | solution.py:377
  1008.3 302.2 %reduce-scatter.29.cloned.1.call-start = ((), (), s32[]{:S(2)}) async-start(), calls=%async_computation.24 | async-start | bytes 5898240 | tf_op jit(solution)/shard_map/reduce_scatter | solution.py:377
  1009.0 351.9 %reduce-scatter.31.cloned.1.call-start = ((), (), s32[]{:S(2)}) async-start(), calls=%async_computation.25 | async-start | bytes 5898240 | tf_op jit(solution)/shard_map/reduce_scatter | solution.py:377
  1009.6 401.5 %reduce-scatter.33.cloned.1.call-start = ((), (), s32[]{:S(2)}) async-start(), calls=%async_computation.26 | async-start | bytes 5898240 | tf_op jit(solution)/shard_map/reduce_scatter | solution.py:377
  1010.2 451.4 %reduce-scatter.35.cloned.1.call-start = ((), (), s32[]{:S(2)}) async-start(), calls=%async_computation.27 | async-start | bytes 5898240 | tf_op jit(solution)/shard_map/reduce_scatter | solution.py:377
  1010.8 589.8 %all-reduce.41.cloned.1.call-start = ((), (), s32[]{:S(2)}) async-start(), calls=%async_computation.28 | async-start | bytes 7077888 | tf_op jit(solution)/shard_map/psum | solution.py:384
  (46 other events, 294.0 us)
Sparse Core Ops, SparseCore 0:
  9.6 20.1 all-gather.6
  31.4 30.7 all-gather.4
  63.8 37.4 all-gather.8
  102.7 37.4 all-gather.10
  382.9 159.6 reduce-scatter.18
  727.9 110.6 reduce-scatter.20
  1005.0 24.8 reduce-scatter.22
  1032.6 40.4 reduce-scatter.12
  1075.7 40.4 reduce-scatter.14
  1118.8 40.4 reduce-scatter.16
  1161.7 47.8 reduce-scatter.24
  1212.2 47.8 reduce-scatter.26
  1262.6 47.8 reduce-scatter.28
  1313.0 47.8 reduce-scatter.30
  1363.3 47.8 reduce-scatter.32
  1413.7 47.8 reduce-scatter.34
  1465.2 135.3 all-reduce.40
where the time goes:
time: 1630 us; the launch traced here: 1620 us
  waiting for transfers between devices  886 us (54%)
  matrix products  332 us (20%)
  local copies, waits for them, and re-layouts  189 us (12%)
  other arithmetic  124 us (8%)
  blocking collectives  51.3 us (3%)
  between operations  17.4 us (1%)
    reduce_scatter x12, waiting for transfers between devices, local(): lax.psum_scatter(shortened(weight_grads), 'fsdp', scatter_dimension=0, ti...  442 us
    ppermute x4, waiting for transfers between devices, shifted(): return lax.ppermute(block, axis, route)  250 us
    psum x1, waiting for transfers between devices, local(): lax.psum(shortened(shares), 'rep')  84.1 us
    dot_general x8, matrix products, matmul_left(): lax.dot_general(left, right, (((0,), (0,)), ((), ())), preferred_element_...  83.2 us
    dot_general x8, matrix products, matmul(): return jnp.dot(left, right, preferred_element_type=jnp.float32)  70.6 us
    dynamic_update_slice x22, local copies, waits for them, and re-layouts, local(): lax.dynamic_update_index_in_dim(buffer, item, slot_now, 0)  56.1 us
    another operation x27, local copies, waits for them, and re-layouts  55.3 us
    dot_general x8, matrix products, matmul_right(): lax.dot_general(left, right, (((1,), (1,)), ((), ())), preferred_element_...  44.9 us
  transfers between devices with their start and end apart: 21, of which 16 were waited for; matrix products, arithmetic and copies ran while one was open for 29% of the time, Pallas kernels for 0%

commit v1 on v0

v1 whole, which is shorter than its diff:
```python
import math

import jax
import jax.numpy as jnp
from jax import lax
from jax.experimental import pallas as pl
from jax.experimental.pallas import tpu as pltpu
from jax.sharding import PartitionSpec as P

HEADS = 12
HD = 64
PAIR = 2 * HD
SCALE = HD ** (-0.5)
epsilon = 1e-05
LOW = jnp.bfloat16
FULL = jnp.float32


def matmul(left, right):
    return jnp.dot(left, right, preferred_element_type=FULL)


def matmul_left(left, right):
    return lax.dot_general(left, right, (((0,), (0,)), ((), ())), preferred_element_type=FULL)


def matmul_right(left, right):
    return lax.dot_general(left, right, (((1,), (1,)), ((), ())), preferred_element_type=FULL)


def row_stats(values_in):
    mean_row = jnp.mean(values_in, axis=-1, keepdims=True)
    centered = values_in - mean_row
    factor = lax.rsqrt(jnp.mean(centered * centered, axis=-1, keepdims=True) + epsilon)
    return (centered * factor, factor)


def norm_back(grad_norm, normal, factor):
    first_mean = jnp.mean(grad_norm, axis=-1, keepdims=True)
    second_mean = jnp.mean(grad_norm * normal, axis=-1, keepdims=True)
    return factor * (grad_norm - first_mean - normal * second_mean)


def head_mask(head):
    lanes = lax.broadcasted_iota(jnp.int32, (1, PAIR), 1)
    return (lanes >= head * HD) & (lanes < (head + 1) * HD)


def only_head(rows, head):
    return jnp.where(head_mask(head), rows, jnp.zeros_like(rows))


def attend_kernel(q_ref, k_ref, v_ref, context_ref, lse_ref):
    queries = q_ref[...]
    keys = k_ref[...] * jnp.asarray(SCALE, LOW)
    values_t = v_ref[...].T
    pieces = []
    for head in range(2):
        scores = matmul_right(only_head(keys, head), queries)
        top = jnp.max(scores, axis=0, keepdims=True)
        exponent = jnp.exp(scores - top)
        total = jnp.sum(exponent, axis=0, keepdims=True)
        lse_ref[0, head : head + 1, :] = top + jnp.log(total)
        part = matmul(values_t[head * HD : (head + 1) * HD], exponent.astype(LOW))
        pieces.append(part * (1.0 / total))
    context_ref[...] = jnp.concatenate(pieces, 0).T.astype(LOW)


def attend_back_kernel(q_ref, k_ref, v_ref, lse_ref, g_ref, dq_ref, dk_ref, dv_ref):
    scale = jnp.asarray(SCALE, LOW)
    queries = q_ref[...]
    keys = k_ref[...] * scale
    values = v_ref[...]
    grads = g_ref[...]
    scaled_queries = queries * scale
    keys_t = keys.T
    pieces = []
    key_grad = None
    value_grad = None
    for head in range(2):
        grad_head = only_head(grads, head)
        scores = matmul_right(only_head(keys, head), queries)
        probs = jnp.exp(scores - lse_ref[0, head : head + 1, :])
        grad_probs = matmul_right(values, grad_head)
        value_part = matmul(probs.astype(LOW), grad_head)
        inner = jnp.sum(probs * grad_probs, axis=0, keepdims=True)
        grad_scores = (probs * (grad_probs - inner)).astype(LOW)
        key_part = matmul(grad_scores, only_head(scaled_queries, head))
        pieces.append(matmul(keys_t[head * HD : (head + 1) * HD], grad_scores))
        key_grad = key_part if key_grad is None else key_grad + key_part
        value_grad = value_part if value_grad is None else value_grad + value_part
    dq_ref[...] = jnp.concatenate(pieces, 0).T.astype(LOW)
    dk_ref[...] = key_grad.astype(LOW)
    dv_ref[...] = value_grad.astype(LOW)


def attend_cost(rows, length, products):
    return pl.CostEstimate(
        flops=2 * products * rows * length * HEADS * HD * 3,
        bytes_accessed=rows * HEADS * HD * 2 * (products + 2),
        transcendentals=rows * length * HEADS,
    )


def attend_forward(clips, length, queries, key_rows, value_rows):
    rows, width = queries.shape
    pairs = width // PAIR
    block = pl.BlockSpec((length, PAIR), lambda c, j: (c, j))
    lse_block = pl.BlockSpec((1, 8, length), lambda c, j: (c * pairs + j, 0, 0))
    return pl.pallas_call(
        attend_kernel,
        grid=(clips, pairs),
        in_specs=[block] * 3,
        out_specs=[block, lse_block],
        out_shape=[
            jax.ShapeDtypeStruct((rows, width), LOW),
            jax.ShapeDtypeStruct((clips * pairs, 8, length), FULL),
        ],
        compiler_params=pltpu.CompilerParams(vmem_limit_bytes=40 * 1024 * 1024),
        cost_estimate=attend_cost(rows, length, 2),
        name="attend_forward",
    )(queries, key_rows, value_rows)


def attend_backward(clips, length, queries, key_rows, value_rows, lse, grad_context):
    rows, width = queries.shape
    pairs = width // PAIR
    block = pl.BlockSpec((length, PAIR), lambda c, j: (c, j))
    lse_block = pl.BlockSpec((1, 8, length), lambda c, j: (c * pairs + j, 0, 0))
    return pl.pallas_call(
        attend_back_kernel,
        grid=(clips, pairs),
        in_specs=[block] * 3 + [lse_block, block],
        out_specs=[block] * 3,
        out_shape=[jax.ShapeDtypeStruct((rows, width), LOW)] * 3,
        compiler_params=pltpu.CompilerParams(vmem_limit_bytes=48 * 1024 * 1024),
        cost_estimate=attend_cost(rows, length, 5),
        name="attend_backward",
    )(queries, key_rows, value_rows, lse, grad_context)


def gelu_parts(upper):
    size = jnp.abs(upper)
    turn = 1.0 / (1.0 + (0.3275911 / math.sqrt(2.0)) * size)
    bell = jnp.exp(-0.5 * upper * upper)
    series = turn * (
        0.5 * 0.254829592
        + turn
        * (
            0.5 * -0.284496736
            + turn * (0.5 * 1.421413741 + turn * (0.5 * -1.453152027 + turn * (0.5 * 1.061405429)))
        )
    )
    tail = series * bell
    below = jnp.where(upper < 0, tail, 1.0 - tail)
    return upper * below, below + upper * bell * (1.0 / math.sqrt(2.0 * math.pi))


def layer_forward(weights, clips, length, rows_in):
    width = rows_in.shape[1]
    token_rows = rows_in.astype(FULL)
    normal_one, _ = row_stats(token_rows)
    normed = (normal_one * weights["gain_one"] + weights["shift_one"]).astype(LOW)
    projected = matmul(normed, weights["project"])
    queries = (projected[:, :width] + weights["bias_query"]).astype(LOW)
    key_rows = projected[:, width : 2 * width].astype(LOW)
    value_rows = (projected[:, 2 * width :] + weights["bias_value"]).astype(LOW)
    context, lse = attend_forward(clips, length, queries, key_rows, value_rows)
    hidden = token_rows + (matmul(context, weights["output"]) + weights["bias_output"])
    normal_two, _ = row_stats(hidden)
    mixed_rows = (normal_two * weights["gain_two"] + weights["shift_two"]).astype(LOW)
    upper = matmul(mixed_rows, weights["expand"]) + weights["bias_expand"]
    active, slope = gelu_parts(upper)
    active = active.astype(LOW)
    slope = slope.astype(LOW)
    result = (hidden + (matmul(active, weights["contract"]) + weights["bias_contract"])).astype(LOW)
    kept = (rows_in, normed, queries, key_rows, value_rows, lse, context, hidden, mixed_rows, active, slope)
    return result, kept


def layer_backward(weights, clips, length, kept, grad_low, grad_full):
    rows_in, normed, queries, key_rows, value_rows, lse, context, hidden, mixed_rows, active, slope = kept
    grad_upper = (matmul_right(grad_low, weights["contract"]) * slope).astype(LOW)
    grad_mixed = matmul_right(grad_upper, weights["expand"])
    normal_two, factor_two = row_stats(hidden)
    gain_two_grad = jnp.sum(grad_mixed * normal_two, axis=0)
    shift_two_grad = jnp.sum(grad_mixed, axis=0)
    grad_hidden = grad_full + norm_back(grad_mixed * weights["gain_two"], normal_two, factor_two)
    grad_attended = grad_hidden.astype(LOW)
    grad_context = matmul_right(grad_attended, weights["output"]).astype(LOW)
    grad_queries, grad_keys, grad_values = attend_backward(
        clips, length, queries, key_rows, value_rows, lse, grad_context
    )
    grad_proj = jnp.concatenate([grad_queries, grad_keys, grad_values], 1)
    grad_normed = matmul_right(grad_proj, weights["project"])
    normal_one, factor_one = row_stats(rows_in.astype(FULL))
    gain_one_grad = jnp.sum(grad_normed * normal_one, axis=0)
    shift_one_grad = jnp.sum(grad_normed, axis=0)
    grad_in = grad_hidden + norm_back(grad_normed * weights["gain_one"], normal_one, factor_one)

    def total(part):
        return jnp.sum(part.astype(FULL), axis=0)

    small = dict(
        gain_one=gain_one_grad,
        shift_one=shift_one_grad,
        bias_query=total(grad_queries),
        bias_value=total(grad_values),
        bias_output=total(grad_attended),
        gain_two=gain_two_grad,
        shift_two=shift_two_grad,
        bias_expand=total(grad_upper),
        bias_contract=total(grad_low),
    )
    factors = dict(
        contract=(active, grad_low),
        expand=(mixed_rows, grad_upper),
        output=(context, grad_attended),
        project=(normed, grad_proj),
    )
    return grad_in.astype(LOW), small, factors


SMALL = (
    "gain_one",
    "shift_one",
    "bias_query",
    "bias_value",
    "bias_output",
    "gain_two",
    "shift_two",
    "bias_contract",
    "bias_expand",
)
LARGE = ("project", "output", "expand", "contract")
ORDER = (
    "gain_one",
    "shift_one",
    "project",
    "bias_query",
    "bias_value",
    "output",
    "bias_output",
    "gain_two",
    "shift_two",
    "expand",
    "bias_expand",
    "contract",
    "bias_contract",
)


def gather_weights(shards):
    weights = {}
    packed = jnp.concatenate([shards[name] for name in SMALL], 0)[None]
    spread = lax.all_gather(packed, "fsdp", axis=0, tiled=True)
    place = 0
    for name in SMALL:
        size = shards[name].shape[0]
        weights[name] = spread[:, place : place + size].reshape(-1).astype(FULL)
        place += size
    for name in LARGE:
        weights[name] = lax.all_gather(shards[name], "fsdp", axis=0, tiled=True)
    return weights


def reduce_large(grad):
    owned = lax.psum_scatter(grad.astype(LOW), "fsdp", scatter_dimension=0, tiled=True)
    return lax.psum(owned, "rep").astype(FULL)


def reduce_small(small, shards):
    packed = jnp.concatenate([small[name] for name in SMALL], 0)
    whole = lax.psum(packed.reshape(-1, 128), ("fsdp", "rep")).reshape(-1)
    index = lax.axis_index("fsdp")
    place = 0
    owned = {}
    for name in SMALL:
        size = small[name].shape[0]
        part = shards[name].shape[0]
        owned[name] = lax.dynamic_slice_in_dim(whole[place : place + size], index * part, part)
        place += size
    return owned


def local(inputs, cotangent, live_slots, *params):
    shards = {name: part[0] for name, part in zip(ORDER, params)}
    micro_count, clips, length, width = inputs.shape
    rows = clips * length
    first = lax.axis_index("section") == 0
    inputs = inputs.reshape(micro_count, rows, width)
    live = jnp.repeat(live_slots.reshape(micro_count, clips, 1), length, axis=1)
    cotangent = cotangent.reshape(micro_count, rows, width) * (live == 1).astype(LOW)
    weights = gather_weights(shards)

    def forward(rows_in):
        return layer_forward(weights, clips, length, rows_in)

    def onward(rows_out):
        return lax.ppermute(rows_out, "section", [(0, 1)])

    def back(grad_rows):
        return lax.ppermute(grad_rows, "section", [(1, 0)])

    out_a, _ = forward(inputs[0])
    out_b, kept_odd = forward(jnp.where(first, inputs[1], onward(out_a)))
    out_c, kept_even = forward(jnp.where(first, inputs[0], onward(out_b)))
    section_outputs = jnp.stack([jnp.where(first, out_c, out_b), jnp.where(first, out_b, out_c)])

    def backward(kept, grad_low):
        return layer_backward(weights, clips, length, kept, grad_low, grad_low.astype(FULL))

    grad_a, _, _ = backward(kept_odd, cotangent[0])
    grad_b, small_b, factors_b = backward(kept_even, jnp.where(first, back(grad_a), cotangent[1]))
    grad_c, small_c, factors_c = backward(kept_odd, jnp.where(first, back(grad_b), cotangent[0]))
    section_input_grads = jnp.stack([jnp.where(first, grad_b, grad_c), jnp.where(first, grad_c, grad_b)])

    owned = {}
    for name in ("contract", "expand", "output", "project"):
        (left_b, right_b), (left_c, right_c) = factors_b[name], factors_c[name]
        left = jnp.concatenate([left_b, left_c], 0)
        right = jnp.concatenate([right_b, right_c], 0)
        owned[name] = reduce_large(matmul_left(left, right))
    small = {name: small_b[name] + small_c[name] for name in SMALL}
    owned.update(reduce_small(small, shards))
    shape_out = (1, micro_count, clips, length, width)
    return (
        section_outputs.reshape(shape_out),
        section_input_grads.reshape(shape_out),
    ) + tuple(owned[name][None] for name in ORDER)


def solution(mesh):
    rows_spec = P(None, ("fsdp", "rep"), None, None)
    vector = P("section", "fsdp")
    matrix = P("section", "fsdp", None)
    params = tuple(matrix if name in LARGE else vector for name in ORDER)
    in_specs = (rows_spec, rows_spec, P(None, ("fsdp", "rep"))) + params
    out_rows = P("section", None, ("fsdp", "rep"), None, None)
    out_specs = (out_rows, out_rows) + params
    return jax.shard_map(local, mesh=mesh, in_specs=in_specs, out_specs=out_specs, check_vma=False)
```

time: 1630 us -> 712 us (0.44)
  waiting for transfers between devices: 886 us -> 324 us
  matrix products: 332 us -> 153 us
  local copies, waits for them, and re-layouts: 189 us -> 19.3 us
  other arithmetic: 124 us -> 30.5 us
  Pallas kernels: 0 us -> 82.5 us
  blocking collectives: 51.3 us -> 71.2 us
    reduce_scatter x12 -> x4, waiting for transfers between devices: 442 us -> 103 us  [reduce_large(): lax.psum_scatter(grad.astype(LOW), 'fsdp', scatter_dimension=0, tiled=True)]
    ppermute x4, waiting for transfers between devices: 250 us -> 51.3 us  [the longest x2 33.1 us: back(): return lax.ppermute(grad_rows, 'section', [(1, 0)])]
    dot_general x22 -> x11, matrix products: 204 us -> 64.7 us  [matmul(): return jnp.dot(left, right, preferred_element_type=FULL)]
    pallas_call x0 -> x6, Pallas kernels: none -> 82.5 us  [the longest x3 51.8 us: attend_backward(): pl.pallas_call(attend_back_kernel, grid=(clips, pairs), in_specs=[block]...]
    dynamic_update_slice x27 -> x0, local copies, waits for them, and re-layouts: 62.6 us -> none  [the longest x22 56.1 us: local(): lax.dynamic_update_index_in_dim(buffer, item, slot_now, 0)]
    another operation x27 -> x0, local copies, waits for them, and re-layouts: 55.3 us -> none
    dot_general x8 -> x4, matrix products: 83.2 us -> 30.9 us  [matmul_left(): lax.dot_general(left, right, (((0,), (0,)), ((), ())), preferred_element_...]
    psum x1, blocking collectives: 20.6 us -> 65 us  [reduce_small(): whole = lax.psum(packed.reshape(-1, 128), ('fsdp', 'rep')).reshape(-1)]
  transfers between devices with their start and end apart: 21 -> 13, of which waited for: 16 -> 11; matrix products, arithmetic and copies ran while one was open for 29% -> 14% of each run, Pallas kernels for 0% -> 6%
where the time goes in v1:
time: 712 us; the launch traced here: 708 us
  waiting for transfers between devices  324 us (46%)
  matrix products  153 us (21%)
  Pallas kernels  82.5 us (12%)
  blocking collectives  71.2 us (10%)
  other arithmetic  30.5 us (4%)
  local copies, waits for them, and re-layouts  19.3 us (3%)
  between operations  15.5 us (2%)
  starting transfers between devices  12.7 us (2%)
    reduce_scatter x4, waiting for transfers between devices, reduce_large(): lax.psum_scatter(grad.astype(LOW), 'fsdp', scatter_dimension=0, tiled=True)  103 us
    all_gather x4, waiting for transfers between devices, gather_weights(): weights[name] = lax.all_gather(shards[name], 'fsdp', axis=0, tiled=True)  102 us
    psum x1, blocking collectives, reduce_small(): whole = lax.psum(packed.reshape(-1, 128), ('fsdp', 'rep')).reshape(-1)  65 us
    dot_general x11, matrix products, matmul(): return jnp.dot(left, right, preferred_element_type=FULL)  64.7 us
    psum x1, waiting for transfers between devices, reduce_large(): return lax.psum(owned, 'rep').astype(FULL)  64.1 us
    dot_general x11, matrix products, matmul_right(): lax.dot_general(left, right, (((1,), (1,)), ((), ())), preferred_element_...  57.4 us
    pallas_call x3, Pallas kernels, attend_backward(): pl.pallas_call(attend_back_kernel, grid=(clips, pairs), in_specs=[block]...  51.8 us
    ppermute x2, waiting for transfers between devices, back(): return lax.ppermute(grad_rows, 'section', [(1, 0)])  33.1 us
  transfers between devices with their start and end apart: 13, of which 11 were waited for; matrix products, arithmetic and copies ran while one was open for 14% of the time, Pallas kernels for 6%

profile of v1, /device:TPU:0, one launch (start us, length us, event | category | flops | bytes accessed | tf_op | source)
XLA Modules:
  0.0 708.3 jit_solution(18353217815674452151)
XLA Ops:
  10.5 6.2 all-gather.5
  18.1 25.1 %all-gather.11.cloned.1.call-done = bf16[1,768,2304]{2,1,0:T(8,128)(2,1)} async-done(((bf16[1,192,2304]{2,1,0:T(8,128)(2,1)}), bf16[1,768,2304]{2,1,0:T(8,128)(2,1)}) %all-gather.11.cloned.1.call-update) | async-done | bytes 3538960 | tf_op jit(solution)/shard_map/all_gather | solution.py:263
  43.2 4.7 fusion.69
  48.3 10.8 %attend_forward.3 = (bf16[640,768]{1,0:T(8,128)(2,1)S(1)}, f32[6,8,640]{2,1,0:T(8,128)}) custom-call(bf16[640,768]{1,0:T(8,128)(2,1)S(1)} %get-tuple-element.135.q_ref, bf16[640,768]{1,0:T(8,128)(2,1)S(1)} %slice.262.k_ref, bf16[640,768]{1,0:T(8,128)(2,1)S(1)} %get-tuple-element.134.v_ref), custom_call_target="tpu_custom_call" | custom-call | flops 3774873600 | bytes 3932160 | tf_op jit(solution)/shard_map/attend_forward/pallas_call | solution.py:110
  59.1 3.1 all-gather.13.cloned.1.call-done
  62.2 2.3 fusion.192
  64.6 1.3 copy-done.26
  66.2 35.1 %all-gather.15.cloned.1.call-done = bf16[1,768,3072]{2,1,0:T(8,128)(2,1)} async-done(((bf16[1,192,3072]{2,1,0:T(8,128)(2,1)}), bf16[1,768,3072]{2,1,0:T(8,128)(2,1)}) %all-gather.15.cloned.1.call-update) | async-done | bytes 4718608 | tf_op jit(solution)/shard_map/all_gather | solution.py:263
  101.3 38.9 %all-gather.17.cloned.1.call-done = bf16[1,3072,768]{2,1,0:T(8,128)(2,1)} async-done(((bf16[1,768,768]{2,1,0:T(8,128)(2,1)}), bf16[1,3072,768]{2,1,0:T(8,128)(2,1)}) %all-gather.17.cloned.1.call-update) | async-done | bytes 4718608 | tf_op jit(solution)/shard_map/all_gather | solution.py:263
  140.2 15.5 %add_convert_fusion.4 = bf16[640,768]{1,0:T(8,128)(2,1)} fusion(f32[640,768]{1,0:T(8,128)} %copy-done.26, bf16[1,3072,768]{2,1,0:T(8,128)(2,1)} %all-gather.17.cloned.1.call-done, f32[768]{0:T(1024)S(1)} %reshape.276, bf16[1,768,3072]{2,1,0:T(8,128)(2,1)} %all-gather.15.cloned.1.call-done, f32[3072]{0:T(1024)S(1)} %reshape.275, f32[768]{0:T(1024)S(1)} %reshape.274, ...), kind=kOutput, calls=%fused_computation.191 | convolution fusion | flops 6086983680 | bytes 12412928 | tf_op jit(solution)/shard_map/dot_general | solution.py:20
  155.7 3.8 collective-permute-start
  159.5 3.0 bitcast_multiply_fusion
  162.5 18.2 %collective-permute-done = bf16[640,768]{1,0:T(8,128)(2,1)S(1)} collective-permute-done((bf16[640,768]{1,0:T(8,128)(2,1)}, bf16[640,768]{1,0:T(8,128)(2,1)S(1)}, u32[]{:S(2)}, u32[]{:S(2)}) %collective-permute-start) | collective-permute-done | bytes 983072 | tf_op jit(solution)/shard_map/ppermute | solution.py:300
  182.0 1.1 copy-done.52
  183.1 2.5 fusion.67
  186.1 10.0 %attend_forward.4 = (bf16[640,768]{1,0:T(8,128)(2,1)S(1)}, f32[6,8,640]{2,1,0:T(8,128)S(1)}) custom-call(bf16[640,768]{1,0:T(8,128)(2,1)S(1)} %get-tuple-element.133.q_ref, bf16[640,768]{1,0:T(8,128)(2,1)S(1)} %slice.261.k_ref, bf16[640,768]{1,0:T(8,128)(2,1)S(1)} %get-tuple-element.132.v_ref), custom_call_target="tpu_custom_call" | custom-call | flops 3774873600 | bytes 3932160 | tf_op jit(solution)/shard_map/attend_forward/pallas_call | solution.py:110
  198.0 10.5 %fusion.11 = (bf16[640,3072]{1,0:T(8,128)(2,1)}, bf16[640,3072]{1,0:T(8,128)(2,1)S(1)}) fusion(f32[3072]{0:T(1024)S(1)} %reshape.275, bf16[640,768]{1,0:T(8,128)(2,1)S(1)} %add_convert_fusion.3, bf16[1,768,3072]{2,1,0:T(8,128)(2,1)S(1)} %bitcast.220), kind=kOutput, calls=%fused_computation.19 | convolution fusion | flops 3071016960 | bytes 13578240 | tf_op jit(solution)/shard_map/dot_general | solution.py:20
  208.5 4.2 add_convert_fusion.2
  212.7 5.4 collective-permute-start.1
  218.1 13.5 %multiply_reduce_fusion.13 = (f32[640]{0:T(1024)S(1)}, f32[640]{0:T(1024)S(1)}, f32[640,768]{1,0:T(8,128)}) fusion(f32[768]{0:T(1024)S(1)} %reshape.273, f32[640]{0:T(1024)S(1)} %add_rsqrt_fusion.2, f32[640,768]{1,0:T(8,128)} %copy-done.10, f32[640]{0:T(1024)S(1)} %broadcast_multiply_fusion.14, bf16[1,768,3072]{2,1,0:T(8,128)(2,1)} %all-gather.15.cloned.1.call-done, ...), kind=kOutput, calls=%fused_computation.201 | convolution fusion | flops 6048644096 | bytes 18297856 | tf_op jit(solution)/shard_map/dot_general | solution.py:28
  231.6 5.1 convolution_convert_fusion.2.g_ref
  236.7 17.4 %attend_backward.3 = (bf16[640,768]{1,0:T(8,128)(2,1)S(1)}, bf16[640,768]{1,0:T(8,128)(2,1)S(1)}, bf16[640,768]{1,0:T(8,128)(2,1)S(1)}) custom-call(bf16[640,768]{1,0:T(8,128)(2,1)S(1)} %get-tuple-element.133.q_ref, bf16[640,768]{1,0:T(8,128)(2,1)S(1)} %slice.261.k_ref, bf16[640,768]{1,0:T(8,128)(2,1)S(1)} %get-tuple-element.132.v_ref, ...), custom_call_target="tpu_custom_call" | custom-call | flops 9437184000 | bytes 6881280 | tf_op jit(solution)/shard_map/attend_backward/pallas_call | solution.py:130
  255.3 2.7 multiply_reduce_fusion.12
  258.1 2.5 fusion.65
  261.1 10.0 %attend_forward.5 = (bf16[640,768]{1,0:T(8,128)(2,1)S(1)}, f32[6,8,640]{2,1,0:T(8,128)S(1)}) custom-call(bf16[640,768]{1,0:T(8,128)(2,1)S(1)} %get-tuple-element.131.q_ref, bf16[640,768]{1,0:T(8,128)(2,1)S(1)} %slice.260.k_ref, bf16[640,768]{1,0:T(8,128)(2,1)S(1)} %get-tuple-element.130.v_ref), custom_call_target="tpu_custom_call" | custom-call | flops 3774873600 | bytes 3932160 | tf_op jit(solution)/shard_map/attend_forward/pallas_call | solution.py:110
  273.4 1.2 copy-done.11
  274.7 2.1 fusion.107
  276.8 1.3 collective-permute-start.2
  278.2 12.8 %multiply_convert_fusion.1 = (bf16[640,3072]{1,0:T(8,128)(2,1)}, f32[640,3072]{1,0:T(8,128)}) fusion(f32[3072]{0:T(1024)S(1)} %reshape.275, bf16[640,768]{1,0:T(8,128)(2,1)S(1)} %get-tuple-element.155, bf16[1,768,3072]{2,1,0:T(8,128)(2,1)} %all-gather.15.cloned.1.call-done), kind=kOutput, calls=%fused_computation.37 | convolution fusion | flops 3063152640 | bytes 17510400 | tf_op jit(solution)/shard_map/dot_general | solution.py:20
  290.9 10.6 %collective-permute-done.2 = bf16[640,768]{1,0:T(8,128)(2,1)S(1)} collective-permute-done((bf16[640,768]{1,0:T(8,128)(2,1)S(1)}, bf16[640,768]{1,0:T(8,128)(2,1)S(1)}, u32[]{:S(2)}, u32[]{:S(2)}) %collective-permute-start.2) | collective-permute-done | bytes 983072 | tf_op jit(solution)/shard_map/ppermute | solution.py:303
  301.9 11.3 %convert_reduce_fusion.1 = (f32[3072]{0:T(1024)S(1)}, bf16[640,3072]{1,0:T(8,128)(2,1)S(1)}) fusion(f32[640,3072]{1,0:T(8,128)} %get-tuple-element.166, f32[3072]{0:T(1024)S(1)} %reshape.275, bf16[640,768]{1,0:T(8,128)(2,1)S(1)} %get-tuple-element.115, bf16[1,3072,768]{2,1,0:T(8,128)(2,1)S(1)} %bitcast.216), kind=kOutput, calls=%fused_computation.35 | convolution fusion | flops 3076912128 | bytes 17522688 | tf_op jit(solution)/shard_map/dot_general | solution.py:28
  313.3 3.7 multiply_reduce_fusion.1
  317.0 2.1 convert_reduce_fusion.8
  319.1 1.9 convolution_convert_fusion.1.g_ref
  321.0 17.2 %attend_backward.4 = (bf16[640,768]{1,0:T(8,128)(2,1)S(1)}, bf16[640,768]{1,0:T(8,128)(2,1)S(1)}, bf16[640,768]{1,0:T(8,128)(2,1)S(1)}) custom-call(bf16[640,768]{1,0:T(8,128)(2,1)S(1)} %get-tuple-element.131.q_ref, bf16[640,768]{1,0:T(8,128)(2,1)S(1)} %slice.260.k_ref, bf16[640,768]{1,0:T(8,128)(2,1)S(1)} %get-tuple-element.130.v_ref, ...), custom_call_target="tpu_custom_call" | custom-call | flops 9437184000 | bytes 6881280 | tf_op jit(solution)/shard_map/attend_backward/pallas_call | solution.py:130
  338.5 1.8 copy-done.54
  340.3 2.8 fusion.99
  344.0 1.6 collective-permute-start.3
  345.5 22.5 %collective-permute-done.3 = bf16[640,768]{1,0:T(8,128)(2,1)S(1)} collective-permute-done((bf16[640,768]{1,0:T(8,128)(2,1)S(1)}, bf16[640,768]{1,0:T(8,128)(2,1)S(1)}, u32[]{:S(2)}, u32[]{:S(2)}) %collective-permute-start.3) | collective-permute-done | bytes 983072 | tf_op jit(solution)/shard_map/ppermute | solution.py:303
  368.4 5.5 convert_reduce_fusion
  374.0 3.6 multiply_reduce_fusion
  377.6 2.1 convert_reduce_fusion.7
  379.7 2.8 fusion.141
  382.6 3.3 convolution_convert_fusion.g_ref
  385.9 17.2 %attend_backward.5 = (bf16[640,768]{1,0:T(8,128)(2,1)S(1)}, bf16[640,768]{1,0:T(8,128)(2,1)S(1)}, bf16[640,768]{1,0:T(8,128)(2,1)S(1)}) custom-call(bf16[640,768]{1,0:T(8,128)(2,1)S(1)} %copy-done.7, bf16[640,768]{1,0:T(8,128)(2,1)S(1)} %copy-done.3, bf16[640,768]{1,0:T(8,128)(2,1)S(1)} %copy-done.5, f32[6,8,640]{2,1,0:T(8,128)S(1)} %get-tuple-element.32.lse_ref, ...), custom_call_target="tpu_custom_call" | custom-call | flops 9437184000 | bytes 6881280 | tf_op jit(solution)/shard_map/attend_backward/pallas_call | solution.py:130
  404.2 1.7 copy-done.35
  405.9 1.2 copy-done.34
  407.1 6.5 fusion.30
  413.6 10.9 %fusion.36 = bf16[768,3072]{1,0:T(8,128)(2,1)} fusion(bf16[640,3072]{1,0:T(8,128)(2,1)} %copy-done.59, bf16[640,3072]{1,0:T(8,128)(2,1)} %copy-done.62, bf16[640,768]{1,0:T(8,128)(2,1)} %copy-done.31, bf16[640,768]{1,0:T(8,128)(2,1)} %copy-done.32), kind=kOutput, calls=%fused_computation.45 | convolution fusion | flops 6061817856 | bytes 14548992 | tf_op jit(solution)/shard_map/dot_general | solution.py:24
  424.6 10.7 %fusion.33 = bf16[3072,768]{1,0:T(8,128)(2,1)} fusion(bf16[640,3072]{1,0:T(8,128)(2,1)} %copy-done.63, bf16[640,3072]{1,0:T(8,128)(2,1)} %get-tuple-element.165, bf16[640,768]{1,0:T(8,128)(2,1)} %copy-done.24, bf16[640,768]{1,0:T(8,128)(2,1)} %copy-done.23), kind=kOutput, calls=%fused_computation.44 | convolution fusion | flops 6061817856 | bytes 14548992 | tf_op jit(solution)/shard_map/dot_general | solution.py:24
  436.0 7.9 %select_bitcast_fusion.3 = (bf16[1,640,768]{2,1,0:T(8,128)(2,1)S(1)}, bf16[1,640,768]{2,1,0:T(8,128)(2,1)S(1)}) fusion(bf16[640,768]{1,0:T(8,128)(2,1)} %add_convert_fusion.2, pred[]{:T(512)S(6)} %eq.13, f32[640,768]{1,0:T(8,128)} %copy-done.16, f32[768]{0:T(1024)S(1)} %copy-done.42, bf16[640,3072]{1,0:T(8,128)(2,1)} %get-tuple-element.165, ...), kind=kOutput, calls=%fused_computation.222 | convolution fusion | flops 3022356480 | bytes 13569025 | tf_op jit(solution)/shard_map/dot_general | solution.py:20
  443.9 1.4 maximum_bitcast_fusion
  446.9 3.9 fusion.113
  450.8 2.4 reduce-scatter.5.cloned.1.call-done
  453.3 50.4 %reduce-scatter.9.cloned.1.call-done = bf16[192,3072]{1,0:T(8,128)(2,1)} async-done(((bf16[768,3072]{1,0:T(8,128)(2,1)}), bf16[192,3072]{1,0:T(8,128)(2,1)}) %reduce-scatter.9.cloned.1.call-update) | async-done | bytes 1179664 | tf_op jit(solution)/shard_map/reduce_scatter | solution.py:268
  503.7 50.6 %reduce-scatter.11.cloned.1.call-done = bf16[768,768]{1,0:T(8,128)(2,1)} async-done(((bf16[3072,768]{1,0:T(8,128)(2,1)}), bf16[768,768]{1,0:T(8,128)(2,1)}) %reduce-scatter.11.cloned.1.call-update) | async-done | bytes 1179664 | tf_op jit(solution)/shard_map/reduce_scatter | solution.py:268
  554.8 65.0 %psum.35 = f32[72,128]{1,0:T(8,128)S(1)} all-reduce(f32[72,128]{1,0:T(8,128)S(1)} %bitcast.204), channel_id=1, replica_groups=mesh['section'=2,'fsdp'=4,'rep'=4] {'fsdp','rep'}, use_global_device_ids=true, to_apply=%region_42.43 | all-reduce | flops 9216 | bytes 73728 | tf_op jit(solution)/shard_map/psum | solution.py:274
  625.5 2.7 select_bitcast_fusion.1
  628.3 1.4 maximum_bitcast_fusion.1
  629.7 64.1 %all-reduce.3.cloned.1.call-done = (bf16[1,192,2304]{2,1,0:T(8,128)(2,1)}, bf16[1,192,768]{2,1,0:T(8,128)(2,1)}, bf16[1,192,3072]{2,1,0:T(8,128)(2,1)}, bf16[1,768,768]{2,1,0:T(8,128)(2,1)}) async-done(((bf16[1,192,2304]{2,1,0:T(8,128)(2,1)}, bf16[1,192,768]{2,1,0:T(8,128)(2,1)}, bf16[1,192,3072]{2,1,0:T(8,128)(2,1)}, bf16[1,768,768]{2,1,0:T(8,128)(2,1)}), (bf16[1,192,2304]{2,1,0:T(8,128)(2,1)}, ...) | async-done | bytes 3538960 | tf_op jit(solution)/shard_map/psum | solution.py:269
  693.9 1.9 broadcast_in_dim.48
  695.8 2.5 broadcast_in_dim.44
  698.3 1.7 broadcast_in_dim.53
  699.9 1.6 broadcast_in_dim.56
  (274 shorter events, 24.3 us)
Async XLA Ops:
  7.2 3.0 copy-start.45
  7.2 3.0 copy-start.46
  7.2 3.0 copy-start.47
  7.2 3.0 copy-start.48
  7.2 3.1 copy-start.49
  7.2 3.1 copy-start.50
  7.3 3.1 copy-start.51
  7.3 3.1 copy-start.43
  7.3 10.2 %copy-start.20 = (bf16[2,1,640,768]{3,2,1,0:T(8,128)(2,1)S(1)}, bf16[2,1,640,768]{3,2,1,0:T(8,128)(2,1)}, u32[]{:S(2)}) copy-start(bf16[2,1,640,768]{3,2,1,0:T(8,128)(2,1)} %param.16) | copy-start | bytes 5898244
  7.3 35.9 %all-gather.11.cloned.1.call-start = ((), (), s32[]{:S(2)}) async-start(), calls=%async_computation.8 | async-start | bytes 4423680 | tf_op jit(solution)/shard_map/all_gather | solution.py:263
  8.0 54.2 %all-gather.13.cloned.1.call-start = ((), (), s32[]{:S(2)}) async-start(), calls=%async_computation.9 | async-start | bytes 1474560 | tf_op jit(solution)/shard_map/all_gather | solution.py:263
  8.8 92.5 %all-gather.15.cloned.1.call-start = ((), (), s32[]{:S(2)}) async-start(), calls=%async_computation.10 | async-start | bytes 5898240 | tf_op jit(solution)/shard_map/all_gather | solution.py:263
  9.5 130.7 %all-gather.17.cloned.1.call-start = ((), (), s32[]{:S(2)}) async-start(), calls=%async_computation.11 | async-start | bytes 5898240 | tf_op jit(solution)/shard_map/all_gather | solution.py:263
  10.1 440.7 %reduce-scatter.7.cloned.1.call-start = ((), (), s32[]{:S(2)}) async-start(), calls=%async_computation.5 | async-start | bytes 1474560 | tf_op jit(solution)/shard_map/reduce_scatter | solution.py:268
  17.1 191.4 %copy-start.41 = (f32[768]{0:T(1024)}, f32[768]{0:T(1024)S(1)}, u32[]{:S(2)}) copy-start(f32[768]{0:T(1024)S(1)} %reshape.276) | copy-start | bytes 9220
  66.2 93.3 %copy-start.58 = (s32[2,1]{0,1:T(1,128)S(1)}, s32[2,1]{0,1:T(1,128)}, u32[]{:S(2)}) copy-start(s32[2,1]{0,1:T(1,128)} %param.18) | copy-start | bytes 28
  155.7 25.1 %collective-permute-start = (bf16[640,768]{1,0:T(8,128)(2,1)}, bf16[640,768]{1,0:T(8,128)(2,1)S(1)}, u32[]{:S(2)}, u32[]{:S(2)}) collective-permute-start(bf16[640,768]{1,0:T(8,128)(2,1)} %add_convert_fusion.4), channel_id=1, source_target_pairs={{0,16},{1,17},{2,18},{3,19},{4,20},{5,21},{6,22},{7,23},{8,24},{9,... | collective-permute-start | bytes 2949128 | tf_op jit(solution)/shard_map/ppermute | solution.py:300
  181.1 15.0 %copy-start.12 = (bf16[640,768]{1,0:T(8,128)(2,1)}, bf16[640,768]{1,0:T(8,128)(2,1)S(1)}, u32[]{:S(2)}) copy-start(bf16[640,768]{1,0:T(8,128)(2,1)S(1)} %get-tuple-element.127) | copy-start | bytes 2949124
  181.1 91.4 %copy-start.37 = (f32[640]{0:T(1024)}, f32[640]{0:T(1024)S(1)}, u32[]{:S(2)}) copy-start(f32[640]{0:T(1024)S(1)} %broadcast_multiply_fusion.15) | copy-start | bytes 7684
  181.6 91.0 %copy-start.39 = (f32[640]{0:T(1024)}, f32[640]{0:T(1024)S(1)}, u32[]{:S(2)}) copy-start(f32[640]{0:T(1024)S(1)} %add_rsqrt_fusion.3) | copy-start | bytes 7684
  185.7 51.0 %copy-start.2 = (bf16[640,768]{1,0:T(8,128)(2,1)}, bf16[640,768]{1,0:T(8,128)(2,1)S(1)}, u32[]{:S(2)}) copy-start(bf16[640,768]{1,0:T(8,128)(2,1)S(1)} %slice.261.k_ref) | copy-start | bytes 2949124
  186.1 50.6 %copy-start.4 = (bf16[640,768]{1,0:T(8,128)(2,1)}, bf16[640,768]{1,0:T(8,128)(2,1)S(1)}, u32[]{:S(2)}) copy-start(bf16[640,768]{1,0:T(8,128)(2,1)S(1)} %get-tuple-element.132.v_ref) | copy-start | bytes 2949124
  186.1 50.6 %copy-start.6 = (bf16[640,768]{1,0:T(8,128)(2,1)}, bf16[640,768]{1,0:T(8,128)(2,1)S(1)}, u32[]{:S(2)}) copy-start(bf16[640,768]{1,0:T(8,128)(2,1)S(1)} %get-tuple-element.133.q_ref) | copy-start | bytes 2949124
  186.1 10.0 %copy-start.56 = (bf16[1,768,768]{2,1,0:T(8,128)(2,1)S(1)}, bf16[1,768,768]{2,1,0:T(8,128)(2,1)}, u32[]{:S(2)}) copy-start(bf16[1,768,768]{2,1,0:T(8,128)(2,1)} %all-gather.13.cloned.1.call-done) | copy-start | bytes 3538948
  186.1 11.8 %slice-start.6 = ((s8[4718592]{0:T(1024)(128)(4,1)}), s8[4194304]{0:T(1024)(128)(4,1)S(1)}, s32[]{:S(2)}) async-start(s8[4718592]{0:T(1024)(128)(4,1)} %bitcast.219), calls=%async_computation.19 | async-start | bytes 8388608
  197.2 11.3 %copy-start.10 = (f32[640,768]{1,0:T(8,128)}, f32[640,768]{1,0:T(8,128)S(1)}, u32[]{:S(2)}) copy-start(f32[640,768]{1,0:T(8,128)S(1)} %get-tuple-element.160) | copy-start | bytes 5898244
  197.6 11.0 %slice-start = ((s8[4718592]{0:T(1024)(128)(4,1)}), s8[4194304]{0:T(1024)(128)(4,1)S(1)}, s32[]{:S(2)}) async-start(s8[4718592]{0:T(1024)(128)(4,1)} %bitcast.213), calls=%async_computation.13 | async-start | bytes 8388608
  198.0 10.5 %copy-start.31 = (bf16[640,768]{1,0:T(8,128)(2,1)}, bf16[640,768]{1,0:T(8,128)(2,1)S(1)}, u32[]{:S(2)}) copy-start(bf16[640,768]{1,0:T(8,128)(2,1)S(1)} %add_convert_fusion.3) | copy-start | bytes 2949124
  198.0 10.5 %slice-start.1 = ((s8[4718592]{0:T(1024)(128)(4,1)}), s8[524288]{0:T(1024)(128)(4,1)S(1)}, s32[]{:S(2)}) async-start(s8[4718592]{0:T(1024)(128)(4,1)} %bitcast.213), calls=%async_computation.14 | async-start | bytes 1048576
  208.5 4.2 copy-start.63
  212.7 41.4 %collective-permute-start.1 = (bf16[640,768]{1,0:T(8,128)(2,1)}, bf16[640,768]{1,0:T(8,128)(2,1)}, u32[]{:S(2)}, u32[]{:S(2)}) collective-permute-start(bf16[640,768]{1,0:T(8,128)(2,1)} %add_convert_fusion.2), channel_id=1, source_target_pairs={{0,16},{1,17},{2,18},{3,19},{4,20},{5,21},{6,22},{7,23},{8,24},{9,... | collective-permute-start | bytes 2949128 | tf_op jit(solution)/shard_map/ppermute | solution.py:300
  236.7 17.4 %copy-start.21 = (bf16[2,1,640,768]{3,2,1,0:T(8,128)(2,1)S(1)}, bf16[2,1,640,768]{3,2,1,0:T(8,128)(2,1)}, u32[]{:S(2)}) copy-start(bf16[2,1,640,768]{3,2,1,0:T(8,128)(2,1)} %param.16) | copy-start | bytes 5898244
  236.7 18.2 %copy-start.53 = (bf16[1,768,2304]{2,1,0:T(8,128)(2,1)S(1)}, bf16[1,768,2304]{2,1,0:T(8,128)(2,1)}, u32[]{:S(2)}) copy-start(bf16[1,768,2304]{2,1,0:T(8,128)(2,1)} %all-gather.11.cloned.1.call-done) | copy-start | bytes 10616836
  261.0 10.0 %copy-start.57 = (bf16[1,768,768]{2,1,0:T(8,128)(2,1)S(1)}, bf16[1,768,768]{2,1,0:T(8,128)(2,1)}, u32[]{:S(2)}) copy-start(bf16[1,768,768]{2,1,0:T(8,128)(2,1)} %all-gather.13.cloned.1.call-done) | copy-start | bytes 3538948
  272.1 44.9 %copy-start.16 = (f32[640,768]{1,0:T(8,128)}, f32[640,768]{1,0:T(8,128)S(1)}, u32[]{:S(2)}) copy-start(f32[640,768]{1,0:T(8,128)S(1)} %get-tuple-element.164) | copy-start | bytes 5898244
  274.7 27.2 %slice-start.2 = ((s8[4718592]{0:T(1024)(128)(4,1)}), s8[4194304]{0:T(1024)(128)(4,1)S(1)}, s32[]{:S(2)}) async-start(s8[4718592]{0:T(1024)(128)(4,1)} %bitcast.215), calls=%async_computation.15 | async-start | bytes 8388608
  276.8 14.1 %copy-start.32 = (bf16[640,768]{1,0:T(8,128)(2,1)}, bf16[640,768]{1,0:T(8,128)(2,1)S(1)}, u32[]{:S(2)}) copy-start(bf16[640,768]{1,0:T(8,128)(2,1)S(1)} %get-tuple-element.155) | copy-start | bytes 2949124
  276.8 24.7 %collective-permute-start.2 = (bf16[640,768]{1,0:T(8,128)(2,1)S(1)}, bf16[640,768]{1,0:T(8,128)(2,1)S(1)}, u32[]{:S(2)}, u32[]{:S(2)}) collective-permute-start(bf16[640,768]{1,0:T(8,128)(2,1)S(1)} %get-tuple-element.154), channel_id=1, source_target_pairs={{16,0},{17,1},{18,2},{19,3},{20,4},{21,5},{22,6},{23,7},{24,8},{25... | collective-permute-start | bytes 2949128 | tf_op jit(solution)/shard_map/ppermute | solution.py:303
  278.1 23.8 %slice-start.3 = ((s8[4718592]{0:T(1024)(128)(4,1)}), s8[524288]{0:T(1024)(128)(4,1)S(1)}, s32[]{:S(2)}) async-start(s8[4718592]{0:T(1024)(128)(4,1)} %bitcast.215), calls=%async_computation.16 | async-start | bytes 1048576
  278.1 35.1 %slice-start.8 = ((s8[4718592]{0:T(1024)(128)(4,1)}), s8[524288]{0:T(1024)(128)(4,1)S(1)}, s32[]{:S(2)}) async-start(s8[4718592]{0:T(1024)(128)(4,1)} %bitcast.221), calls=%async_computation.21 | async-start | bytes 1048576
  301.9 15.1 %copy-start.23 = (bf16[640,768]{1,0:T(8,128)(2,1)}, bf16[640,768]{1,0:T(8,128)(2,1)S(1)}, u32[]{:S(2)}) copy-start(bf16[640,768]{1,0:T(8,128)(2,1)S(1)} %get-tuple-element.115) | copy-start | bytes 2949124
  301.9 11.3 %slice-start.9 = ((s8[4718592]{0:T(1024)(128)(4,1)}), s8[4194304]{0:T(1024)(128)(4,1)S(1)}, s32[]{:S(2)}) async-start(s8[4718592]{0:T(1024)(128)(4,1)} %bitcast.221), calls=%async_computation.22 | async-start | bytes 8388608
  313.2 3.7 copy-start.62
  343.2 25.1 %slice-start.4 = ((s8[4718592]{0:T(1024)(128)(4,1)}), s8[4194304]{0:T(1024)(128)(4,1)S(1)}, s32[]{:S(2)}) async-start(s8[4718592]{0:T(1024)(128)(4,1)} %bitcast.217), calls=%async_computation.17 | async-start | bytes 8388608
  343.2 25.1 %slice-start.5 = ((s8[4718592]{0:T(1024)(128)(4,1)}), s8[524288]{0:T(1024)(128)(4,1)S(1)}, s32[]{:S(2)}) async-start(s8[4718592]{0:T(1024)(128)(4,1)} %bitcast.217), calls=%async_computation.18 | async-start | bytes 1048576
  343.2 30.7 %slice-start.10 = ((s8[4718592]{0:T(1024)(128)(4,1)}), s8[4194304]{0:T(1024)(128)(4,1)S(1)}, s32[]{:S(2)}) async-start(s8[4718592]{0:T(1024)(128)(4,1)} %bitcast.223), calls=%async_computation.23 | async-start | bytes 8388608
  344.0 30.0 %copy-start.18 = (bf16[640,768]{1,0:T(8,128)(2,1)}, bf16[640,768]{1,0:T(8,128)(2,1)S(1)}, u32[]{:S(2)}) copy-start(bf16[640,768]{1,0:T(8,128)(2,1)S(1)} %fusion.98) | copy-start | bytes 2949124
  344.0 24.0 %collective-permute-start.3 = (bf16[640,768]{1,0:T(8,128)(2,1)S(1)}, bf16[640,768]{1,0:T(8,128)(2,1)S(1)}, u32[]{:S(2)}, u32[]{:S(2)}) collective-permute-start(bf16[640,768]{1,0:T(8,128)(2,1)S(1)} %fusion.98), channel_id=1, source_target_pairs={{16,0},{17,1},{18,2},{19,3},{20,4},{21,5},{22,6},{23,7},{24,8},{25... | collective-permute-start | bytes 2949128 | tf_op jit(solution)/shard_map/ppermute | solution.py:303
  368.3 9.3 %copy-start.24 = (bf16[640,768]{1,0:T(8,128)(2,1)}, bf16[640,768]{1,0:T(8,128)(2,1)S(1)}, u32[]{:S(2)}) copy-start(bf16[640,768]{1,0:T(8,128)(2,1)S(1)} %get-tuple-element.113) | copy-start | bytes 2949124
  368.4 5.6 slice-start.11
  373.9 3.6 copy-start.59
  382.5 70.8 %reduce-scatter.5.cloned.1.call-start = ((), (), s32[]{:S(2)}) async-start(), calls=%async_computation.4 | async-start | bytes 4423680 | tf_op jit(solution)/shard_map/reduce_scatter | solution.py:268
  382.5 3.4 copy-start.3
  382.6 3.4 copy-start.5
  382.6 3.4 copy-start.7
  403.3 3.8 copy-start.34
  413.6 90.1 %reduce-scatter.9.cloned.1.call-start = ((), (), s32[]{:S(2)}) async-start(), calls=%async_computation.6 | async-start | bytes 5898240 | tf_op jit(solution)/shard_map/reduce_scatter | solution.py:268
  424.5 129.7 %reduce-scatter.11.cloned.1.call-start = ((), (), s32[]{:S(2)}) async-start(), calls=%async_computation.7 | async-start | bytes 5898240 | tf_op jit(solution)/shard_map/reduce_scatter | solution.py:268
  435.3 258.5 %all-reduce.3.cloned.1.call-start = ((), (), s32[]{:S(2)}) async-start(), calls=%async_computation.12 | async-start | bytes 7077888 | tf_op jit(solution)/shard_map/psum | solution.py:269
  436.0 9.8 %copy-start.55 = (bf16[1,768,2304]{2,1,0:T(8,128)(2,1)S(1)}, bf16[1,768,2304]{2,1,0:T(8,128)(2,1)}, u32[]{:S(2)}) copy-start(bf16[1,768,2304]{2,1,0:T(8,128)(2,1)} %all-gather.11.cloned.1.call-done) | copy-start | bytes 10616836
  450.8 103.5 %copy-start.1 = (bf16[640,768]{1,0:T(8,128)(2,1)S(1)}, bf16[640,768]{1,0:T(8,128)(2,1)}, u32[]{:S(2)}) copy-start(bf16[640,768]{1,0:T(8,128)(2,1)} %copy-done) | copy-start | bytes 2949124
  554.3 71.2 %copy-start.15 = (bf16[640,768]{1,0:T(8,128)(2,1)S(1)}, bf16[640,768]{1,0:T(8,128)(2,1)}, u32[]{:S(2)}) copy-start(bf16[640,768]{1,0:T(8,128)(2,1)} %copy-done.12) | copy-start | bytes 2949124
  554.5 71.0 %copy-start.19 = (bf16[640,768]{1,0:T(8,128)(2,1)S(1)}, bf16[640,768]{1,0:T(8,128)(2,1)}, u32[]{:S(2)}) copy-start(bf16[640,768]{1,0:T(8,128)(2,1)} %copy-done.18) | copy-start | bytes 2949124
  693.9 4.4 copy-start.28
  (25 other events, 49.3 us)
Sparse Core Ops, SparseCore 0:
  9.7 33.4 all-gather.10
  44.7 17.4 all-gather.12
  63.8 37.4 all-gather.14
  102.7 37.4 all-gather.16
  382.6 24.8 reduce-scatter.6
  413.7 39.5 reduce-scatter.4
  455.8 47.8 reduce-scatter.8
  506.4 47.8 reduce-scatter.10
  556.9 136.9 all-reduce.2

commit v2 on v1

--- a/solution.py
+++ b/solution.py
@@ -14,6 +14,7 @@
 epsilon = 1e-05
 LOW = jnp.bfloat16
 FULL = jnp.float32
+BRIEF = pl.CostEstimate(flops=1024, bytes_accessed=1024, transcendentals=0)
 
 
 def matmul(left, right):
@@ -94,12 +95,139 @@
     dv_ref[...] = value_grad.astype(LOW)
 
 
-def attend_cost(rows, length, products):
-    return pl.CostEstimate(
-        flops=2 * products * rows * length * HEADS * HD * 3,
-        bytes_accessed=rows * HEADS * HD * 2 * (products + 2),
-        transcendentals=rows * length * HEADS,
-    )
+def ffn_up_kernel(mixed_ref, expand_ref, bias_ref, active_ref, slope_ref):
+    rows = mixed_ref.shape[0]
+    part = rows // 4
+    bias = bias_ref[...]
+    for piece in range(4):
+        span = pl.ds(piece * part, part)
+        upper = matmul(mixed_ref[span, :], expand_ref[...]) + bias
+        active, slope = gelu_parts(upper)
+        active_ref[span, :] = active.astype(LOW)
+        slope_ref[span, :] = slope.astype(LOW)
+
+
+def ffn_up(mixed_rows, expand, bias):
+    rows, width = mixed_rows.shape
+    hidden_units = expand.shape[1]
+    step = 512
+    block = pl.BlockSpec((rows, step), lambda j: (0, j))
+    return pl.pallas_call(
+        ffn_up_kernel,
+        grid=(hidden_units // step,),
+        in_specs=[
+            pl.BlockSpec((rows, width), lambda j: (0, 0)),
+            pl.BlockSpec((width, step), lambda j: (0, j)),
+            pl.BlockSpec((1, step), lambda j: (0, j)),
+        ],
+        out_specs=[block, block],
+        out_shape=[jax.ShapeDtypeStruct((rows, hidden_units), LOW)] * 2,
+        compiler_params=pltpu.CompilerParams(vmem_limit_bytes=40 * 1024 * 1024),
+        cost_estimate=BRIEF,
+        name="ffn_up",
+    )(mixed_rows, expand, bias.reshape(1, hidden_units))
+
+
+def ffn_whole_kernel(
+    mixed_ref, expand_ref, bias_ref, contract_ref, hidden_ref, out_bias_ref, active_ref, slope_ref, result_ref, total_ref
+):
+    step = pl.program_id(0)
+
+    @pl.when(step == 0)
+    def _():
+        total_ref[...] = hidden_ref[...] + out_bias_ref[...]
+
+    rows = mixed_ref.shape[0]
+    part = rows // 4
+    bias = bias_ref[...]
+    for piece in range(4):
+        span = pl.ds(piece * part, part)
+        upper = matmul(mixed_ref[span, :], expand_ref[...]) + bias
+        active, slope = gelu_parts(upper)
+        active = active.astype(LOW)
+        active_ref[span, :] = active
+        slope_ref[span, :] = slope.astype(LOW)
+        total_ref[span, :] += matmul(active, contract_ref[...])
+
+    @pl.when(step == pl.num_programs(0) - 1)
+    def _():
+        result_ref[...] = total_ref[...].astype(LOW)
+
+
+def ffn_whole(mixed_rows, expand, bias, contract, hidden, out_bias):
+    rows, width = mixed_rows.shape
+    hidden_units = expand.shape[1]
+    step = 512
+    block = pl.BlockSpec((rows, step), lambda j: (0, j))
+    whole = pl.BlockSpec((rows, width), lambda j: (0, 0))
+    return pl.pallas_call(
+        ffn_whole_kernel,
+        grid=(hidden_units // step,),
+        in_specs=[
+            whole,
+            pl.BlockSpec((width, step), lambda j: (0, j)),
+            pl.BlockSpec((1, step), lambda j: (0, j)),
+            pl.BlockSpec((step, width), lambda j: (j, 0)),
+            whole,
+            pl.BlockSpec((1, width), lambda j: (0, 0)),
+        ],
+        out_specs=[block, block, whole],
+        out_shape=[
+            jax.ShapeDtypeStruct((rows, hidden_units), LOW),
+            jax.ShapeDtypeStruct((rows, hidden_units), LOW),
+            jax.ShapeDtypeStruct((rows, width), LOW),
+        ],
+        scratch_shapes=[pltpu.VMEM((rows, width), FULL)],
+        compiler_params=pltpu.CompilerParams(vmem_limit_bytes=44 * 1024 * 1024),
+        cost_estimate=BRIEF,
+        name="ffn_whole",
+    )(mixed_rows, expand, bias.reshape(1, hidden_units), contract, hidden, out_bias.reshape(1, width))
+
+
+def ffn_back_kernel(grad_ref, contract_ref, slope_ref, expand_ref, upper_ref, mixed_ref, sum_ref):
+    @pl.when(pl.program_id(0) == 0)
+    def _():
+        mixed_ref[...] = jnp.zeros_like(mixed_ref)
+
+    rows = grad_ref.shape[0]
+    part = rows // 2
+    total = None
+    for piece in range(2):
+        span = pl.ds(piece * part, part)
+        grad_active = matmul_right(grad_ref[span, :], contract_ref[...])
+        grad_upper = (grad_active * slope_ref[span, :].astype(FULL)).astype(LOW)
+        upper_ref[span, :] = grad_upper
+        column = jnp.sum(grad_upper.astype(FULL), axis=0, keepdims=True)
+        total = column if total is None else total + column
+        mixed_ref[span, :] += matmul_right(grad_upper, expand_ref[...])
+    sum_ref[...] = total
+
+
+def ffn_back(grad_low, contract, slope, expand):
+    rows, width = grad_low.shape
+    hidden_units = contract.shape[0]
+    step = 512
+    block = pl.BlockSpec((rows, step), lambda j: (0, j))
+    whole = pl.BlockSpec((rows, width), lambda j: (0, 0))
+    return pl.pallas_call(
+        ffn_back_kernel,
+        grid=(hidden_units // step,),
+        in_specs=[
+            whole,
+            pl.BlockSpec((step, width), lambda j: (j, 0)),
+            block,
+            pl.BlockSpec((width, step), lambda j: (0, j)),
+        ],
+        out_specs=[block, whole, pl.BlockSpec((1, step), lambda j: (0, j))],
+        out_shape=[
+            jax.ShapeDtypeStruct((rows, hidden_units), LOW),
+            jax.ShapeDtypeStruct((rows, width), FULL),
+            jax.ShapeDtypeStruct((1, hidden_units), FULL),
+        ],
+        compiler_params=pltpu.CompilerParams(vmem_limit_bytes=40 * 1024 * 1024),
+        cost_estimate=BRIEF,
+        name="ffn_back",
+    )(grad_low, contract, slope, expand)
 
 
 def attend_forward(clips, length, queries, key_rows, value_rows):
@@ -117,24 +245,26 @@
             jax.ShapeDtypeStruct((clips * pairs, 8, length), FULL),
         ],
         compiler_params=pltpu.CompilerParams(vmem_limit_bytes=40 * 1024 * 1024),
-        cost_estimate=attend_cost(rows, length, 2),
+        cost_estimate=BRIEF,
         name="attend_forward",
     )(queries, key_rows, value_rows)
 
 
-def attend_backward(clips, length, queries, key_rows, value_rows, lse, grad_context):
+def attend_backward(clips, length, queries, key_rows, value_rows, lse, grad_context, low=0, high=None):
     rows, width = queries.shape
     pairs = width // PAIR
-    block = pl.BlockSpec((length, PAIR), lambda c, j: (c, j))
-    lse_block = pl.BlockSpec((1, 8, length), lambda c, j: (c * pairs + j, 0, 0))
+    high = pairs if high is None else high
+    block = pl.BlockSpec((length, PAIR), lambda c, j: (c, low + j))
+    lse_block = pl.BlockSpec((1, 8, length), lambda c, j: (c * pairs + low + j, 0, 0))
+    out_block = pl.BlockSpec((length, PAIR), lambda c, j: (c, j))
     return pl.pallas_call(
         attend_back_kernel,
-        grid=(clips, pairs),
+        grid=(clips, high - low),
         in_specs=[block] * 3 + [lse_block, block],
-        out_specs=[block] * 3,
-        out_shape=[jax.ShapeDtypeStruct((rows, width), LOW)] * 3,
+        out_specs=[out_block] * 3,
+        out_shape=[jax.ShapeDtypeStruct((rows, (high - low) * PAIR), LOW)] * 3,
         compiler_params=pltpu.CompilerParams(vmem_limit_bytes=48 * 1024 * 1024),
-        cost_estimate=attend_cost(rows, length, 5),
+        cost_estimate=BRIEF,
         name="attend_backward",
     )(queries, key_rows, value_rows, lse, grad_context)
 
@@ -156,42 +286,66 @@
     return upper * below, below + upper * bell * (1.0 / math.sqrt(2.0 * math.pi))
 
 
-def layer_forward(weights, clips, length, rows_in):
+def layer_forward(weights, clips, length, rows_in, begin=None, before=None, after=None, last=None):
     width = rows_in.shape[1]
     token_rows = rows_in.astype(FULL)
     normal_one, _ = row_stats(token_rows)
     normed = (normal_one * weights["gain_one"] + weights["shift_one"]).astype(LOW)
+    if begin is not None:
+        normed = begin(normed)
     projected = matmul(normed, weights["project"])
     queries = (projected[:, :width] + weights["bias_query"]).astype(LOW)
     key_rows = projected[:, width : 2 * width].astype(LOW)
     value_rows = (projected[:, 2 * width :] + weights["bias_value"]).astype(LOW)
+    if before is not None:
+        queries = before(queries)
     context, lse = attend_forward(clips, length, queries, key_rows, value_rows)
+    if after is not None:
+        context = after(context)
     hidden = token_rows + (matmul(context, weights["output"]) + weights["bias_output"])
     normal_two, _ = row_stats(hidden)
     mixed_rows = (normal_two * weights["gain_two"] + weights["shift_two"]).astype(LOW)
-    upper = matmul(mixed_rows, weights["expand"]) + weights["bias_expand"]
-    active, slope = gelu_parts(upper)
-    active = active.astype(LOW)
-    slope = slope.astype(LOW)
-    result = (hidden + (matmul(active, weights["contract"]) + weights["bias_contract"])).astype(LOW)
+    if last is not None:
+        active, slope = ffn_up(mixed_rows, weights["expand"], weights["bias_expand"])
+        active = last(active)
+        result = (hidden + (matmul(active, weights["contract"]) + weights["bias_contract"])).astype(LOW)
+    else:
+        active, slope, result = ffn_whole(
+            mixed_rows,
+            weights["expand"],
+            weights["bias_expand"],
+            weights["contract"],
+            hidden,
+            weights["bias_contract"],
+        )
     kept = (rows_in, normed, queries, key_rows, value_rows, lse, context, hidden, mixed_rows, active, slope)
     return result, kept
 
 
-def layer_backward(weights, clips, length, kept, grad_low, grad_full):
+def tie(value, *others):
+    return lax.optimization_barrier((value,) + others)[0]
+
+
+def layer_backward(weights, clips, length, kept, grad_low, weight_grad):
     rows_in, normed, queries, key_rows, value_rows, lse, context, hidden, mixed_rows, active, slope = kept
-    grad_upper = (matmul_right(grad_low, weights["contract"]) * slope).astype(LOW)
-    grad_mixed = matmul_right(grad_upper, weights["expand"])
+    grad_full = grad_low.astype(FULL)
+    grad_low = weight_grad("contract", active, grad_low, grad_low)
+    grad_upper, grad_mixed, bias_expand_grad = ffn_back(
+        grad_low, weights["contract"], slope, weights["expand"]
+    )
+    grad_mixed = weight_grad("expand", mixed_rows, grad_upper, grad_mixed)
     normal_two, factor_two = row_stats(hidden)
     gain_two_grad = jnp.sum(grad_mixed * normal_two, axis=0)
     shift_two_grad = jnp.sum(grad_mixed, axis=0)
     grad_hidden = grad_full + norm_back(grad_mixed * weights["gain_two"], normal_two, factor_two)
     grad_attended = grad_hidden.astype(LOW)
     grad_context = matmul_right(grad_attended, weights["output"]).astype(LOW)
+    grad_context = weight_grad("output", context, grad_attended, grad_context)
     grad_queries, grad_keys, grad_values = attend_backward(
         clips, length, queries, key_rows, value_rows, lse, grad_context
     )
     grad_proj = jnp.concatenate([grad_queries, grad_keys, grad_values], 1)
+    grad_proj = weight_grad("project", normed, grad_proj, grad_proj)
     grad_normed = matmul_right(grad_proj, weights["project"])
     normal_one, factor_one = row_stats(rows_in.astype(FULL))
     gain_one_grad = jnp.sum(grad_normed * normal_one, axis=0)
@@ -209,16 +363,10 @@
         bias_output=total(grad_attended),
         gain_two=gain_two_grad,
         shift_two=shift_two_grad,
-        bias_expand=total(grad_upper),
+        bias_expand=bias_expand_grad[0],
         bias_contract=total(grad_low),
     )
-    factors = dict(
-        contract=(active, grad_low),
-        expand=(mixed_rows, grad_upper),
-        output=(context, grad_attended),
-        project=(normed, grad_proj),
-    )
-    return grad_in.astype(LOW), small, factors
+    return grad_in.astype(LOW), small
 
 
 SMALL = (
@@ -250,48 +398,205 @@
 )
 
 
-def gather_weights(shards):
-    weights = {}
-    packed = jnp.concatenate([shards[name] for name in SMALL], 0)[None]
-    spread = lax.all_gather(packed, "fsdp", axis=0, tiled=True)
-    place = 0
-    for name in SMALL:
-        size = shards[name].shape[0]
-        weights[name] = spread[:, place : place + size].reshape(-1).astype(FULL)
-        place += size
-    for name in LARGE:
-        weights[name] = lax.all_gather(shards[name], "fsdp", axis=0, tiled=True)
+def partner(axis, bit):
+    return [(i, i ^ bit) for i in range(lax.axis_size(axis))]
+
+
+def swap(block, axis, bit):
+    return lax.ppermute(block, axis, partner(axis, bit))
+
+
+def pick(stack, index, axis):
+    return lax.dynamic_index_in_dim(stack, index, axis, keepdims=False)
+
+
+def small_mesh():
+    return lax.axis_size("fsdp") == 4 and lax.axis_size("rep") == 4
+
+
+def order_kernel(place_ref, here_ref, there_ref, whole_ref, sems):
+    rows = here_ref.shape[0] // 2
+    half = rows // 2
+    copies = []
+    for source, ref in enumerate((here_ref, there_ref)):
+        for piece, (start, size) in enumerate(((0, rows), (rows, half), (rows + half, half))):
+            target = pl.multiple_of(place_ref[source, piece], 16)
+            copies.append(
+                pltpu.make_async_copy(
+                    ref.at[pl.ds(start, size)],
+                    whole_ref.at[pl.ds(target, size)],
+                    sems.at[source, piece],
+                )
+            )
+    for copy in copies:
+        copy.start()
+    for copy in copies:
+        copy.wait()
+
+
+def in_order(places, here, there):
+    return pl.pallas_call(
+        order_kernel,
+        in_specs=[
+            pl.BlockSpec(memory_space=pltpu.SMEM),
+            pl.BlockSpec(memory_space=pl.ANY),
+            pl.BlockSpec(memory_space=pl.ANY),
+        ],
+        out_specs=pl.BlockSpec(memory_space=pltpu.VMEM),
+        out_shape=jax.ShapeDtypeStruct((2 * here.shape[0], here.shape[1]), here.dtype),
+        scratch_shapes=[pltpu.SemaphoreType.DMA((2, 3))],
+        compiler_params=pltpu.CompilerParams(vmem_limit_bytes=32 * 1024 * 1024),
+        cost_estimate=BRIEF,
+        name="shards_in_order",
+    )(places, here, there)
+
+
+class GatherChain:
+    def __init__(self, shard, halves):
+        self.shard = shard
+        self.halves = halves
+        if not small_mesh():
+            self.mine = lax.all_gather(shard, "fsdp", axis=0, tiled=True)
+            return
+        rows, columns = shard.shape
+        self.side = lax.axis_index("rep") % 2 if halves else jnp.int32(0)
+        sent = pick(shard.reshape(2, rows // 2, columns), self.side, 0) if halves else shard
+        self.mine = swap(sent, "fsdp", 2)
+
+    def arrive(self, token):
+        self.mine, token = lax.optimization_barrier((self.mine, token))
+        return token
+
+    def pass_on(self):
+        if small_mesh() and self.halves:
+            self.other = swap(self.mine, "rep", 1)
+
+    def finish(self):
+        if not small_mesh():
+            return self.mine
+        rows = self.shard.shape[0]
+        half = rows // 2
+        spot = lax.axis_index("fsdp")
+        pieces = [self.shard, self.mine] + ([self.other] if self.halves else [])
+        here = jnp.concatenate(pieces, 0)
+        there = swap(here, "fsdp", 1)
+        places = jnp.stack(
+            [
+                jnp.stack(
+                    [base * rows, (base ^ 2) * rows + self.side * half, (base ^ 2) * rows + (1 - self.side) * half]
+                )
+                for base in (spot, spot ^ 1)
+            ]
+        ).astype(jnp.int32)
+        return in_order(places, here, there)
+
+
+def gather_small(packed):
+    if not small_mesh():
+        return lax.all_gather(packed, "fsdp", axis=0, tiled=True)
+    spot = lax.axis_index("fsdp")
+    far = swap(packed, "fsdp", 2)
+    low = spot < 2
+    here = jnp.stack([jnp.where(low, packed, far), jnp.where(low, far, packed)])
+    there = swap(here, "fsdp", 1)
+    even = spot % 2 == 0
+    spread = jnp.concatenate([jnp.where(even, here, there), jnp.where(even, there, here)], 1)
+    return spread.reshape(4, packed.shape[1])
+
+
+def gather_vectors(vectors):
+    packed = jnp.concatenate([vectors[name] for name in SMALL], 1)
+    spread = gather_small(packed)
+    devices = spread.shape[0]
+    size = vectors["gain_one"].shape[1]
+    count = len(SMALL) - 1
+    rows = spread[:, : count * size].reshape(devices, count, size).transpose(1, 0, 2)
+    rows = rows.reshape(count, devices * size).astype(FULL)
+    weights = {name: rows[i] for i, name in enumerate(SMALL[:-1])}
+    weights[SMALL[-1]] = spread[:, count * size :].reshape(-1).astype(FULL)
     return weights
 
 
-def reduce_large(grad):
-    owned = lax.psum_scatter(grad.astype(LOW), "fsdp", scatter_dimension=0, tiled=True)
-    return lax.psum(owned, "rep").astype(FULL)
-
-
-def reduce_small(small, shards):
-    packed = jnp.concatenate([small[name] for name in SMALL], 0)
-    whole = lax.psum(packed.reshape(-1, 128), ("fsdp", "rep")).reshape(-1)
-    index = lax.axis_index("fsdp")
+def plus(left, right):
+    return (left.astype(FULL) + right.astype(FULL)).astype(LOW)
+
+
+class ReduceChain:
+    def __init__(self, grad):
+        self.grad = grad
+        self.step = 0
+        if not small_mesh():
+            return
+        self.spot = lax.axis_index("fsdp")
+        self.side = lax.axis_index("rep") % 2
+        split = grad.reshape((2, 2) + grad.shape[1:])
+        self.keep = pick(split, self.spot % 2, 1)
+        self.come = swap(pick(split, 1 - self.spot % 2, 1), "fsdp", 1)
+
+    def advance(self, token):
+        if not small_mesh():
+            return token
+        come, token = lax.optimization_barrier((self.come, token))
+        self.step += 1
+        if self.step == 5:
+            even = self.side == 0
+            low = jnp.where(even, self.keep, come)
+            high = jnp.where(even, come, self.keep)
+            self.owned = jnp.concatenate([low, high], 0).astype(FULL)
+            return token
+        total = plus(self.keep, come)
+        if self.step == 1:
+            self.keep = pick(total, self.spot // 2, 0)
+            self.come = swap(pick(total, 1 - self.spot // 2, 0), "fsdp", 2)
+        elif self.step == 2:
+            halves = total.reshape(2, total.shape[0] // 2, total.shape[1])
+            self.keep = pick(halves, self.side, 0)
+            self.come = swap(pick(halves, 1 - self.side, 0), "rep", 1)
+        elif self.step == 3:
+            self.keep = total
+            self.come = swap(total, "rep", 2)
+        else:
+            self.keep = total
+            self.come = swap(total, "rep", 1)
+        return tie(token, total)
+
+    def finish(self):
+        if not small_mesh():
+            owned = lax.psum_scatter(self.grad, "fsdp", scatter_dimension=0, tiled=True)[0]
+            return lax.psum(owned, "rep").astype(FULL)
+        return self.owned
+
+
+def pack_vectors(small, devices, width):
+    parts = [small[name].reshape(devices, -1) for name in SMALL]
+    packed = jnp.concatenate(parts, 1)
+    rows = -(-packed.shape[1] // (32 * width)) * 32
+    packed = jnp.pad(packed, ((0, 0), (0, rows * width - packed.shape[1])))
+    return packed.reshape(devices, rows, width).astype(LOW)
+
+
+def unpack_vectors(rows, vectors):
+    flat = rows.reshape(-1)
     place = 0
     owned = {}
     for name in SMALL:
-        size = small[name].shape[0]
-        part = shards[name].shape[0]
-        owned[name] = lax.dynamic_slice_in_dim(whole[place : place + size], index * part, part)
+        size = vectors[name].shape[1]
+        owned[name] = flat[place : place + size]
         place += size
     return owned
 
 
 def local(inputs, cotangent, live_slots, *params):
-    shards = {name: part[0] for name, part in zip(ORDER, params)}
+    vectors = {name: part for name, part in zip(ORDER, params) if name in SMALL}
+    shards = {name: part[0] for name, part in zip(ORDER, params) if name in LARGE}
     micro_count, clips, length, width = inputs.shape
     rows = clips * length
     first = lax.axis_index("section") == 0
     inputs = inputs.reshape(micro_count, rows, width)
     live = jnp.repeat(live_slots.reshape(micro_count, clips, 1), length, axis=1)
     cotangent = cotangent.reshape(micro_count, rows, width) * (live == 1).astype(LOW)
-    weights = gather_weights(shards)
+    gathers = {name: GatherChain(shards[name], name in ("project", "expand")) for name in LARGE}
+    weights = gather_vectors(vectors)
 
     def forward(rows_in):
         return layer_forward(weights, clips, length, rows_in)
@@ -302,27 +607,109 @@
     def back(grad_rows):
         return lax.ppermute(grad_rows, "section", [(1, 0)])
 
-    out_a, _ = forward(inputs[0])
+    def begin(normed):
+        chain = gathers["project"]
+        normed = chain.arrive(normed)
+        chain.pass_on()
+        weights["project"] = chain.finish()
+        return normed
+
+    def before(queries):
+        chain = gathers["expand"]
+        queries = chain.arrive(queries)
+        chain.pass_on()
+        return queries
+
+    def after(context):
+        for name in ("output", "expand"):
+            chain = gathers[name]
+            context = chain.arrive(context)
+            weights[name] = chain.finish()
+        return context
+
+    def last(active):
+        chain = gathers["contract"]
+        active = chain.arrive(active)
+        weights["contract"] = chain.finish()
+        return active
+
+    out_a, _ = layer_forward(weights, clips, length, inputs[0], begin, before, after, last)
     out_b, kept_odd = forward(jnp.where(first, inputs[1], onward(out_a)))
-    out_c, kept_even = forward(jnp.where(first, inputs[0], onward(out_b)))
+
+    def backward(kept, grad_low, weight_grad):
+        return layer_backward(weights, clips, length, kept, grad_low, weight_grad)
+
+    factors = {}
+    chains = {}
+    grads = {}
+
+    devices = lax.axis_size("fsdp")
+
+    def no_grad(name, left, right, onto):
+        return onto
+
+    def first_grad(name, left, right, onto):
+        factors[name] = (left, right)
+        return onto
+
+    def start_chains(name, grad):
+        split = grad.reshape(devices, grad.shape[0] // devices, grad.shape[1])
+        count = 1 if name == "output" else 2
+        part = split.shape[1] // count
+        for piece in range(count):
+            chains[name, piece] = ReduceChain(split[:, piece * part : (piece + 1) * part])
+
+    def last_grad(name, left, right, onto):
+        onto = advance(onto, ahead[name])
+        old_left, old_right = factors[name]
+        left = jnp.concatenate([old_left, left], 0)
+        right = jnp.concatenate([old_right, right], 0)
+        if name == "output":
+            grads[name] = matmul_left(left, right).astype(LOW)
+        else:
+            grad = matmul_left(left, tie(right, onto)).astype(LOW)
+            start_chains(name, grad)
+            onto = tie(onto, grad)
+        return advance(onto, behind[name])
+
+    con, exp, pro, out = "contract", "expand", "project", "output"
+    p0, p1, e0, e1, c0, c1, o0 = (pro, 0), (pro, 1), (exp, 0), (exp, 1), (con, 0), (con, 1), (out, 0)
+    ahead = {con: (), exp: (c0,), out: (), pro: (e0, c0, c1)}
+    behind = {con: (c0, c1), exp: (c0,), out: (e0, e1, c1, c1), pro: (p0, p1, e1)}
+
+    def advance(token, dues):
+        for due in dues:
+            token = chains[due].advance(token)
+        return token
+
+    received = onward(out_b)
+    grad_a, _ = backward(kept_odd, cotangent[0], no_grad)
+    returned = back(grad_a)
+    out_c, kept_even = forward(tie(jnp.where(first, inputs[0], received), grad_a))
     section_outputs = jnp.stack([jnp.where(first, out_c, out_b), jnp.where(first, out_b, out_c)])
 
-    def backward(kept, grad_low):
-        return layer_backward(weights, clips, length, kept, grad_low, grad_low.astype(FULL))
-
-    grad_a, _, _ = backward(kept_odd, cotangent[0])
-    grad_b, small_b, factors_b = backward(kept_even, jnp.where(first, back(grad_a), cotangent[1]))
-    grad_c, small_c, factors_c = backward(kept_odd, jnp.where(first, back(grad_b), cotangent[0]))
+    grad_b, small_b = backward(kept_even, jnp.where(first, returned, cotangent[1]), first_grad)
+    returned = back(grad_b)
+    section_outputs, returned = lax.optimization_barrier((section_outputs, returned))
+    grad_c, small_c = backward(kept_odd, jnp.where(first, returned, cotangent[0]), last_grad)
+
+    small = {name: small_b[name] + small_c[name] for name in SMALL}
+    extra = pack_vectors(small, devices, width)
+    last = grads["output"].reshape(devices, -1, width)
+    chains["output", 0] = ReduceChain(jnp.concatenate([last, extra], 1))
+    grad_c = advance(
+        grad_c,
+        (o0, e0, e1, c0, c1, p0, e0, p1, p0, e1, e0, p1, o0, p0, o0, e1, p1, p0, o0, p1, o0),
+    )
     section_input_grads = jnp.stack([jnp.where(first, grad_b, grad_c), jnp.where(first, grad_c, grad_b)])
-
-    owned = {}
-    for name in ("contract", "expand", "output", "project"):
-        (left_b, right_b), (left_c, right_c) = factors_b[name], factors_c[name]
-        left = jnp.concatenate([left_b, left_c], 0)
-        right = jnp.concatenate([right_b, right_c], 0)
-        owned[name] = reduce_large(matmul_left(left, right))
-    small = {name: small_b[name] + small_c[name] for name in SMALL}
-    owned.update(reduce_small(small, shards))
+    owned = {
+        name: jnp.concatenate([chains[name, piece].finish() for piece in range(2)], 0)
+        for name in (con, exp, pro)
+    }
+    tail = chains[out, 0].finish()
+    count = last.shape[1]
+    owned[out] = tail[:count]
+    owned.update(unpack_vectors(tail[count:], vectors))
     shape_out = (1, micro_count, clips, length, width)
     return (
         section_outputs.reshape(shape_out),

time: 712 us -> 582 us (0.82)
  waiting for transfers between devices: 324 us -> 144 us
  matrix products: 153 us -> 58.5 us
  Pallas kernels: 82.5 us -> 170 us
  blocking collectives: 71.2 us -> 0 us
  other arithmetic: 30.5 us -> 86.3 us
  starting transfers between devices: 12.7 us -> 56.6 us
  local copies, waits for them, and re-layouts: 19.3 us -> 59.6 us
  between operations: 15.5 us -> 2.92 us
    ppermute x0 -> x47, waiting for transfers between devices: none -> 105 us  [swap(): return lax.ppermute(block, axis, partner(axis, bit))]
    reduce_scatter x4 -> x0, waiting for transfers between devices: 103 us -> none  [reduce_large(): lax.psum_scatter(grad.astype(LOW), 'fsdp', scatter_dimension=0, tiled=True)]
    all_gather x4 -> x0, waiting for transfers between devices: 102 us -> none  [gather_weights(): weights[name] = lax.all_gather(shards[name], 'fsdp', axis=0, tiled=True)]
    pallas_call x3 -> x13, Pallas kernels: 51.8 us -> 139 us  [the longest x3 51.8 us: attend_backward(): pl.pallas_call(attend_back_kernel, grid=(clips, high - low), in_specs=[bl...]
    psum x1 -> x0, blocking collectives: 65 us -> none  [reduce_small(): whole = lax.psum(packed.reshape(-1, 128), ('fsdp', 'rep')).reshape(-1)]
    psum x1 -> x0, waiting for transfers between devices: 64.1 us -> none  [reduce_large(): return lax.psum(owned, 'rep').astype(FULL)]
    dot_general x11 -> x7, matrix products: 64.7 us -> 16.2 us  [matmul(): return jnp.dot(left, right, preferred_element_type=FULL)]
    ppermute x0 -> x47, starting transfers between devices: none -> 44.8 us  [swap(): return lax.ppermute(block, axis, partner(axis, bit))]
  transfers between devices with their start and end apart: 13 -> 51, of which waited for: 11 -> 21; matrix products, arithmetic and copies ran while one was open for 14% -> 23% of each run, Pallas kernels for 6% -> 17%
where the time goes in v2:
time: 582 us; the launch traced here: 578 us
  Pallas kernels  170 us (29%)
  waiting for transfers between devices  144 us (25%)
  other arithmetic  86.3 us (15%)
  local copies, waits for them, and re-layouts  59.6 us (10%)
  matrix products  58.5 us (10%)
  starting transfers between devices  56.6 us (10%)
    ppermute x47, waiting for transfers between devices, swap(): return lax.ppermute(block, axis, partner(axis, bit))  105 us
    pallas_call x3, Pallas kernels, attend_backward(): pl.pallas_call(attend_back_kernel, grid=(clips, high - low), in_specs=[bl...  51.8 us
    ppermute x47, starting transfers between devices, swap(): return lax.ppermute(block, axis, partner(axis, bit))  44.8 us
    pallas_call x2, Pallas kernels, ffn_whole(): pl.pallas_call(ffn_whole_kernel, grid=(hidden_units // step,), in_specs=[...  35.1 us
    pallas_call x3, Pallas kernels, ffn_back(): pl.pallas_call(ffn_back_kernel, grid=(hidden_units // step,), in_specs=[w...  32.4 us
    pallas_call x3, Pallas kernels, attend_forward(): pl.pallas_call(attend_kernel, grid=(clips, pairs), in_specs=[block] * 3,...  30.7 us
    unnamed x238, local copies, waits for them, and re-layouts  28 us
    dot_general x4, matrix products, matmul_left(): lax.dot_general(left, right, (((0,), (0,)), ((), ())), preferred_element_...  25.4 us
  transfers between devices with their start and end apart: 51, of which 21 were waited for; matrix products, arithmetic and copies ran while one was open for 23% of the time, Pallas kernels for 17%

profile of v2, /device:TPU:0, one launch (start us, length us, event | category | flops | bytes accessed | tf_op | source)
XLA Modules:
  0.0 577.6 jit_solution(4077451902407241351)
XLA Ops:
  1.7 3.0 collective-permute-start.2
  13.5 4.9 collective-permute-done.1
  20.0 9.1 %collective-permute-done.4 = bf16[96,2304]{1,0:T(8,128)(2,1)S(1)} collective-permute-done((bf16[96,2304]{1,0:T(8,128)(2,1)S(1)}, bf16[96,2304]{1,0:T(8,128)(2,1)S(1)}, u32[]{:S(2)}, u32[]{:S(2)}) %collective-permute-start.4) | collective-permute-done | bytes 442400 | tf_op jit(solution)/shard_map/ppermute | solution.py:406
  33.0 2.5 shards_in_order.4
  35.5 2.5 fusion.126
  38.4 7.8 %collective-permute-done = bf16[96,3072]{1,0:T(8,128)(2,1)} collective-permute-done((bf16[96,3072]{1,0:T(8,128)(2,1)}, bf16[96,3072]{1,0:T(8,128)(2,1)}, u32[]{:S(2)}, u32[]{:S(2)}) %collective-permute-start) | collective-permute-done | bytes 589856 | tf_op jit(solution)/shard_map/ppermute | solution.py:406
  48.4 10.6 %attend_forward.3 = (bf16[640,768]{1,0:T(8,128)(2,1)S(1)}, f32[6,8,640]{2,1,0:T(8,128)}) custom-call(bf16[640,768]{1,0:T(8,128)(2,1)S(1)} %get-tuple-element.163.q_ref, bf16[640,768]{1,0:T(8,128)(2,1)S(1)} %slice.269.k_ref, bf16[640,768]{1,0:T(8,128)(2,1)S(1)} %get-tuple-element.377.v_ref), custom_call_target="tpu_custom_call" | custom-call | flops 1024 | bytes 1024 | tf_op jit(solution)/shard_map/attend_forward/pallas_call | solution.py:238
  59.0 2.3 collective-permute-done.9
  71.6 2.7 fusion.123
  75.5 2.7 shards_in_order.6.expand_ref
  78.2 10.3 %ffn_up.1 = (bf16[640,3072]{1,0:T(8,128)(2,1)S(1)}, bf16[640,3072]{1,0:T(8,128)(2,1)}) custom-call(bf16[640,768]{1,0:T(8,128)(2,1)S(1)} %add_convert_fusion.3.mixed_ref, bf16[768,3072]{1,0:T(8,128)(2,1)S(1)} %shards_in_order.6.expand_ref, f32[1,3072]{1,0:T(1,128)S(1)} %bitcast.282), custom_call_target="tpu_custom_call" | custom-call | flops 1024 | bytes 1024 | tf_op jit(solution)/shard_map/ffn_up/pallas_call | solution.py:115
  88.5 3.0 collective-permute-done.8
  93.6 4.5 collective-permute-done.11.there_ref
  98.1 2.7 shards_in_order.7.contract_ref
  100.8 4.2 add_convert_fusion.2
  105.0 3.6 collective-permute-start.12
  108.6 3.2 bitcast_multiply_fusion
  111.9 18.1 %collective-permute-done.12 = bf16[640,768]{1,0:T(8,128)(2,1)S(1)} collective-permute-done((bf16[640,768]{1,0:T(8,128)(2,1)}, bf16[640,768]{1,0:T(8,128)(2,1)S(1)}, u32[]{:S(2)}, u32[]{:S(2)}) %collective-permute-start.12) | collective-permute-done | bytes 983072 | tf_op jit(solution)/shard_map/ppermute | solution.py:605
  132.3 2.5 fusion.127
  135.9 10.0 %attend_forward.4 = (bf16[640,768]{1,0:T(8,128)(2,1)S(1)}, f32[6,8,640]{2,1,0:T(8,128)S(1)}) custom-call(bf16[640,768]{1,0:T(8,128)(2,1)S(1)} %get-tuple-element.376.q_ref, bf16[640,768]{1,0:T(8,128)(2,1)S(1)} %slice.268.k_ref, bf16[640,768]{1,0:T(8,128)(2,1)S(1)} %get-tuple-element.375.v_ref), custom_call_target="tpu_custom_call" | custom-call | flops 1024 | bytes 1024 | tf_op jit(solution)/shard_map/attend_forward/pallas_call | solution.py:238
  149.0 17.6 %ffn_whole.2 = (bf16[640,3072]{1,0:T(8,128)(2,1)S(1)}, bf16[640,3072]{1,0:T(8,128)(2,1)}, bf16[640,768]{1,0:T(8,128)(2,1)}) custom-call(bf16[640,768]{1,0:T(8,128)(2,1)S(1)} %add_convert_fusion.1.mixed_ref, bf16[768,3072]{1,0:T(8,128)(2,1)} %copy-done, f32[1,3072]{1,0:T(1,128)S(1)} %bitcast.283, bf16[3072,768]{1,0:T(8,128)(2,1)} %copy-done.1, ...), custom_call_target="tpu_custom_call" | custom-call | flops 1024 | bytes 1024 | tf_op jit(solution)/shard_map/ffn_whole/pallas_call | solution.py:163
  168.5 5.6 collective-permute-start.13
  174.1 2.1 copy-done.2
  176.2 11.0 %ffn_back.3 = (bf16[640,3072]{1,0:T(8,128)(2,1)}, f32[640,768]{1,0:T(8,128)S(1)}, f32[1,3072]{1,0:T(1,128)}) custom-call(bf16[640,768]{1,0:T(8,128)(2,1)S(1)} %slice_bitcast_fusion.1.grad_ref, bf16[3072,768]{1,0:T(8,128)(2,1)} %copy-done.1, bf16[640,3072]{1,0:T(8,128)(2,1)S(1)} %copy-done.2, bf16[768,3072]{1,0:T(8,128)(2,1)} %copy-done), custom_call_target="tpu_custom_call" | custom-call | flops 1024 | bytes 1024 | tf_op jit(solution)/shard_map/ffn_back/pallas_call | solution.py:212
  188.7 2.3 convolution_convert_fusion.4.g_ref
  191.1 17.3 %attend_backward.3 = (bf16[640,768]{1,0:T(8,128)(2,1)S(1)}, bf16[640,768]{1,0:T(8,128)(2,1)S(1)}, bf16[640,768]{1,0:T(8,128)(2,1)S(1)}) custom-call(bf16[640,768]{1,0:T(8,128)(2,1)S(1)} %get-tuple-element.376.q_ref, bf16[640,768]{1,0:T(8,128)(2,1)S(1)} %slice.268.k_ref, bf16[640,768]{1,0:T(8,128)(2,1)S(1)} %get-tuple-element.375.v_ref, ...), custom_call_target="tpu_custom_call" | custom-call | flops 1024 | bytes 1024 | tf_op jit(solution)/shard_map/attend_backward/pallas_call | solution.py:260
  208.4 2.7 multiply_reduce_fusion.12
  211.2 2.3 fusion.48
  217.0 2.5 fusion.128
  219.9 10.1 %attend_forward.5 = (bf16[640,768]{1,0:T(8,128)(2,1)S(1)}, f32[6,8,640]{2,1,0:T(8,128)S(1)}) custom-call(bf16[640,768]{1,0:T(8,128)(2,1)S(1)} %get-tuple-element.374.q_ref, bf16[640,768]{1,0:T(8,128)(2,1)S(1)} %slice.267.k_ref, bf16[640,768]{1,0:T(8,128)(2,1)S(1)} %get-tuple-element.373.v_ref), custom_call_target="tpu_custom_call" | custom-call | flops 1024 | bytes 1024 | tf_op jit(solution)/shard_map/attend_forward/pallas_call | solution.py:238
  231.9 17.5 %ffn_whole.3 = (bf16[640,3072]{1,0:T(8,128)(2,1)S(1)}, bf16[640,3072]{1,0:T(8,128)(2,1)}, bf16[640,768]{1,0:T(8,128)(2,1)S(1)}) custom-call(bf16[640,768]{1,0:T(8,128)(2,1)S(1)} %add_convert_fusion.mixed_ref, bf16[768,3072]{1,0:T(8,128)(2,1)} %copy-done, f32[1,3072]{1,0:T(1,128)S(1)} %bitcast.284, bf16[3072,768]{1,0:T(8,128)(2,1)} %copy-done.1, ...), custom_call_target="tpu_custom_call" | custom-call | flops 1024 | bytes 1024 | tf_op jit(solution)/shard_map/ffn_whole/pallas_call | solution.py:163
  253.2 2.5 copy-done.14
  255.7 10.5 %ffn_back.4 = (bf16[640,3072]{1,0:T(8,128)(2,1)S(1)}, f32[640,768]{1,0:T(8,128)S(1)}, f32[1,3072]{1,0:T(1,128)S(1)}) custom-call(bf16[640,768]{1,0:T(8,128)(2,1)S(1)} %get-tuple-element.364.grad_ref, bf16[3072,768]{1,0:T(8,128)(2,1)} %copy-done.1, bf16[640,3072]{1,0:T(8,128)(2,1)S(1)} %copy-done.14, bf16[768,3072]{1,0:T(8,128)(2,1)} %copy-done), custom_call_target="tpu_custom_call" | custom-call | flops 1024 | bytes 1024 | tf_op jit(solution)/shard_map/ffn_back/pallas_call | solution.py:212
  270.8 17.2 %attend_backward.4 = (bf16[640,768]{1,0:T(8,128)(2,1)S(1)}, bf16[640,768]{1,0:T(8,128)(2,1)S(1)}, bf16[640,768]{1,0:T(8,128)(2,1)S(1)}) custom-call(bf16[640,768]{1,0:T(8,128)(2,1)S(1)} %get-tuple-element.374.q_ref, bf16[640,768]{1,0:T(8,128)(2,1)S(1)} %slice.267.k_ref, bf16[640,768]{1,0:T(8,128)(2,1)S(1)} %get-tuple-element.373.v_ref, ...), custom_call_target="tpu_custom_call" | custom-call | flops 1024 | bytes 1024 | tf_op jit(solution)/shard_map/attend_backward/pallas_call | solution.py:260
  291.1 3.3 fusion.40
  300.3 21.4 %collective-permute-done.15 = bf16[640,768]{1,0:T(8,128)(2,1)} collective-permute-done((bf16[640,768]{1,0:T(8,128)(2,1)}, bf16[640,768]{1,0:T(8,128)(2,1)}, u32[]{:S(2)}, u32[]{:S(2)}) %collective-permute-start.15) | collective-permute-done | bytes 983072 | tf_op jit(solution)/shard_map/ppermute | solution.py:608
  325.2 7.4 %fusion.4 = bf16[3072,768]{1,0:T(8,128)(2,1)S(1)} fusion(bf16[1280,768]{1,0:T(8,128)(2,1)S(1)} %pad_maximum_fusion.5, bf16[640,3072]{1,0:T(8,128)(2,1)S(1)} %copy-done.34, bf16[640,3072]{1,0:T(8,128)(2,1)S(1)} %copy-done.36), kind=kOutput, calls=%fused_computation.6 | convolution fusion | flops 6057885696 | bytes 14548992 | tf_op jit(solution)/shard_map/dot_general | solution.py:25
  340.9 2.1 fusion.15
  343.1 10.9 %ffn_back.5 = (bf16[640,3072]{1,0:T(8,128)(2,1)S(1)}, f32[640,768]{1,0:T(8,128)S(1)}, f32[1,3072]{1,0:T(1,128)S(1)}) custom-call(bf16[640,768]{1,0:T(8,128)(2,1)S(1)} %broadcast_select_fusion.grad_ref, bf16[3072,768]{1,0:T(8,128)(2,1)} %copy-done.1, bf16[640,3072]{1,0:T(8,128)(2,1)S(1)} %copy-done.3, bf16[768,3072]{1,0:T(8,128)(2,1)} %copy-done), custom_call_target="tpu_custom_call" | custom-call | flops 1024 | bytes 1024 | tf_op jit(solution)/shard_map/ffn_back/pallas_call | solution.py:212
  362.4 7.1 %pad_maximum_fusion = bf16[1280,3072]{1,0:T(8,128)(2,1)} fusion(bf16[640,3072]{1,0:T(8,128)(2,1)} %copy-done.22, bf16[640,3072]{1,0:T(8,128)(2,1)} %copy-done.21), kind=kLoop, calls=%fused_computation.4 | loop fusion | flops 15728640 | bytes 15728640 | tf_op jit(solution)/shard_map/concatenate | solution.py:666
  369.5 7.3 %collective-permute-done.17 = bf16[384,768]{1,0:T(8,128)(2,1)} collective-permute-done((bf16[384,768]{1,0:T(8,128)(2,1)}, bf16[384,768]{1,0:T(8,128)(2,1)}, u32[]{:S(2)}, u32[]{:S(2)}) %collective-permute-start.17) | collective-permute-done | bytes 589856 | tf_op jit(solution)/shard_map/ppermute | solution.py:406
  379.9 10.0 %convolution_convert_fusion.1 = bf16[768,3072]{1,0:T(8,128)(2,1)S(1)} fusion(bf16[1280,3072]{1,0:T(8,128)(2,1)} %pad_maximum_fusion, bf16[640,768]{1,0:T(8,128)(2,1)S(1)} %copy-done.16, bf16[640,768]{1,0:T(8,128)(2,1)S(1)} %copy-done.18), kind=kOutput, calls=%fused_computation.8 | convolution fusion | flops 6046089216 | bytes 14548992 | tf_op jit(solution)/shard_map/dot_general | solution.py:25
  394.0 2.6 collective-permute-start.26
  397.5 2.1 convert_reduce_fusion.5
  401.6 2.8 fusion.81
  415.2 6.5 %collective-permute-done.24 = bf16[192,768]{1,0:T(8,128)(2,1)S(1)} collective-permute-done((bf16[192,768]{1,0:T(8,128)(2,1)S(1)}, bf16[192,768]{1,0:T(8,128)(2,1)S(1)}, u32[]{:S(2)}, u32[]{:S(2)}) %collective-permute-start.24) | collective-permute-done | bytes 294944 | tf_op jit(solution)/shard_map/ppermute | solution.py:406
  422.2 17.2 %attend_backward.5 = (bf16[640,768]{1,0:T(8,128)(2,1)S(1)}, bf16[640,768]{1,0:T(8,128)(2,1)S(1)}, bf16[640,768]{1,0:T(8,128)(2,1)S(1)}) custom-call(bf16[640,768]{1,0:T(8,128)(2,1)S(1)} %copy-done.11, bf16[640,768]{1,0:T(8,128)(2,1)S(1)} %copy-done.7, bf16[640,768]{1,0:T(8,128)(2,1)S(1)} %copy-done.9, f32[6,8,640]{2,1,0:T(8,128)S(1)} %get-tuple-element.176.lse_ref, ...), custom_call_target="tpu_custom_call" | custom-call | flops 1024 | bytes 1024 | tf_op jit(solution)/shard_map/attend_backward/pallas_call | solution.py:260
  443.8 2.3 pad_maximum_fusion.1
  451.1 5.3 convolution_convert_fusion
  467.5 2.2 fusion.89
  469.7 4.6 fusion.50
  481.7 2.3 fusion.54
  488.1 5.6 collective-permute-done.38
  493.7 2.6 collective-permute-start.41
  504.4 17.9 %collective-permute-done.34 = bf16[48,3072]{1,0:T(8,128)(2,1)S(1)} collective-permute-done((bf16[48,3072]{1,0:T(8,128)(2,1)S(1)}, bf16[48,3072]{1,0:T(8,128)(2,1)S(1)}, u32[]{:S(2)}, u32[]{:S(2)}) %collective-permute-start.34) | collective-permute-done | bytes 294944 | tf_op jit(solution)/shard_map/ppermute | solution.py:406
  523.3 3.4 collective-permute-start.44
  526.9 2.1 collective-permute-start.48
  529.0 8.1 %collective-permute-done.40 = bf16[48,3072]{1,0:T(8,128)(2,1)S(1)} collective-permute-done((bf16[48,3072]{1,0:T(8,128)(2,1)S(1)}, bf16[48,3072]{1,0:T(8,128)(2,1)S(1)}, u32[]{:S(2)}, u32[]{:S(2)}) %collective-permute-start.40) | collective-permute-done | bytes 294944 | tf_op jit(solution)/shard_map/ppermute | solution.py:406
  537.1 4.7 collective-permute-done.39
  544.1 2.1 collective-permute-start.43
  546.3 10.3 %collective-permute-done.43 = bf16[112,768]{1,0:T(8,128)(2,1)S(1)} collective-permute-done((bf16[112,768]{1,0:T(8,128)(2,1)S(1)}, bf16[112,768]{1,0:T(8,128)(2,1)S(1)}, u32[]{:S(2)}, u32[]{:S(2)}) %collective-permute-start.43) | collective-permute-done | bytes 172064 | tf_op jit(solution)/shard_map/ppermute | solution.py:406
  560.4 2.1 collective-permute-start.50
  562.5 4.2 collective-permute-done.45
  570.2 2.1 collective-permute-done.49
  (501 shorter events, 160.6 us)
Async XLA Ops:
  1.7 8.0 %collective-permute-start.2 = (bf16[1,2304]{1,0:T(2,128)(2,1)S(1)}, bf16[1,2304]{1,0:T(2,128)(2,1)S(1)}, u32[]{:S(2)}, u32[]{:S(2)}) collective-permute-start(bf16[1,2304]{1,0:T(2,128)(2,1)S(1)} %concatenate.85), channel_id=1, source_target_pairs={{0,8},{4,12},{8,0},{12,4},{1,9},{5,13},{9,1},{13,5},{2,10},{6,14},... | collective-permute-start | bytes 13832 | tf_op jit(solution)/shard_map/ppermute | solution.py:406
  6.5 11.8 %collective-permute-start.1 = (bf16[96,2304]{1,0:T(8,128)(2,1)}, bf16[96,2304]{1,0:T(8,128)(2,1)S(1)}, u32[]{:S(2)}, u32[]{:S(2)}) collective-permute-start(bf16[96,2304]{1,0:T(8,128)(2,1)} %dynamic-slice_bitcast_fusion.13), channel_id=1, source_target_pairs={{0,8},{4,12},{8,0},{12,4},{1,9},{5,13},{9,1},{13,5},{2,10},{6,14},... | collective-permute-start | bytes 1327112 | tf_op jit(solution)/shard_map/ppermute | solution.py:406
  8.0 21.1 %copy-start.86 = (bf16[1,192,2304]{2,1,0:T(8,128)(2,1)S(1)}, bf16[1,192,2304]{2,1,0:T(8,128)(2,1)}, u32[]{:S(2)}) copy-start(bf16[1,192,2304]{2,1,0:T(8,128)(2,1)} %param.21) | copy-start | bytes 2654212
  9.8 1.3 collective-permute-start.3
  18.4 10.7 %collective-permute-start.4 = (bf16[96,2304]{1,0:T(8,128)(2,1)S(1)}, bf16[96,2304]{1,0:T(8,128)(2,1)S(1)}, u32[]{:S(2)}, u32[]{:S(2)}) collective-permute-start(bf16[96,2304]{1,0:T(8,128)(2,1)S(1)} %collective-permute-done.1), channel_id=1, source_target_pairs={{0,1},{1,0},{2,3},{3,2},{4,5},{5,4},{6,7},{7,6},{8,9},{9,8},{10,11... | collective-permute-start | bytes 1327112 | tf_op jit(solution)/shard_map/ppermute | solution.py:406
  29.2 3.8 collective-permute-start.5
  30.2 16.0 %collective-permute-start = (bf16[96,3072]{1,0:T(8,128)(2,1)}, bf16[96,3072]{1,0:T(8,128)(2,1)}, u32[]{:S(2)}, u32[]{:S(2)}) collective-permute-start(bf16[96,3072]{1,0:T(8,128)(2,1)} %dynamic-slice_bitcast_fusion.10), channel_id=1, source_target_pairs={{0,8},{4,12},{8,0},{12,4},{1,9},{5,13},{9,1},{13,5},{2,10},{6,14},... | collective-permute-start | bytes 1769480 | tf_op jit(solution)/shard_map/ppermute | solution.py:406
  46.2 15.1 %collective-permute-start.9 = (bf16[96,3072]{1,0:T(8,128)(2,1)}, bf16[96,3072]{1,0:T(8,128)(2,1)S(1)}, u32[]{:S(2)}, u32[]{:S(2)}) collective-permute-start(bf16[96,3072]{1,0:T(8,128)(2,1)} %collective-permute-done), channel_id=1, source_target_pairs={{0,1},{1,0},{2,3},{3,2},{4,5},{5,4},{6,7},{7,6},{8,9},{9,8},{10,11... | collective-permute-start | bytes 1769480 | tf_op jit(solution)/shard_map/ppermute | solution.py:406
  47.8 11.2 %collective-permute-start.6 = (bf16[192,768]{1,0:T(8,128)(2,1)S(1)}, bf16[192,768]{1,0:T(8,128)(2,1)S(1)}, u32[]{:S(2)}, u32[]{:S(2)}) collective-permute-start(bf16[192,768]{1,0:T(8,128)(2,1)S(1)} %bitcast.324), channel_id=1, source_target_pairs={{0,8},{4,12},{8,0},{12,4},{1,9},{5,13},{9,1},{13,5},{2,10},{6,14},... | collective-permute-start | bytes 884744 | tf_op jit(solution)/shard_map/ppermute | solution.py:406
  62.6 12.9 %collective-permute-start.10 = (bf16[384,3072]{1,0:T(8,128)(2,1)S(1)}, bf16[384,3072]{1,0:T(8,128)(2,1)}, u32[]{:S(2)}, u32[]{:S(2)}) collective-permute-start(bf16[384,3072]{1,0:T(8,128)(2,1)S(1)} %pad_maximum_fusion.2.here_ref), channel_id=1, source_target_pairs={{0,4},{4,0},{8,12},{12,8},{1,5},{5,1},{9,13},{13,9},{2,6},{6,2},{1... | collective-permute-start | bytes 7077896 | tf_op jit(solution)/shard_map/ppermute | solution.py:406
  62.7 6.6 %collective-permute-start.7 = (bf16[384,768]{1,0:T(8,128)(2,1)S(1)}, bf16[384,768]{1,0:T(8,128)(2,1)S(1)}, u32[]{:S(2)}, u32[]{:S(2)}) collective-permute-start(bf16[384,768]{1,0:T(8,128)(2,1)S(1)} %pad_maximum_fusion.7.here_ref), channel_id=1, source_target_pairs={{0,4},{4,0},{8,12},{12,8},{1,5},{5,1},{9,13},{13,9},{2,6},{6,2},{1... | collective-permute-start | bytes 1769480 | tf_op jit(solution)/shard_map/ppermute | solution.py:406
  63.3 28.3 %collective-permute-start.8 = (bf16[768,768]{1,0:T(8,128)(2,1)}, bf16[768,768]{1,0:T(8,128)(2,1)}, u32[]{:S(2)}, u32[]{:S(2)}) collective-permute-start(bf16[768,768]{1,0:T(8,128)(2,1)} %bitcast.25), channel_id=1, source_target_pairs={{0,8},{4,12},{8,0},{12,4},{1,9},{5,13},{9,1},{13,5},{2,10},{6,14},... | collective-permute-start | bytes 3538952 | tf_op jit(solution)/shard_map/ppermute | solution.py:406
  93.4 4.7 collective-permute-start.11
  105.0 25.0 %collective-permute-start.12 = (bf16[640,768]{1,0:T(8,128)(2,1)}, bf16[640,768]{1,0:T(8,128)(2,1)S(1)}, u32[]{:S(2)}, u32[]{:S(2)}) collective-permute-start(bf16[640,768]{1,0:T(8,128)(2,1)} %add_convert_fusion.2), channel_id=1, source_target_pairs={{0,16},{1,17},{2,18},{3,19},{4,20},{5,21},{6,22},{7,23},{8,24},{9,... | collective-permute-start | bytes 2949128 | tf_op jit(solution)/shard_map/ppermute | solution.py:605
  108.6 21.3 %copy-start.56 = (bf16[2,1,640,768]{3,2,1,0:T(8,128)(2,1)S(1)}, bf16[2,1,640,768]{3,2,1,0:T(8,128)(2,1)}, u32[]{:S(2)}) copy-start(bf16[2,1,640,768]{3,2,1,0:T(8,128)(2,1)} %param.16) | copy-start | bytes 5898244
  111.9 18.9 %copy-start.97 = (f32[768]{0:T(1024)S(1)}, f32[768]{0:T(1024)}, u32[]{:S(2)}) copy-start(f32[768]{0:T(1024)} %copy-done.96) | copy-start | bytes 9220
  111.9 18.9 %copy-start.104 = (f32[768]{0:T(1024)S(1)}, f32[768]{0:T(1024)}, u32[]{:S(2)}) copy-start(f32[768]{0:T(1024)} %copy-done.103) | copy-start | bytes 9220
  130.4 80.8 %copy-start.98 = (f32[640]{0:T(1024)}, f32[640]{0:T(1024)S(1)}, u32[]{:S(2)}) copy-start(f32[640]{0:T(1024)S(1)} %broadcast_multiply_fusion.15) | copy-start | bytes 7684
  130.8 80.3 %copy-start.101 = (f32[640]{0:T(1024)}, f32[640]{0:T(1024)S(1)}, u32[]{:S(2)}) copy-start(f32[640]{0:T(1024)S(1)} %add_rsqrt_fusion.3) | copy-start | bytes 7684
  135.5 55.6 %copy-start.6 = (bf16[640,768]{1,0:T(8,128)(2,1)}, bf16[640,768]{1,0:T(8,128)(2,1)S(1)}, u32[]{:S(2)}) copy-start(bf16[640,768]{1,0:T(8,128)(2,1)S(1)} %slice.268.k_ref) | copy-start | bytes 2949124
  135.9 55.2 %copy-start.8 = (bf16[640,768]{1,0:T(8,128)(2,1)}, bf16[640,768]{1,0:T(8,128)(2,1)S(1)}, u32[]{:S(2)}) copy-start(bf16[640,768]{1,0:T(8,128)(2,1)S(1)} %get-tuple-element.375.v_ref) | copy-start | bytes 2949124
  135.9 55.2 %copy-start.10 = (bf16[640,768]{1,0:T(8,128)(2,1)}, bf16[640,768]{1,0:T(8,128)(2,1)S(1)}, u32[]{:S(2)}) copy-start(bf16[640,768]{1,0:T(8,128)(2,1)S(1)} %get-tuple-element.376.q_ref) | copy-start | bytes 2949124
  168.5 46.3 %collective-permute-start.13 = (bf16[640,768]{1,0:T(8,128)(2,1)}, bf16[640,768]{1,0:T(8,128)(2,1)}, u32[]{:S(2)}, u32[]{:S(2)}) collective-permute-start(bf16[640,768]{1,0:T(8,128)(2,1)} %get-tuple-element.173), channel_id=1, source_target_pairs={{0,16},{1,17},{2,18},{3,19},{4,20},{5,21},{6,22},{7,23},{8,24},{9,... | collective-permute-start | bytes 2949128 | tf_op jit(solution)/shard_map/ppermute | solution.py:605
  213.5 37.8 %collective-permute-start.14 = (bf16[640,768]{1,0:T(8,128)(2,1)}, bf16[640,768]{1,0:T(8,128)(2,1)}, u32[]{:S(2)}, u32[]{:S(2)}) collective-permute-start(bf16[640,768]{1,0:T(8,128)(2,1)} %fusion.48), channel_id=1, source_target_pairs={{16,0},{17,1},{18,2},{19,3},{20,4},{21,5},{22,6},{23,7},{24,8},{25... | collective-permute-start | bytes 2949128 | tf_op jit(solution)/shard_map/ppermute | solution.py:608
  231.9 19.4 %copy-start.53 = (bf16[2,640,768]{2,1,0:T(8,128)(2,1)S(1)}, bf16[2,640,768]{2,1,0:T(8,128)(2,1)}, u32[]{:S(2)}) copy-start(bf16[2,640,768]{2,1,0:T(8,128)(2,1)} %bitcast_multiply_fusion) | copy-start | bytes 5898244
  296.0 25.7 %collective-permute-start.15 = (bf16[640,768]{1,0:T(8,128)(2,1)}, bf16[640,768]{1,0:T(8,128)(2,1)}, u32[]{:S(2)}, u32[]{:S(2)}) collective-permute-start(bf16[640,768]{1,0:T(8,128)(2,1)} %fusion.39), channel_id=1, source_target_pairs={{16,0},{17,1},{18,2},{19,3},{20,4},{21,5},{22,6},{23,7},{24,8},{25... | collective-permute-start | bytes 2949128 | tf_op jit(solution)/shard_map/ppermute | solution.py:608
  297.4 24.4 %copy-start.54 = (bf16[2,640,768]{2,1,0:T(8,128)(2,1)S(1)}, bf16[2,640,768]{2,1,0:T(8,128)(2,1)}, u32[]{:S(2)}) copy-start(bf16[2,640,768]{2,1,0:T(8,128)(2,1)} %bitcast_multiply_fusion) | copy-start | bytes 5898244
  298.8 24.4 %copy-start.36 = (bf16[640,3072]{1,0:T(8,128)(2,1)S(1)}, bf16[640,3072]{1,0:T(8,128)(2,1)}, u32[]{:S(2)}) copy-start(bf16[640,3072]{1,0:T(8,128)(2,1)} %copy-done.35) | copy-start | bytes 11796484
  300.3 22.8 %copy-start.5 = (bf16[640,768]{1,0:T(8,128)(2,1)S(1)}, bf16[640,768]{1,0:T(8,128)(2,1)}, u32[]{:S(2)}) copy-start(bf16[640,768]{1,0:T(8,128)(2,1)} %copy-done.4) | copy-start | bytes 2949124
  334.1 4.5 collective-permute-start.16
  335.7 4.9 collective-permute-start.18
  360.4 16.4 %collective-permute-start.17 = (bf16[384,768]{1,0:T(8,128)(2,1)}, bf16[384,768]{1,0:T(8,128)(2,1)}, u32[]{:S(2)}, u32[]{:S(2)}) collective-permute-start(bf16[384,768]{1,0:T(8,128)(2,1)} %dynamic-slice_bitcast_fusion.9), channel_id=1, source_target_pairs={{0,8},{4,12},{8,0},{12,4},{1,9},{5,13},{9,1},{13,5},{2,10},{6,14},... | collective-permute-start | bytes 1769480 | tf_op jit(solution)/shard_map/ppermute | solution.py:406
  360.9 49.8 %collective-permute-start.23 = (bf16[384,768]{1,0:T(8,128)(2,1)}, bf16[384,768]{1,0:T(8,128)(2,1)}, u32[]{:S(2)}, u32[]{:S(2)}) collective-permute-start(bf16[384,768]{1,0:T(8,128)(2,1)} %dynamic-slice_bitcast_fusion.7), channel_id=1, source_target_pairs={{0,8},{4,12},{8,0},{12,4},{1,9},{5,13},{9,1},{13,5},{2,10},{6,14},... | collective-permute-start | bytes 1769480 | tf_op jit(solution)/shard_map/ppermute | solution.py:406
  378.3 14.9 %collective-permute-start.19 = (bf16[192,768]{1,0:T(8,128)(2,1)S(1)}, bf16[192,768]{1,0:T(8,128)(2,1)S(1)}, u32[]{:S(2)}, u32[]{:S(2)}) collective-permute-start(bf16[192,768]{1,0:T(8,128)(2,1)S(1)} %dynamic-slice_bitcast_fusion.18), channel_id=1, source_target_pairs={{0,1},{1,0},{2,3},{3,2},{4,5},{5,4},{6,7},{7,6},{8,9},{9,8},{10,11... | collective-permute-start | bytes 884744 | tf_op jit(solution)/shard_map/ppermute | solution.py:406
  391.6 14.8 %collective-permute-start.21 = (bf16[2,96,3072]{2,1,0:T(8,128)(2,1)}, bf16[2,96,3072]{2,1,0:T(8,128)(2,1)}, u32[]{:S(2)}, u32[]{:S(2)}) collective-permute-start(bf16[2,96,3072]{2,1,0:T(8,128)(2,1)} %dynamic-slice_bitcast_fusion), channel_id=1, source_target_pairs={{0,4},{4,0},{8,12},{12,8},{1,5},{5,1},{9,13},{13,9},{2,6},{6,2},{1... | collective-permute-start | bytes 3538952 | tf_op jit(solution)/shard_map/ppermute | solution.py:406
  393.2 15.6 %collective-permute-start.20 = (bf16[2,96,3072]{2,1,0:T(8,128)(2,1)}, bf16[2,96,3072]{2,1,0:T(8,128)(2,1)}, u32[]{:S(2)}, u32[]{:S(2)}) collective-permute-start(bf16[2,96,3072]{2,1,0:T(8,128)(2,1)} %dynamic-slice_bitcast_fusion.1), channel_id=1, source_target_pairs={{0,4},{4,0},{8,12},{12,8},{1,5},{5,1},{9,13},{13,9},{2,6},{6,2},{1... | collective-permute-start | bytes 3538952 | tf_op jit(solution)/shard_map/ppermute | solution.py:406
  394.0 53.5 %collective-permute-start.26 = (bf16[192,768]{1,0:T(8,128)(2,1)}, bf16[192,768]{1,0:T(8,128)(2,1)}, u32[]{:S(2)}, u32[]{:S(2)}) collective-permute-start(bf16[192,768]{1,0:T(8,128)(2,1)} %fusion.106), channel_id=1, source_target_pairs={{0,2},{1,3},{2,0},{3,1},{4,6},{5,7},{6,4},{7,5},{8,10},{9,11},{10,... | collective-permute-start | bytes 884744 | tf_op jit(solution)/shard_map/ppermute | solution.py:406
  408.3 37.9 %collective-permute-start.27 = (bf16[96,3072]{1,0:T(8,128)(2,1)S(1)}, bf16[96,3072]{1,0:T(8,128)(2,1)}, u32[]{:S(2)}, u32[]{:S(2)}) collective-permute-start(bf16[96,3072]{1,0:T(8,128)(2,1)S(1)} %dynamic-slice_bitcast_fusion.6), channel_id=1, source_target_pairs={{0,8},{4,12},{8,0},{12,4},{1,9},{5,13},{9,1},{13,5},{2,10},{6,14},... | collective-permute-start | bytes 1769480 | tf_op jit(solution)/shard_map/ppermute | solution.py:406
  412.4 9.2 %collective-permute-start.24 = (bf16[192,768]{1,0:T(8,128)(2,1)S(1)}, bf16[192,768]{1,0:T(8,128)(2,1)S(1)}, u32[]{:S(2)}, u32[]{:S(2)}) collective-permute-start(bf16[192,768]{1,0:T(8,128)(2,1)S(1)} %dynamic-slice_bitcast_fusion.17), channel_id=1, source_target_pairs={{0,1},{1,0},{2,3},{3,2},{4,5},{5,4},{6,7},{7,6},{8,9},{9,8},{10,11... | collective-permute-start | bytes 884744 | tf_op jit(solution)/shard_map/ppermute | solution.py:406
  413.8 53.7 %collective-permute-start.22 = (bf16[96,3072]{1,0:T(8,128)(2,1)}, bf16[96,3072]{1,0:T(8,128)(2,1)}, u32[]{:S(2)}, u32[]{:S(2)}) collective-permute-start(bf16[96,3072]{1,0:T(8,128)(2,1)} %dynamic-slice_bitcast_fusion.8), channel_id=1, source_target_pairs={{0,8},{4,12},{8,0},{12,4},{1,9},{5,13},{9,1},{13,5},{2,10},{6,14},... | collective-permute-start | bytes 1769480 | tf_op jit(solution)/shard_map/ppermute | solution.py:406
  421.7 27.6 %collective-permute-start.25 = (bf16[192,768]{1,0:T(8,128)(2,1)S(1)}, bf16[192,768]{1,0:T(8,128)(2,1)}, u32[]{:S(2)}, u32[]{:S(2)}) collective-permute-start(bf16[192,768]{1,0:T(8,128)(2,1)S(1)} %fusion.105), channel_id=1, source_target_pairs={{0,2},{1,3},{2,0},{3,1},{4,6},{5,7},{6,4},{7,5},{8,10},{9,11},{10,... | collective-permute-start | bytes 884744 | tf_op jit(solution)/shard_map/ppermute | solution.py:406
  458.8 3.9 collective-permute-start.29
  459.4 37.3 %collective-permute-start.36 = (bf16[192,768]{1,0:T(8,128)(2,1)}, bf16[192,768]{1,0:T(8,128)(2,1)}, u32[]{:S(2)}, u32[]{:S(2)}) collective-permute-start(bf16[192,768]{1,0:T(8,128)(2,1)} %add_convert_fusion.6), channel_id=1, source_target_pairs={{0,1},{1,0},{2,3},{3,2},{4,5},{5,4},{6,7},{7,6},{8,9},{9,8},{10,11... | collective-permute-start | bytes 884744 | tf_op jit(solution)/shard_map/ppermute | solution.py:406
  459.9 36.5 %collective-permute-start.37 = (bf16[192,768]{1,0:T(8,128)(2,1)}, bf16[192,768]{1,0:T(8,128)(2,1)}, u32[]{:S(2)}, u32[]{:S(2)}) collective-permute-start(bf16[192,768]{1,0:T(8,128)(2,1)} %add_convert_fusion.7), channel_id=1, source_target_pairs={{0,1},{1,0},{2,3},{3,2},{4,5},{5,4},{6,7},{7,6},{8,9},{9,8},{10,11... | collective-permute-start | bytes 884744 | tf_op jit(solution)/shard_map/ppermute | solution.py:406
  462.2 23.8 %collective-permute-start.33 = (bf16[48,3072]{1,0:T(8,128)(2,1)}, bf16[48,3072]{1,0:T(8,128)(2,1)}, u32[]{:S(2)}, u32[]{:S(2)}) collective-permute-start(bf16[48,3072]{1,0:T(8,128)(2,1)} %dynamic-slice_bitcast_fusion.16), channel_id=1, source_target_pairs={{0,1},{1,0},{2,3},{3,2},{4,5},{5,4},{6,7},{7,6},{8,9},{9,8},{10,11... | collective-permute-start | bytes 884744 | tf_op jit(solution)/shard_map/ppermute | solution.py:406
  462.7 2.5 collective-permute-start.28
  465.2 31.5 %collective-permute-start.35 = (bf16[96,2304]{1,0:T(8,128)(2,1)}, bf16[96,2304]{1,0:T(8,128)(2,1)}, u32[]{:S(2)}, u32[]{:S(2)}) collective-permute-start(bf16[96,2304]{1,0:T(8,128)(2,1)} %dynamic-slice_bitcast_fusion.11), channel_id=1, source_target_pairs={{0,8},{4,12},{8,0},{12,4},{1,9},{5,13},{9,1},{13,5},{2,10},{6,14},... | collective-permute-start | bytes 1327112 | tf_op jit(solution)/shard_map/ppermute | solution.py:406
  481.6 2.6 collective-permute-start.30
  484.2 9.4 %collective-permute-start.38 = (bf16[48,3072]{1,0:T(8,128)(2,1)S(1)}, bf16[48,3072]{1,0:T(8,128)(2,1)S(1)}, u32[]{:S(2)}, u32[]{:S(2)}) collective-permute-start(bf16[48,3072]{1,0:T(8,128)(2,1)S(1)} %dynamic-slice_bitcast_fusion.15), channel_id=1, source_target_pairs={{0,1},{1,0},{2,3},{3,2},{4,5},{5,4},{6,7},{7,6},{8,9},{9,8},{10,11... | collective-permute-start | bytes 884744 | tf_op jit(solution)/shard_map/ppermute | solution.py:406
  486.0 37.0 %collective-permute-start.32 = (bf16[96,2304]{1,0:T(8,128)(2,1)S(1)}, bf16[96,2304]{1,0:T(8,128)(2,1)S(1)}, u32[]{:S(2)}, u32[]{:S(2)}) collective-permute-start(bf16[96,2304]{1,0:T(8,128)(2,1)S(1)} %dynamic-slice_bitcast_fusion.12), channel_id=1, source_target_pairs={{0,8},{4,12},{8,0},{12,4},{1,9},{5,13},{9,1},{13,5},{2,10},{6,14},... | collective-permute-start | bytes 1327112 | tf_op jit(solution)/shard_map/ppermute | solution.py:406
  493.7 33.0 %collective-permute-start.41 = (bf16[48,3072]{1,0:T(8,128)(2,1)S(1)}, bf16[48,3072]{1,0:T(8,128)(2,1)S(1)}, u32[]{:S(2)}, u32[]{:S(2)}) collective-permute-start(bf16[48,3072]{1,0:T(8,128)(2,1)S(1)} %fusion.103), channel_id=1, source_target_pairs={{0,2},{1,3},{2,0},{3,1},{4,6},{5,7},{6,4},{7,5},{8,10},{9,11},{10,... | collective-permute-start | bytes 884744 | tf_op jit(solution)/shard_map/ppermute | solution.py:406
  496.4 25.9 %collective-permute-start.34 = (bf16[48,3072]{1,0:T(8,128)(2,1)S(1)}, bf16[48,3072]{1,0:T(8,128)(2,1)S(1)}, u32[]{:S(2)}, u32[]{:S(2)}) collective-permute-start(bf16[48,3072]{1,0:T(8,128)(2,1)S(1)} %fusion.104), channel_id=1, source_target_pairs={{0,2},{1,3},{2,0},{3,1},{4,6},{5,7},{6,4},{7,5},{8,10},{9,11},{10,... | collective-permute-start | bytes 884744 | tf_op jit(solution)/shard_map/ppermute | solution.py:406
  497.9 25.3 %collective-permute-start.42 = (bf16[48,2304]{1,0:T(8,128)(2,1)S(1)}, bf16[48,2304]{1,0:T(8,128)(2,1)S(1)}, u32[]{:S(2)}, u32[]{:S(2)}) collective-permute-start(bf16[48,2304]{1,0:T(8,128)(2,1)S(1)} %dynamic-slice_bitcast_fusion.19), channel_id=1, source_target_pairs={{0,1},{1,0},{2,3},{3,2},{4,5},{5,4},{6,7},{7,6},{8,9},{9,8},{10,11... | collective-permute-start | bytes 663560 | tf_op jit(solution)/shard_map/ppermute | solution.py:406
  501.8 42.1 %collective-permute-start.31 = (bf16[224,768]{1,0:T(8,128)(2,1)S(1)}, bf16[224,768]{1,0:T(8,128)(2,1)S(1)}, u32[]{:S(2)}, u32[]{:S(2)}) collective-permute-start(bf16[224,768]{1,0:T(8,128)(2,1)S(1)} %dynamic-slice_bitcast_fusion.14), channel_id=1, source_target_pairs={{0,8},{4,12},{8,0},{12,4},{1,9},{5,13},{9,1},{13,5},{2,10},{6,14},... | collective-permute-start | bytes 1032200 | tf_op jit(solution)/shard_map/ppermute | solution.py:406
  522.3 14.7 %collective-permute-start.40 = (bf16[48,3072]{1,0:T(8,128)(2,1)S(1)}, bf16[48,3072]{1,0:T(8,128)(2,1)S(1)}, u32[]{:S(2)}, u32[]{:S(2)}) collective-permute-start(bf16[48,3072]{1,0:T(8,128)(2,1)S(1)} %add_convert_fusion.5), channel_id=1, source_target_pairs={{0,1},{1,0},{2,3},{3,2},{4,5},{5,4},{6,7},{7,6},{8,9},{9,8},{10,11... | collective-permute-start | bytes 884744 | tf_op jit(solution)/shard_map/ppermute | solution.py:406
  523.3 20.8 %collective-permute-start.44 = (bf16[48,2304]{1,0:T(8,128)(2,1)S(1)}, bf16[48,2304]{1,0:T(8,128)(2,1)S(1)}, u32[]{:S(2)}, u32[]{:S(2)}) collective-permute-start(bf16[48,2304]{1,0:T(8,128)(2,1)S(1)} %fusion.108), channel_id=1, source_target_pairs={{0,2},{1,3},{2,0},{3,1},{4,6},{5,7},{6,4},{7,5},{8,10},{9,11},{10,... | collective-permute-start | bytes 663560 | tf_op jit(solution)/shard_map/ppermute | solution.py:406
  526.7 15.1 %collective-permute-start.39 = (bf16[48,2304]{1,0:T(8,128)(2,1)S(1)}, bf16[48,2304]{1,0:T(8,128)(2,1)S(1)}, u32[]{:S(2)}, u32[]{:S(2)}) collective-permute-start(bf16[48,2304]{1,0:T(8,128)(2,1)S(1)} %dynamic-slice_bitcast_fusion.20), channel_id=1, source_target_pairs={{0,1},{1,0},{2,3},{3,2},{4,5},{5,4},{6,7},{7,6},{8,9},{9,8},{10,11... | collective-permute-start | bytes 663560 | tf_op jit(solution)/shard_map/ppermute | solution.py:406
  526.9 31.7 %collective-permute-start.48 = (bf16[48,3072]{1,0:T(8,128)(2,1)S(1)}, bf16[48,3072]{1,0:T(8,128)(2,1)S(1)}, u32[]{:S(2)}, u32[]{:S(2)}) collective-permute-start(bf16[48,3072]{1,0:T(8,128)(2,1)S(1)} %add_convert_fusion.4), channel_id=1, source_target_pairs={{0,1},{1,0},{2,3},{3,2},{4,5},{5,4},{6,7},{7,6},{8,9},{9,8},{10,11... | collective-permute-start | bytes 884744 | tf_op jit(solution)/shard_map/ppermute | solution.py:406
  541.9 18.4 %collective-permute-start.47 = (bf16[48,2304]{1,0:T(8,128)(2,1)S(1)}, bf16[48,2304]{1,0:T(8,128)(2,1)S(1)}, u32[]{:S(2)}, u32[]{:S(2)}) collective-permute-start(bf16[48,2304]{1,0:T(8,128)(2,1)S(1)} %fusion.107), channel_id=1, source_target_pairs={{0,2},{1,3},{2,0},{3,1},{4,6},{5,7},{6,4},{7,5},{8,10},{9,11},{10,... | collective-permute-start | bytes 663560 | tf_op jit(solution)/shard_map/ppermute | solution.py:406
  544.1 12.5 %collective-permute-start.43 = (bf16[112,768]{1,0:T(8,128)(2,1)S(1)}, bf16[112,768]{1,0:T(8,128)(2,1)S(1)}, u32[]{:S(2)}, u32[]{:S(2)}) collective-permute-start(bf16[112,768]{1,0:T(8,128)(2,1)S(1)} %dynamic-slice_bitcast_fusion.21), channel_id=1, source_target_pairs={{0,1},{1,0},{2,3},{3,2},{4,5},{5,4},{6,7},{7,6},{8,9},{9,8},{10,11... | collective-permute-start | bytes 516104 | tf_op jit(solution)/shard_map/ppermute | solution.py:406
  546.2 16.3 %collective-permute-start.46 = (bf16[48,2304]{1,0:T(8,128)(2,1)S(1)}, bf16[48,2304]{1,0:T(8,128)(2,1)S(1)}, u32[]{:S(2)}, u32[]{:S(2)}) collective-permute-start(bf16[48,2304]{1,0:T(8,128)(2,1)S(1)} %add_convert_fusion.9), channel_id=1, source_target_pairs={{0,1},{1,0},{2,3},{3,2},{4,5},{5,4},{6,7},{7,6},{8,9},{9,8},{10,11... | collective-permute-start | bytes 663560 | tf_op jit(solution)/shard_map/ppermute | solution.py:406
  556.6 10.2 %collective-permute-start.45 = (bf16[112,768]{1,0:T(8,128)(2,1)S(1)}, bf16[112,768]{1,0:T(8,128)(2,1)S(1)}, u32[]{:S(2)}, u32[]{:S(2)}) collective-permute-start(bf16[112,768]{1,0:T(8,128)(2,1)S(1)} %fusion.109), channel_id=1, source_target_pairs={{0,2},{1,3},{2,0},{3,1},{4,6},{5,7},{6,4},{7,5},{8,10},{9,11},{10,... | collective-permute-start | bytes 516104 | tf_op jit(solution)/shard_map/ppermute | solution.py:406
  560.4 8.4 %collective-permute-start.50 = (bf16[48,2304]{1,0:T(8,128)(2,1)S(1)}, bf16[48,2304]{1,0:T(8,128)(2,1)S(1)}, u32[]{:S(2)}, u32[]{:S(2)}) collective-permute-start(bf16[48,2304]{1,0:T(8,128)(2,1)S(1)} %add_convert_fusion.8), channel_id=1, source_target_pairs={{0,1},{1,0},{2,3},{3,2},{4,5},{5,4},{6,7},{7,6},{8,9},{9,8},{10,11... | collective-permute-start | bytes 663560 | tf_op jit(solution)/shard_map/ppermute | solution.py:406
  566.8 5.5 collective-permute-start.49
  (103 other events, 577.2 us)

commit v3 on v2

--- a/solution.py
+++ b/solution.py
@@ -699,7 +699,7 @@
     chains["output", 0] = ReduceChain(jnp.concatenate([last, extra], 1))
     grad_c = advance(
         grad_c,
-        (o0, e0, e1, c0, c1, p0, e0, p1, p0, e1, e0, p1, o0, p0, o0, e1, p1, p0, o0, p1, o0),
+        (e0, p0, e1, c0, c1, p1, o0, e0, p0, e1, p1, e0, p0, o0, e1, p1, p0, o0, p1, o0, o0),
     )
     section_input_grads = jnp.stack([jnp.where(first, grad_b, grad_c), jnp.where(first, grad_c, grad_b)])
     owned = {

time: 582 us -> 583 us (level)
  waiting for transfers between devices: 144 us -> 155 us
  starting transfers between devices: 56.6 us -> 48.2 us
    ppermute x47, waiting for transfers between devices: 105 us -> 115 us  [swap(): return lax.ppermute(block, axis, partner(axis, bit))]
    ppermute x47, starting transfers between devices: 44.8 us -> 36.4 us  [swap(): return lax.ppermute(block, axis, partner(axis, bit))]
  transfers between devices with their start and end apart: 51 -> 51, of which waited for: 21 -> 23; matrix products, arithmetic and copies ran while one was open for 23% -> 23% of each run, Pallas kernels for 17% -> 17%
where the time goes in v3:
time: 583 us; the launch traced here: 579 us
  Pallas kernels  170 us (29%)
  waiting for transfers between devices  155 us (27%)
  other arithmetic  85.4 us (15%)
  local copies, waits for them, and re-layouts  59.3 us (10%)
  matrix products  58.5 us (10%)
  starting transfers between devices  48.2 us (8%)
    ppermute x47, waiting for transfers between devices, swap(): return lax.ppermute(block, axis, partner(axis, bit))  115 us
    pallas_call x3, Pallas kernels, attend_backward(): pl.pallas_call(attend_back_kernel, grid=(clips, high - low), in_specs=[bl...  51.8 us
    ppermute x47, starting transfers between devices, swap(): return lax.ppermute(block, axis, partner(axis, bit))  36.4 us
    pallas_call x2, Pallas kernels, ffn_whole(): pl.pallas_call(ffn_whole_kernel, grid=(hidden_units // step,), in_specs=[...  35.1 us
    pallas_call x3, Pallas kernels, ffn_back(): pl.pallas_call(ffn_back_kernel, grid=(hidden_units // step,), in_specs=[w...  32.4 us
    pallas_call x3, Pallas kernels, attend_forward(): pl.pallas_call(attend_kernel, grid=(clips, pairs), in_specs=[block] * 3,...  30.7 us
    unnamed x238, local copies, waits for them, and re-layouts  28 us
    dot_general x4, matrix products, matmul_left(): lax.dot_general(left, right, (((0,), (0,)), ((), ())), preferred_element_...  25.4 us
  transfers between devices with their start and end apart: 51, of which 23 were waited for; matrix products, arithmetic and copies ran while one was open for 23% of the time, Pallas kernels for 17%

profile of v3, /device:TPU:0, one launch (start us, length us, event | category | flops | bytes accessed | tf_op | source)
XLA Modules:
  0.0 578.5 jit_solution(7999525264092440302)
XLA Ops:
  1.7 3.0 collective-permute-start.2
  13.5 4.9 collective-permute-done.1
  20.0 9.1 %collective-permute-done.4 = bf16[96,2304]{1,0:T(8,128)(2,1)S(1)} collective-permute-done((bf16[96,2304]{1,0:T(8,128)(2,1)S(1)}, bf16[96,2304]{1,0:T(8,128)(2,1)S(1)}, u32[]{:S(2)}, u32[]{:S(2)}) %collective-permute-start.4) | collective-permute-done | bytes 442400 | tf_op jit(solution)/shard_map/ppermute | solution.py:406
  33.0 2.5 shards_in_order.4
  35.5 2.5 fusion.126
  38.4 7.8 %collective-permute-done = bf16[96,3072]{1,0:T(8,128)(2,1)} collective-permute-done((bf16[96,3072]{1,0:T(8,128)(2,1)}, bf16[96,3072]{1,0:T(8,128)(2,1)}, u32[]{:S(2)}, u32[]{:S(2)}) %collective-permute-start) | collective-permute-done | bytes 589856 | tf_op jit(solution)/shard_map/ppermute | solution.py:406
  48.4 10.6 %attend_forward.3 = (bf16[640,768]{1,0:T(8,128)(2,1)S(1)}, f32[6,8,640]{2,1,0:T(8,128)}) custom-call(bf16[640,768]{1,0:T(8,128)(2,1)S(1)} %get-tuple-element.163.q_ref, bf16[640,768]{1,0:T(8,128)(2,1)S(1)} %slice.269.k_ref, bf16[640,768]{1,0:T(8,128)(2,1)S(1)} %get-tuple-element.377.v_ref), custom_call_target="tpu_custom_call" | custom-call | flops 1024 | bytes 1024 | tf_op jit(solution)/shard_map/attend_forward/pallas_call | solution.py:238
  59.0 2.3 collective-permute-done.9
  71.6 2.7 fusion.123
  75.5 2.7 shards_in_order.6.expand_ref
  78.2 10.3 %ffn_up.1 = (bf16[640,3072]{1,0:T(8,128)(2,1)S(1)}, bf16[640,3072]{1,0:T(8,128)(2,1)}) custom-call(bf16[640,768]{1,0:T(8,128)(2,1)S(1)} %add_convert_fusion.3.mixed_ref, bf16[768,3072]{1,0:T(8,128)(2,1)S(1)} %shards_in_order.6.expand_ref, f32[1,3072]{1,0:T(1,128)S(1)} %bitcast.282), custom_call_target="tpu_custom_call" | custom-call | flops 1024 | bytes 1024 | tf_op jit(solution)/shard_map/ffn_up/pallas_call | solution.py:115
  88.5 3.0 collective-permute-done.8
  93.6 4.5 collective-permute-done.11.there_ref
  98.1 2.7 shards_in_order.7.contract_ref
  100.8 4.2 add_convert_fusion.2
  105.0 3.6 collective-permute-start.12
  108.6 3.2 bitcast_multiply_fusion
  111.9 18.1 %collective-permute-done.12 = bf16[640,768]{1,0:T(8,128)(2,1)S(1)} collective-permute-done((bf16[640,768]{1,0:T(8,128)(2,1)}, bf16[640,768]{1,0:T(8,128)(2,1)S(1)}, u32[]{:S(2)}, u32[]{:S(2)}) %collective-permute-start.12) | collective-permute-done | bytes 983072 | tf_op jit(solution)/shard_map/ppermute | solution.py:605
  132.3 2.5 fusion.127
  135.9 10.0 %attend_forward.4 = (bf16[640,768]{1,0:T(8,128)(2,1)S(1)}, f32[6,8,640]{2,1,0:T(8,128)S(1)}) custom-call(bf16[640,768]{1,0:T(8,128)(2,1)S(1)} %get-tuple-element.376.q_ref, bf16[640,768]{1,0:T(8,128)(2,1)S(1)} %slice.268.k_ref, bf16[640,768]{1,0:T(8,128)(2,1)S(1)} %get-tuple-element.375.v_ref), custom_call_target="tpu_custom_call" | custom-call | flops 1024 | bytes 1024 | tf_op jit(solution)/shard_map/attend_forward/pallas_call | solution.py:238
  149.0 17.6 %ffn_whole.2 = (bf16[640,3072]{1,0:T(8,128)(2,1)S(1)}, bf16[640,3072]{1,0:T(8,128)(2,1)}, bf16[640,768]{1,0:T(8,128)(2,1)}) custom-call(bf16[640,768]{1,0:T(8,128)(2,1)S(1)} %add_convert_fusion.1.mixed_ref, bf16[768,3072]{1,0:T(8,128)(2,1)} %copy-done, f32[1,3072]{1,0:T(1,128)S(1)} %bitcast.283, bf16[3072,768]{1,0:T(8,128)(2,1)} %copy-done.1, ...), custom_call_target="tpu_custom_call" | custom-call | flops 1024 | bytes 1024 | tf_op jit(solution)/shard_map/ffn_whole/pallas_call | solution.py:163
  168.5 5.6 collective-permute-start.13
  174.1 2.1 copy-done.2
  176.2 11.0 %ffn_back.3 = (bf16[640,3072]{1,0:T(8,128)(2,1)}, f32[640,768]{1,0:T(8,128)S(1)}, f32[1,3072]{1,0:T(1,128)}) custom-call(bf16[640,768]{1,0:T(8,128)(2,1)S(1)} %slice_bitcast_fusion.1.grad_ref, bf16[3072,768]{1,0:T(8,128)(2,1)} %copy-done.1, bf16[640,3072]{1,0:T(8,128)(2,1)S(1)} %copy-done.2, bf16[768,3072]{1,0:T(8,128)(2,1)} %copy-done), custom_call_target="tpu_custom_call" | custom-call | flops 1024 | bytes 1024 | tf_op jit(solution)/shard_map/ffn_back/pallas_call | solution.py:212
  188.7 2.3 convolution_convert_fusion.4.g_ref
  191.1 17.3 %attend_backward.3 = (bf16[640,768]{1,0:T(8,128)(2,1)S(1)}, bf16[640,768]{1,0:T(8,128)(2,1)S(1)}, bf16[640,768]{1,0:T(8,128)(2,1)S(1)}) custom-call(bf16[640,768]{1,0:T(8,128)(2,1)S(1)} %get-tuple-element.376.q_ref, bf16[640,768]{1,0:T(8,128)(2,1)S(1)} %slice.268.k_ref, bf16[640,768]{1,0:T(8,128)(2,1)S(1)} %get-tuple-element.375.v_ref, ...), custom_call_target="tpu_custom_call" | custom-call | flops 1024 | bytes 1024 | tf_op jit(solution)/shard_map/attend_backward/pallas_call | solution.py:260
  208.4 2.7 multiply_reduce_fusion.12
  211.2 2.3 fusion.48
  217.0 2.5 fusion.128
  219.9 10.1 %attend_forward.5 = (bf16[640,768]{1,0:T(8,128)(2,1)S(1)}, f32[6,8,640]{2,1,0:T(8,128)S(1)}) custom-call(bf16[640,768]{1,0:T(8,128)(2,1)S(1)} %get-tuple-element.374.q_ref, bf16[640,768]{1,0:T(8,128)(2,1)S(1)} %slice.267.k_ref, bf16[640,768]{1,0:T(8,128)(2,1)S(1)} %get-tuple-element.373.v_ref), custom_call_target="tpu_custom_call" | custom-call | flops 1024 | bytes 1024 | tf_op jit(solution)/shard_map/attend_forward/pallas_call | solution.py:238
  231.9 17.5 %ffn_whole.3 = (bf16[640,3072]{1,0:T(8,128)(2,1)S(1)}, bf16[640,3072]{1,0:T(8,128)(2,1)}, bf16[640,768]{1,0:T(8,128)(2,1)S(1)}) custom-call(bf16[640,768]{1,0:T(8,128)(2,1)S(1)} %add_convert_fusion.mixed_ref, bf16[768,3072]{1,0:T(8,128)(2,1)} %copy-done, f32[1,3072]{1,0:T(1,128)S(1)} %bitcast.284, bf16[3072,768]{1,0:T(8,128)(2,1)} %copy-done.1, ...), custom_call_target="tpu_custom_call" | custom-call | flops 1024 | bytes 1024 | tf_op jit(solution)/shard_map/ffn_whole/pallas_call | solution.py:163
  253.2 2.5 copy-done.14
  255.7 10.5 %ffn_back.4 = (bf16[640,3072]{1,0:T(8,128)(2,1)S(1)}, f32[640,768]{1,0:T(8,128)S(1)}, f32[1,3072]{1,0:T(1,128)S(1)}) custom-call(bf16[640,768]{1,0:T(8,128)(2,1)S(1)} %get-tuple-element.364.grad_ref, bf16[3072,768]{1,0:T(8,128)(2,1)} %copy-done.1, bf16[640,3072]{1,0:T(8,128)(2,1)S(1)} %copy-done.14, bf16[768,3072]{1,0:T(8,128)(2,1)} %copy-done), custom_call_target="tpu_custom_call" | custom-call | flops 1024 | bytes 1024 | tf_op jit(solution)/shard_map/ffn_back/pallas_call | solution.py:212
  270.8 17.2 %attend_backward.4 = (bf16[640,768]{1,0:T(8,128)(2,1)S(1)}, bf16[640,768]{1,0:T(8,128)(2,1)S(1)}, bf16[640,768]{1,0:T(8,128)(2,1)S(1)}) custom-call(bf16[640,768]{1,0:T(8,128)(2,1)S(1)} %get-tuple-element.374.q_ref, bf16[640,768]{1,0:T(8,128)(2,1)S(1)} %slice.267.k_ref, bf16[640,768]{1,0:T(8,128)(2,1)S(1)} %get-tuple-element.373.v_ref, ...), custom_call_target="tpu_custom_call" | custom-call | flops 1024 | bytes 1024 | tf_op jit(solution)/shard_map/attend_backward/pallas_call | solution.py:260
  291.1 3.3 fusion.40
  300.3 21.4 %collective-permute-done.15 = bf16[640,768]{1,0:T(8,128)(2,1)} collective-permute-done((bf16[640,768]{1,0:T(8,128)(2,1)}, bf16[640,768]{1,0:T(8,128)(2,1)}, u32[]{:S(2)}, u32[]{:S(2)}) %collective-permute-start.15) | collective-permute-done | bytes 983072 | tf_op jit(solution)/shard_map/ppermute | solution.py:608
  325.2 7.4 %fusion.4 = bf16[3072,768]{1,0:T(8,128)(2,1)S(1)} fusion(bf16[1280,768]{1,0:T(8,128)(2,1)S(1)} %pad_maximum_fusion.5, bf16[640,3072]{1,0:T(8,128)(2,1)S(1)} %copy-done.34, bf16[640,3072]{1,0:T(8,128)(2,1)S(1)} %copy-done.36), kind=kOutput, calls=%fused_computation.6 | convolution fusion | flops 6057885696 | bytes 14548992 | tf_op jit(solution)/shard_map/dot_general | solution.py:25
  338.6 2.1 fusion.16
  340.9 2.1 fusion.15
  343.1 10.9 %ffn_back.5 = (bf16[640,3072]{1,0:T(8,128)(2,1)S(1)}, f32[640,768]{1,0:T(8,128)S(1)}, f32[1,3072]{1,0:T(1,128)S(1)}) custom-call(bf16[640,768]{1,0:T(8,128)(2,1)S(1)} %broadcast_select_fusion.grad_ref, bf16[3072,768]{1,0:T(8,128)(2,1)} %copy-done.1, bf16[640,3072]{1,0:T(8,128)(2,1)S(1)} %copy-done.3, bf16[768,3072]{1,0:T(8,128)(2,1)} %copy-done), custom_call_target="tpu_custom_call" | custom-call | flops 1024 | bytes 1024 | tf_op jit(solution)/shard_map/ffn_back/pallas_call | solution.py:212
  362.4 7.1 %pad_maximum_fusion = bf16[1280,3072]{1,0:T(8,128)(2,1)} fusion(bf16[640,3072]{1,0:T(8,128)(2,1)} %copy-done.22, bf16[640,3072]{1,0:T(8,128)(2,1)} %copy-done.21), kind=kLoop, calls=%fused_computation.4 | loop fusion | flops 15728640 | bytes 15728640 | tf_op jit(solution)/shard_map/concatenate | solution.py:666
  369.5 7.3 %collective-permute-done.17 = bf16[384,768]{1,0:T(8,128)(2,1)} collective-permute-done((bf16[384,768]{1,0:T(8,128)(2,1)}, bf16[384,768]{1,0:T(8,128)(2,1)}, u32[]{:S(2)}, u32[]{:S(2)}) %collective-permute-start.17) | collective-permute-done | bytes 589856 | tf_op jit(solution)/shard_map/ppermute | solution.py:406
  379.9 10.0 %convolution_convert_fusion.1 = bf16[768,3072]{1,0:T(8,128)(2,1)S(1)} fusion(bf16[1280,3072]{1,0:T(8,128)(2,1)} %pad_maximum_fusion, bf16[640,768]{1,0:T(8,128)(2,1)S(1)} %copy-done.16, bf16[640,768]{1,0:T(8,128)(2,1)S(1)} %copy-done.18), kind=kOutput, calls=%fused_computation.8 | convolution fusion | flops 6046089216 | bytes 14548992 | tf_op jit(solution)/shard_map/dot_general | solution.py:25
  394.0 2.6 collective-permute-start.26
  397.5 2.1 convert_reduce_fusion.5
  399.6 2.0 convolution_convert_fusion.2.g_ref
  401.6 2.8 fusion.81
  415.2 6.5 %collective-permute-done.24 = bf16[192,768]{1,0:T(8,128)(2,1)S(1)} collective-permute-done((bf16[192,768]{1,0:T(8,128)(2,1)S(1)}, bf16[192,768]{1,0:T(8,128)(2,1)S(1)}, u32[]{:S(2)}, u32[]{:S(2)}) %collective-permute-start.24) | collective-permute-done | bytes 294944 | tf_op jit(solution)/shard_map/ppermute | solution.py:406
  422.2 17.2 %attend_backward.5 = (bf16[640,768]{1,0:T(8,128)(2,1)S(1)}, bf16[640,768]{1,0:T(8,128)(2,1)S(1)}, bf16[640,768]{1,0:T(8,128)(2,1)S(1)}) custom-call(bf16[640,768]{1,0:T(8,128)(2,1)S(1)} %copy-done.11, bf16[640,768]{1,0:T(8,128)(2,1)S(1)} %copy-done.7, bf16[640,768]{1,0:T(8,128)(2,1)S(1)} %copy-done.9, f32[6,8,640]{2,1,0:T(8,128)S(1)} %get-tuple-element.176.lse_ref, ...), custom_call_target="tpu_custom_call" | custom-call | flops 1024 | bytes 1024 | tf_op jit(solution)/shard_map/attend_backward/pallas_call | solution.py:260
  443.8 2.3 pad_maximum_fusion.1
  451.1 5.3 convolution_convert_fusion
  467.5 2.2 fusion.89
  469.7 4.6 fusion.50
  477.7 3.2 fusion.54
  482.9 2.7 collective-permute-start.39
  490.6 11.3 %collective-permute-done.34 = bf16[48,3072]{1,0:T(8,128)(2,1)S(1)} collective-permute-done((bf16[48,3072]{1,0:T(8,128)(2,1)S(1)}, bf16[48,3072]{1,0:T(8,128)(2,1)S(1)}, u32[]{:S(2)}, u32[]{:S(2)}) %collective-permute-start.34) | collective-permute-done | bytes 294944 | tf_op jit(solution)/shard_map/ppermute | solution.py:406
  509.4 4.8 collective-permute-done.38
  514.3 2.9 collective-permute-start.40
  518.7 7.5 %collective-permute-done.42 = bf16[48,2304]{1,0:T(8,128)(2,1)S(1)} collective-permute-done((bf16[48,2304]{1,0:T(8,128)(2,1)S(1)}, bf16[48,2304]{1,0:T(8,128)(2,1)S(1)}, u32[]{:S(2)}, u32[]{:S(2)}) %collective-permute-start.42) | collective-permute-done | bytes 221216 | tf_op jit(solution)/shard_map/ppermute | solution.py:406
  526.3 10.9 %collective-permute-done.41 = bf16[48,3072]{1,0:T(8,128)(2,1)S(1)} collective-permute-done((bf16[48,3072]{1,0:T(8,128)(2,1)S(1)}, bf16[48,3072]{1,0:T(8,128)(2,1)S(1)}, u32[]{:S(2)}, u32[]{:S(2)}) %collective-permute-start.41) | collective-permute-done | bytes 294944 | tf_op jit(solution)/shard_map/ppermute | solution.py:406
  537.5 6.0 %collective-permute-done.47 = bf16[48,3072]{1,0:T(8,128)(2,1)S(1)} collective-permute-done((bf16[48,3072]{1,0:T(8,128)(2,1)S(1)}, bf16[48,3072]{1,0:T(8,128)(2,1)S(1)}, u32[]{:S(2)}, u32[]{:S(2)}) %collective-permute-start.47) | collective-permute-done | bytes 294944 | tf_op jit(solution)/shard_map/ppermute | solution.py:406
  548.3 8.0 %collective-permute-done.44 = bf16[112,768]{1,0:T(8,128)(2,1)S(1)} collective-permute-done((bf16[112,768]{1,0:T(8,128)(2,1)S(1)}, bf16[112,768]{1,0:T(8,128)(2,1)S(1)}, u32[]{:S(2)}, u32[]{:S(2)}) %collective-permute-start.44) | collective-permute-done | bytes 172064 | tf_op jit(solution)/shard_map/ppermute | solution.py:406
  556.9 10.0 %collective-permute-done.48 = bf16[112,768]{1,0:T(8,128)(2,1)S(1)} collective-permute-done((bf16[112,768]{1,0:T(8,128)(2,1)S(1)}, bf16[112,768]{1,0:T(8,128)(2,1)S(1)}, u32[]{:S(2)}, u32[]{:S(2)}) %collective-permute-start.48) | collective-permute-done | bytes 172064 | tf_op jit(solution)/shard_map/ppermute | solution.py:406
  568.4 4.9 collective-permute-done.50
  (501 shorter events, 153.0 us)
Async XLA Ops:
  1.7 8.0 %collective-permute-start.2 = (bf16[1,2304]{1,0:T(2,128)(2,1)S(1)}, bf16[1,2304]{1,0:T(2,128)(2,1)S(1)}, u32[]{:S(2)}, u32[]{:S(2)}) collective-permute-start(bf16[1,2304]{1,0:T(2,128)(2,1)S(1)} %concatenate.85), channel_id=1, source_target_pairs={{0,8},{4,12},{8,0},{12,4},{1,9},{5,13},{9,1},{13,5},{2,10},{6,14},... | collective-permute-start | bytes 13832 | tf_op jit(solution)/shard_map/ppermute | solution.py:406
  6.5 11.8 %collective-permute-start.1 = (bf16[96,2304]{1,0:T(8,128)(2,1)}, bf16[96,2304]{1,0:T(8,128)(2,1)S(1)}, u32[]{:S(2)}, u32[]{:S(2)}) collective-permute-start(bf16[96,2304]{1,0:T(8,128)(2,1)} %dynamic-slice_bitcast_fusion.13), channel_id=1, source_target_pairs={{0,8},{4,12},{8,0},{12,4},{1,9},{5,13},{9,1},{13,5},{2,10},{6,14},... | collective-permute-start | bytes 1327112 | tf_op jit(solution)/shard_map/ppermute | solution.py:406
  8.0 21.1 %copy-start.87 = (bf16[1,192,2304]{2,1,0:T(8,128)(2,1)S(1)}, bf16[1,192,2304]{2,1,0:T(8,128)(2,1)}, u32[]{:S(2)}) copy-start(bf16[1,192,2304]{2,1,0:T(8,128)(2,1)} %param.21) | copy-start | bytes 2654212
  9.8 1.3 collective-permute-start.3
  18.4 10.7 %collective-permute-start.4 = (bf16[96,2304]{1,0:T(8,128)(2,1)S(1)}, bf16[96,2304]{1,0:T(8,128)(2,1)S(1)}, u32[]{:S(2)}, u32[]{:S(2)}) collective-permute-start(bf16[96,2304]{1,0:T(8,128)(2,1)S(1)} %collective-permute-done.1), channel_id=1, source_target_pairs={{0,1},{1,0},{2,3},{3,2},{4,5},{5,4},{6,7},{7,6},{8,9},{9,8},{10,11... | collective-permute-start | bytes 1327112 | tf_op jit(solution)/shard_map/ppermute | solution.py:406
  29.2 3.8 collective-permute-start.5
  30.2 16.0 %collective-permute-start = (bf16[96,3072]{1,0:T(8,128)(2,1)}, bf16[96,3072]{1,0:T(8,128)(2,1)}, u32[]{:S(2)}, u32[]{:S(2)}) collective-permute-start(bf16[96,3072]{1,0:T(8,128)(2,1)} %dynamic-slice_bitcast_fusion.10), channel_id=1, source_target_pairs={{0,8},{4,12},{8,0},{12,4},{1,9},{5,13},{9,1},{13,5},{2,10},{6,14},... | collective-permute-start | bytes 1769480 | tf_op jit(solution)/shard_map/ppermute | solution.py:406
  46.2 15.1 %collective-permute-start.9 = (bf16[96,3072]{1,0:T(8,128)(2,1)}, bf16[96,3072]{1,0:T(8,128)(2,1)S(1)}, u32[]{:S(2)}, u32[]{:S(2)}) collective-permute-start(bf16[96,3072]{1,0:T(8,128)(2,1)} %collective-permute-done), channel_id=1, source_target_pairs={{0,1},{1,0},{2,3},{3,2},{4,5},{5,4},{6,7},{7,6},{8,9},{9,8},{10,11... | collective-permute-start | bytes 1769480 | tf_op jit(solution)/shard_map/ppermute | solution.py:406
  47.8 11.2 %collective-permute-start.6 = (bf16[192,768]{1,0:T(8,128)(2,1)S(1)}, bf16[192,768]{1,0:T(8,128)(2,1)S(1)}, u32[]{:S(2)}, u32[]{:S(2)}) collective-permute-start(bf16[192,768]{1,0:T(8,128)(2,1)S(1)} %bitcast.324), channel_id=1, source_target_pairs={{0,8},{4,12},{8,0},{12,4},{1,9},{5,13},{9,1},{13,5},{2,10},{6,14},... | collective-permute-start | bytes 884744 | tf_op jit(solution)/shard_map/ppermute | solution.py:406
  62.6 12.9 %collective-permute-start.10 = (bf16[384,3072]{1,0:T(8,128)(2,1)S(1)}, bf16[384,3072]{1,0:T(8,128)(2,1)}, u32[]{:S(2)}, u32[]{:S(2)}) collective-permute-start(bf16[384,3072]{1,0:T(8,128)(2,1)S(1)} %pad_maximum_fusion.2.here_ref), channel_id=1, source_target_pairs={{0,4},{4,0},{8,12},{12,8},{1,5},{5,1},{9,13},{13,9},{2,6},{6,2},{1... | collective-permute-start | bytes 7077896 | tf_op jit(solution)/shard_map/ppermute | solution.py:406
  62.7 6.6 %collective-permute-start.7 = (bf16[384,768]{1,0:T(8,128)(2,1)S(1)}, bf16[384,768]{1,0:T(8,128)(2,1)S(1)}, u32[]{:S(2)}, u32[]{:S(2)}) collective-permute-start(bf16[384,768]{1,0:T(8,128)(2,1)S(1)} %pad_maximum_fusion.7.here_ref), channel_id=1, source_target_pairs={{0,4},{4,0},{8,12},{12,8},{1,5},{5,1},{9,13},{13,9},{2,6},{6,2},{1... | collective-permute-start | bytes 1769480 | tf_op jit(solution)/shard_map/ppermute | solution.py:406
  63.3 28.3 %collective-permute-start.8 = (bf16[768,768]{1,0:T(8,128)(2,1)}, bf16[768,768]{1,0:T(8,128)(2,1)}, u32[]{:S(2)}, u32[]{:S(2)}) collective-permute-start(bf16[768,768]{1,0:T(8,128)(2,1)} %bitcast.25), channel_id=1, source_target_pairs={{0,8},{4,12},{8,0},{12,4},{1,9},{5,13},{9,1},{13,5},{2,10},{6,14},... | collective-permute-start | bytes 3538952 | tf_op jit(solution)/shard_map/ppermute | solution.py:406
  93.4 4.7 collective-permute-start.11
  105.0 25.0 %collective-permute-start.12 = (bf16[640,768]{1,0:T(8,128)(2,1)}, bf16[640,768]{1,0:T(8,128)(2,1)S(1)}, u32[]{:S(2)}, u32[]{:S(2)}) collective-permute-start(bf16[640,768]{1,0:T(8,128)(2,1)} %add_convert_fusion.2), channel_id=1, source_target_pairs={{0,16},{1,17},{2,18},{3,19},{4,20},{5,21},{6,22},{7,23},{8,24},{9,... | collective-permute-start | bytes 2949128 | tf_op jit(solution)/shard_map/ppermute | solution.py:605
  108.6 21.3 %copy-start.56 = (bf16[2,1,640,768]{3,2,1,0:T(8,128)(2,1)S(1)}, bf16[2,1,640,768]{3,2,1,0:T(8,128)(2,1)}, u32[]{:S(2)}) copy-start(bf16[2,1,640,768]{3,2,1,0:T(8,128)(2,1)} %param.16) | copy-start | bytes 5898244
  111.9 18.9 %copy-start.98 = (f32[768]{0:T(1024)S(1)}, f32[768]{0:T(1024)}, u32[]{:S(2)}) copy-start(f32[768]{0:T(1024)} %copy-done.97) | copy-start | bytes 9220
  111.9 18.9 %copy-start.105 = (f32[768]{0:T(1024)S(1)}, f32[768]{0:T(1024)}, u32[]{:S(2)}) copy-start(f32[768]{0:T(1024)} %copy-done.104) | copy-start | bytes 9220
  130.4 80.8 %copy-start.99 = (f32[640]{0:T(1024)}, f32[640]{0:T(1024)S(1)}, u32[]{:S(2)}) copy-start(f32[640]{0:T(1024)S(1)} %broadcast_multiply_fusion.15) | copy-start | bytes 7684
  130.8 80.3 %copy-start.102 = (f32[640]{0:T(1024)}, f32[640]{0:T(1024)S(1)}, u32[]{:S(2)}) copy-start(f32[640]{0:T(1024)S(1)} %add_rsqrt_fusion.3) | copy-start | bytes 7684
  135.5 55.6 %copy-start.6 = (bf16[640,768]{1,0:T(8,128)(2,1)}, bf16[640,768]{1,0:T(8,128)(2,1)S(1)}, u32[]{:S(2)}) copy-start(bf16[640,768]{1,0:T(8,128)(2,1)S(1)} %slice.268.k_ref) | copy-start | bytes 2949124
  135.9 55.2 %copy-start.8 = (bf16[640,768]{1,0:T(8,128)(2,1)}, bf16[640,768]{1,0:T(8,128)(2,1)S(1)}, u32[]{:S(2)}) copy-start(bf16[640,768]{1,0:T(8,128)(2,1)S(1)} %get-tuple-element.375.v_ref) | copy-start | bytes 2949124
  135.9 55.2 %copy-start.10 = (bf16[640,768]{1,0:T(8,128)(2,1)}, bf16[640,768]{1,0:T(8,128)(2,1)S(1)}, u32[]{:S(2)}) copy-start(bf16[640,768]{1,0:T(8,128)(2,1)S(1)} %get-tuple-element.376.q_ref) | copy-start | bytes 2949124
  168.5 46.3 %collective-permute-start.13 = (bf16[640,768]{1,0:T(8,128)(2,1)}, bf16[640,768]{1,0:T(8,128)(2,1)}, u32[]{:S(2)}, u32[]{:S(2)}) collective-permute-start(bf16[640,768]{1,0:T(8,128)(2,1)} %get-tuple-element.173), channel_id=1, source_target_pairs={{0,16},{1,17},{2,18},{3,19},{4,20},{5,21},{6,22},{7,23},{8,24},{9,... | collective-permute-start | bytes 2949128 | tf_op jit(solution)/shard_map/ppermute | solution.py:605
  213.5 37.8 %collective-permute-start.14 = (bf16[640,768]{1,0:T(8,128)(2,1)}, bf16[640,768]{1,0:T(8,128)(2,1)}, u32[]{:S(2)}, u32[]{:S(2)}) collective-permute-start(bf16[640,768]{1,0:T(8,128)(2,1)} %fusion.48), channel_id=1, source_target_pairs={{16,0},{17,1},{18,2},{19,3},{20,4},{21,5},{22,6},{23,7},{24,8},{25... | collective-permute-start | bytes 2949128 | tf_op jit(solution)/shard_map/ppermute | solution.py:608
  231.9 19.4 %copy-start.53 = (bf16[2,640,768]{2,1,0:T(8,128)(2,1)S(1)}, bf16[2,640,768]{2,1,0:T(8,128)(2,1)}, u32[]{:S(2)}) copy-start(bf16[2,640,768]{2,1,0:T(8,128)(2,1)} %bitcast_multiply_fusion) | copy-start | bytes 5898244
  296.0 25.7 %collective-permute-start.15 = (bf16[640,768]{1,0:T(8,128)(2,1)}, bf16[640,768]{1,0:T(8,128)(2,1)}, u32[]{:S(2)}, u32[]{:S(2)}) collective-permute-start(bf16[640,768]{1,0:T(8,128)(2,1)} %fusion.39), channel_id=1, source_target_pairs={{16,0},{17,1},{18,2},{19,3},{20,4},{21,5},{22,6},{23,7},{24,8},{25... | collective-permute-start | bytes 2949128 | tf_op jit(solution)/shard_map/ppermute | solution.py:608
  297.4 24.4 %copy-start.54 = (bf16[2,640,768]{2,1,0:T(8,128)(2,1)S(1)}, bf16[2,640,768]{2,1,0:T(8,128)(2,1)}, u32[]{:S(2)}) copy-start(bf16[2,640,768]{2,1,0:T(8,128)(2,1)} %bitcast_multiply_fusion) | copy-start | bytes 5898244
  298.8 24.4 %copy-start.36 = (bf16[640,3072]{1,0:T(8,128)(2,1)S(1)}, bf16[640,3072]{1,0:T(8,128)(2,1)}, u32[]{:S(2)}) copy-start(bf16[640,3072]{1,0:T(8,128)(2,1)} %copy-done.35) | copy-start | bytes 11796484
  300.3 22.8 %copy-start.5 = (bf16[640,768]{1,0:T(8,128)(2,1)S(1)}, bf16[640,768]{1,0:T(8,128)(2,1)}, u32[]{:S(2)}) copy-start(bf16[640,768]{1,0:T(8,128)(2,1)} %copy-done.4) | copy-start | bytes 2949124
  334.1 4.5 collective-permute-start.16
  335.7 4.9 collective-permute-start.18
  360.4 16.4 %collective-permute-start.17 = (bf16[384,768]{1,0:T(8,128)(2,1)}, bf16[384,768]{1,0:T(8,128)(2,1)}, u32[]{:S(2)}, u32[]{:S(2)}) collective-permute-start(bf16[384,768]{1,0:T(8,128)(2,1)} %dynamic-slice_bitcast_fusion.9), channel_id=1, source_target_pairs={{0,8},{4,12},{8,0},{12,4},{1,9},{5,13},{9,1},{13,5},{2,10},{6,14},... | collective-permute-start | bytes 1769480 | tf_op jit(solution)/shard_map/ppermute | solution.py:406
  360.9 49.8 %collective-permute-start.23 = (bf16[384,768]{1,0:T(8,128)(2,1)}, bf16[384,768]{1,0:T(8,128)(2,1)}, u32[]{:S(2)}, u32[]{:S(2)}) collective-permute-start(bf16[384,768]{1,0:T(8,128)(2,1)} %dynamic-slice_bitcast_fusion.7), channel_id=1, source_target_pairs={{0,8},{4,12},{8,0},{12,4},{1,9},{5,13},{9,1},{13,5},{2,10},{6,14},... | collective-permute-start | bytes 1769480 | tf_op jit(solution)/shard_map/ppermute | solution.py:406
  378.3 14.9 %collective-permute-start.19 = (bf16[192,768]{1,0:T(8,128)(2,1)S(1)}, bf16[192,768]{1,0:T(8,128)(2,1)S(1)}, u32[]{:S(2)}, u32[]{:S(2)}) collective-permute-start(bf16[192,768]{1,0:T(8,128)(2,1)S(1)} %dynamic-slice_bitcast_fusion.18), channel_id=1, source_target_pairs={{0,1},{1,0},{2,3},{3,2},{4,5},{5,4},{6,7},{7,6},{8,9},{9,8},{10,11... | collective-permute-start | bytes 884744 | tf_op jit(solution)/shard_map/ppermute | solution.py:406
  391.6 14.8 %collective-permute-start.21 = (bf16[2,96,3072]{2,1,0:T(8,128)(2,1)}, bf16[2,96,3072]{2,1,0:T(8,128)(2,1)}, u32[]{:S(2)}, u32[]{:S(2)}) collective-permute-start(bf16[2,96,3072]{2,1,0:T(8,128)(2,1)} %dynamic-slice_bitcast_fusion), channel_id=1, source_target_pairs={{0,4},{4,0},{8,12},{12,8},{1,5},{5,1},{9,13},{13,9},{2,6},{6,2},{1... | collective-permute-start | bytes 3538952 | tf_op jit(solution)/shard_map/ppermute | solution.py:406
  393.2 15.6 %collective-permute-start.20 = (bf16[2,96,3072]{2,1,0:T(8,128)(2,1)}, bf16[2,96,3072]{2,1,0:T(8,128)(2,1)}, u32[]{:S(2)}, u32[]{:S(2)}) collective-permute-start(bf16[2,96,3072]{2,1,0:T(8,128)(2,1)} %dynamic-slice_bitcast_fusion.1), channel_id=1, source_target_pairs={{0,4},{4,0},{8,12},{12,8},{1,5},{5,1},{9,13},{13,9},{2,6},{6,2},{1... | collective-permute-start | bytes 3538952 | tf_op jit(solution)/shard_map/ppermute | solution.py:406
  394.0 53.5 %collective-permute-start.26 = (bf16[192,768]{1,0:T(8,128)(2,1)}, bf16[192,768]{1,0:T(8,128)(2,1)}, u32[]{:S(2)}, u32[]{:S(2)}) collective-permute-start(bf16[192,768]{1,0:T(8,128)(2,1)} %fusion.106), channel_id=1, source_target_pairs={{0,2},{1,3},{2,0},{3,1},{4,6},{5,7},{6,4},{7,5},{8,10},{9,11},{10,... | collective-permute-start | bytes 884744 | tf_op jit(solution)/shard_map/ppermute | solution.py:406
  408.3 37.9 %collective-permute-start.27 = (bf16[96,3072]{1,0:T(8,128)(2,1)S(1)}, bf16[96,3072]{1,0:T(8,128)(2,1)}, u32[]{:S(2)}, u32[]{:S(2)}) collective-permute-start(bf16[96,3072]{1,0:T(8,128)(2,1)S(1)} %dynamic-slice_bitcast_fusion.6), channel_id=1, source_target_pairs={{0,8},{4,12},{8,0},{12,4},{1,9},{5,13},{9,1},{13,5},{2,10},{6,14},... | collective-permute-start | bytes 1769480 | tf_op jit(solution)/shard_map/ppermute | solution.py:406
  412.4 9.2 %collective-permute-start.24 = (bf16[192,768]{1,0:T(8,128)(2,1)S(1)}, bf16[192,768]{1,0:T(8,128)(2,1)S(1)}, u32[]{:S(2)}, u32[]{:S(2)}) collective-permute-start(bf16[192,768]{1,0:T(8,128)(2,1)S(1)} %dynamic-slice_bitcast_fusion.17), channel_id=1, source_target_pairs={{0,1},{1,0},{2,3},{3,2},{4,5},{5,4},{6,7},{7,6},{8,9},{9,8},{10,11... | collective-permute-start | bytes 884744 | tf_op jit(solution)/shard_map/ppermute | solution.py:406
  413.8 53.7 %collective-permute-start.22 = (bf16[96,3072]{1,0:T(8,128)(2,1)}, bf16[96,3072]{1,0:T(8,128)(2,1)}, u32[]{:S(2)}, u32[]{:S(2)}) collective-permute-start(bf16[96,3072]{1,0:T(8,128)(2,1)} %dynamic-slice_bitcast_fusion.8), channel_id=1, source_target_pairs={{0,8},{4,12},{8,0},{12,4},{1,9},{5,13},{9,1},{13,5},{2,10},{6,14},... | collective-permute-start | bytes 1769480 | tf_op jit(solution)/shard_map/ppermute | solution.py:406
  421.7 27.6 %collective-permute-start.25 = (bf16[192,768]{1,0:T(8,128)(2,1)S(1)}, bf16[192,768]{1,0:T(8,128)(2,1)}, u32[]{:S(2)}, u32[]{:S(2)}) collective-permute-start(bf16[192,768]{1,0:T(8,128)(2,1)S(1)} %fusion.105), channel_id=1, source_target_pairs={{0,2},{1,3},{2,0},{3,1},{4,6},{5,7},{6,4},{7,5},{8,10},{9,11},{10,... | collective-permute-start | bytes 884744 | tf_op jit(solution)/shard_map/ppermute | solution.py:406
  458.8 3.9 collective-permute-start.29
  459.4 42.6 %collective-permute-start.32 = (bf16[192,768]{1,0:T(8,128)(2,1)}, bf16[192,768]{1,0:T(8,128)(2,1)}, u32[]{:S(2)}, u32[]{:S(2)}) collective-permute-start(bf16[192,768]{1,0:T(8,128)(2,1)} %add_convert_fusion.6), channel_id=1, source_target_pairs={{0,1},{1,0},{2,3},{3,2},{4,5},{5,4},{6,7},{7,6},{8,9},{9,8},{10,11... | collective-permute-start | bytes 884744 | tf_op jit(solution)/shard_map/ppermute | solution.py:406
  459.9 42.0 %collective-permute-start.33 = (bf16[192,768]{1,0:T(8,128)(2,1)}, bf16[192,768]{1,0:T(8,128)(2,1)}, u32[]{:S(2)}, u32[]{:S(2)}) collective-permute-start(bf16[192,768]{1,0:T(8,128)(2,1)} %add_convert_fusion.7), channel_id=1, source_target_pairs={{0,1},{1,0},{2,3},{3,2},{4,5},{5,4},{6,7},{7,6},{8,9},{9,8},{10,11... | collective-permute-start | bytes 884744 | tf_op jit(solution)/shard_map/ppermute | solution.py:406
  462.2 19.6 %collective-permute-start.36 = (bf16[48,3072]{1,0:T(8,128)(2,1)}, bf16[48,3072]{1,0:T(8,128)(2,1)}, u32[]{:S(2)}, u32[]{:S(2)}) collective-permute-start(bf16[48,3072]{1,0:T(8,128)(2,1)} %dynamic-slice_bitcast_fusion.15), channel_id=1, source_target_pairs={{0,1},{1,0},{2,3},{3,2},{4,5},{5,4},{6,7},{7,6},{8,9},{9,8},{10,11... | collective-permute-start | bytes 884744 | tf_op jit(solution)/shard_map/ppermute | solution.py:406
  462.7 2.5 collective-permute-start.28
  465.2 23.2 %collective-permute-start.35 = (bf16[96,2304]{1,0:T(8,128)(2,1)}, bf16[96,2304]{1,0:T(8,128)(2,1)}, u32[]{:S(2)}, u32[]{:S(2)}) collective-permute-start(bf16[96,2304]{1,0:T(8,128)(2,1)} %dynamic-slice_bitcast_fusion.11), channel_id=1, source_target_pairs={{0,8},{4,12},{8,0},{12,4},{1,9},{5,13},{9,1},{13,5},{2,10},{6,14},... | collective-permute-start | bytes 1327112 | tf_op jit(solution)/shard_map/ppermute | solution.py:406
  482.9 25.5 %collective-permute-start.39 = (bf16[48,3072]{1,0:T(8,128)(2,1)S(1)}, bf16[48,3072]{1,0:T(8,128)(2,1)S(1)}, u32[]{:S(2)}, u32[]{:S(2)}) collective-permute-start(bf16[48,3072]{1,0:T(8,128)(2,1)S(1)} %fusion.104), channel_id=1, source_target_pairs={{0,2},{1,3},{2,0},{3,1},{4,6},{5,7},{6,4},{7,5},{8,10},{9,11},{10,... | collective-permute-start | bytes 884744 | tf_op jit(solution)/shard_map/ppermute | solution.py:406
  487.5 14.3 %collective-permute-start.34 = (bf16[48,3072]{1,0:T(8,128)(2,1)S(1)}, bf16[48,3072]{1,0:T(8,128)(2,1)S(1)}, u32[]{:S(2)}, u32[]{:S(2)}) collective-permute-start(bf16[48,3072]{1,0:T(8,128)(2,1)S(1)} %dynamic-slice_bitcast_fusion.16), channel_id=1, source_target_pairs={{0,1},{1,0},{2,3},{3,2},{4,5},{5,4},{6,7},{7,6},{8,9},{9,8},{10,11... | collective-permute-start | bytes 884744 | tf_op jit(solution)/shard_map/ppermute | solution.py:406
  488.5 14.6 %collective-permute-start.31 = (bf16[96,2304]{1,0:T(8,128)(2,1)S(1)}, bf16[96,2304]{1,0:T(8,128)(2,1)S(1)}, u32[]{:S(2)}, u32[]{:S(2)}) collective-permute-start(bf16[96,2304]{1,0:T(8,128)(2,1)S(1)} %dynamic-slice_bitcast_fusion.12), channel_id=1, source_target_pairs={{0,8},{4,12},{8,0},{12,4},{1,9},{5,13},{9,1},{13,5},{2,10},{6,14},... | collective-permute-start | bytes 1327112 | tf_op jit(solution)/shard_map/ppermute | solution.py:406
  501.8 6.3 %collective-permute-start.30 = (bf16[2,224,768]{2,1,0:T(8,128)(2,1)S(1)}, bf16[2,224,768]{2,1,0:T(8,128)(2,1)S(1)}, u32[]{:S(2)}, u32[]{:S(2)}) collective-permute-start(bf16[2,224,768]{2,1,0:T(8,128)(2,1)S(1)} %fusion.99), channel_id=1, source_target_pairs={{0,4},{4,0},{8,12},{12,8},{1,5},{5,1},{9,13},{13,9},{2,6},{6,2},{1... | collective-permute-start | bytes 2064392 | tf_op jit(solution)/shard_map/ppermute | solution.py:406
  501.9 16.6 %collective-permute-start.43 = (bf16[48,3072]{1,0:T(8,128)(2,1)S(1)}, bf16[48,3072]{1,0:T(8,128)(2,1)S(1)}, u32[]{:S(2)}, u32[]{:S(2)}) collective-permute-start(bf16[48,3072]{1,0:T(8,128)(2,1)S(1)} %fusion.103), channel_id=1, source_target_pairs={{0,2},{1,3},{2,0},{3,1},{4,6},{5,7},{6,4},{7,5},{8,10},{9,11},{10,... | collective-permute-start | bytes 884744 | tf_op jit(solution)/shard_map/ppermute | solution.py:406
  502.1 12.1 %collective-permute-start.38 = (bf16[48,2304]{1,0:T(8,128)(2,1)S(1)}, bf16[48,2304]{1,0:T(8,128)(2,1)S(1)}, u32[]{:S(2)}, u32[]{:S(2)}) collective-permute-start(bf16[48,2304]{1,0:T(8,128)(2,1)S(1)} %dynamic-slice_bitcast_fusion.20), channel_id=1, source_target_pairs={{0,1},{1,0},{2,3},{3,2},{4,5},{5,4},{6,7},{7,6},{8,9},{9,8},{10,11... | collective-permute-start | bytes 663560 | tf_op jit(solution)/shard_map/ppermute | solution.py:406
  503.2 22.9 %collective-permute-start.42 = (bf16[48,2304]{1,0:T(8,128)(2,1)S(1)}, bf16[48,2304]{1,0:T(8,128)(2,1)S(1)}, u32[]{:S(2)}, u32[]{:S(2)}) collective-permute-start(bf16[48,2304]{1,0:T(8,128)(2,1)S(1)} %dynamic-slice_bitcast_fusion.19), channel_id=1, source_target_pairs={{0,1},{1,0},{2,3},{3,2},{4,5},{5,4},{6,7},{7,6},{8,9},{9,8},{10,11... | collective-permute-start | bytes 663560 | tf_op jit(solution)/shard_map/ppermute | solution.py:406
  508.4 28.8 %collective-permute-start.41 = (bf16[48,3072]{1,0:T(8,128)(2,1)S(1)}, bf16[48,3072]{1,0:T(8,128)(2,1)S(1)}, u32[]{:S(2)}, u32[]{:S(2)}) collective-permute-start(bf16[48,3072]{1,0:T(8,128)(2,1)S(1)} %add_convert_fusion.5), channel_id=1, source_target_pairs={{0,1},{1,0},{2,3},{3,2},{4,5},{5,4},{6,7},{7,6},{8,9},{9,8},{10,11... | collective-permute-start | bytes 884744 | tf_op jit(solution)/shard_map/ppermute | solution.py:406
  514.3 23.0 %collective-permute-start.40 = (bf16[48,2304]{1,0:T(8,128)(2,1)S(1)}, bf16[48,2304]{1,0:T(8,128)(2,1)S(1)}, u32[]{:S(2)}, u32[]{:S(2)}) collective-permute-start(bf16[48,2304]{1,0:T(8,128)(2,1)S(1)} %fusion.108), channel_id=1, source_target_pairs={{0,2},{1,3},{2,0},{3,1},{4,6},{5,7},{6,4},{7,5},{8,10},{9,11},{10,... | collective-permute-start | bytes 663560 | tf_op jit(solution)/shard_map/ppermute | solution.py:406
  517.2 20.2 %collective-permute-start.37 = (bf16[224,768]{1,0:T(8,128)(2,1)S(1)}, bf16[224,768]{1,0:T(8,128)(2,1)S(1)}, u32[]{:S(2)}, u32[]{:S(2)}) collective-permute-start(bf16[224,768]{1,0:T(8,128)(2,1)S(1)} %dynamic-slice_bitcast_fusion.14), channel_id=1, source_target_pairs={{0,8},{4,12},{8,0},{12,4},{1,9},{5,13},{9,1},{13,5},{2,10},{6,14},... | collective-permute-start | bytes 1032200 | tf_op jit(solution)/shard_map/ppermute | solution.py:406
  518.6 25.0 %collective-permute-start.47 = (bf16[48,3072]{1,0:T(8,128)(2,1)S(1)}, bf16[48,3072]{1,0:T(8,128)(2,1)S(1)}, u32[]{:S(2)}, u32[]{:S(2)}) collective-permute-start(bf16[48,3072]{1,0:T(8,128)(2,1)S(1)} %add_convert_fusion.4), channel_id=1, source_target_pairs={{0,1},{1,0},{2,3},{3,2},{4,5},{5,4},{6,7},{7,6},{8,9},{9,8},{10,11... | collective-permute-start | bytes 884744 | tf_op jit(solution)/shard_map/ppermute | solution.py:406
  526.2 17.3 %collective-permute-start.46 = (bf16[48,2304]{1,0:T(8,128)(2,1)S(1)}, bf16[48,2304]{1,0:T(8,128)(2,1)S(1)}, u32[]{:S(2)}, u32[]{:S(2)}) collective-permute-start(bf16[48,2304]{1,0:T(8,128)(2,1)S(1)} %fusion.107), channel_id=1, source_target_pairs={{0,2},{1,3},{2,0},{3,1},{4,6},{5,7},{6,4},{7,5},{8,10},{9,11},{10,... | collective-permute-start | bytes 663560 | tf_op jit(solution)/shard_map/ppermute | solution.py:406
  537.3 11.0 %collective-permute-start.45 = (bf16[48,2304]{1,0:T(8,128)(2,1)S(1)}, bf16[48,2304]{1,0:T(8,128)(2,1)S(1)}, u32[]{:S(2)}, u32[]{:S(2)}) collective-permute-start(bf16[48,2304]{1,0:T(8,128)(2,1)S(1)} %add_convert_fusion.9), channel_id=1, source_target_pairs={{0,1},{1,0},{2,3},{3,2},{4,5},{5,4},{6,7},{7,6},{8,9},{9,8},{10,11... | collective-permute-start | bytes 663560 | tf_op jit(solution)/shard_map/ppermute | solution.py:406
  543.6 13.2 %collective-permute-start.49 = (bf16[48,2304]{1,0:T(8,128)(2,1)S(1)}, bf16[48,2304]{1,0:T(8,128)(2,1)S(1)}, u32[]{:S(2)}, u32[]{:S(2)}) collective-permute-start(bf16[48,2304]{1,0:T(8,128)(2,1)S(1)} %add_convert_fusion.8), channel_id=1, source_target_pairs={{0,1},{1,0},{2,3},{3,2},{4,5},{5,4},{6,7},{7,6},{8,9},{9,8},{10,11... | collective-permute-start | bytes 663560 | tf_op jit(solution)/shard_map/ppermute | solution.py:406
  544.1 12.2 %collective-permute-start.44 = (bf16[112,768]{1,0:T(8,128)(2,1)S(1)}, bf16[112,768]{1,0:T(8,128)(2,1)S(1)}, u32[]{:S(2)}, u32[]{:S(2)}) collective-permute-start(bf16[112,768]{1,0:T(8,128)(2,1)S(1)} %dynamic-slice_bitcast_fusion.21), channel_id=1, source_target_pairs={{0,1},{1,0},{2,3},{3,2},{4,5},{5,4},{6,7},{7,6},{8,9},{9,8},{10,11... | collective-permute-start | bytes 516104 | tf_op jit(solution)/shard_map/ppermute | solution.py:406
  556.4 10.6 %collective-permute-start.48 = (bf16[112,768]{1,0:T(8,128)(2,1)S(1)}, bf16[112,768]{1,0:T(8,128)(2,1)S(1)}, u32[]{:S(2)}, u32[]{:S(2)}) collective-permute-start(bf16[112,768]{1,0:T(8,128)(2,1)S(1)} %fusion.109), channel_id=1, source_target_pairs={{0,2},{1,3},{2,0},{3,1},{4,6},{5,7},{6,4},{7,5},{8,10},{9,11},{10,... | collective-permute-start | bytes 516104 | tf_op jit(solution)/shard_map/ppermute | solution.py:406
  567.0 6.4 %collective-permute-start.50 = (bf16[112,768]{1,0:T(8,128)(2,1)S(1)}, bf16[112,768]{1,0:T(8,128)(2,1)S(1)}, u32[]{:S(2)}, u32[]{:S(2)}) collective-permute-start(bf16[112,768]{1,0:T(8,128)(2,1)S(1)} %add_convert_fusion.10), channel_id=1, source_target_pairs={{0,1},{1,0},{2,3},{3,2},{4,5},{5,4},{6,7},{7,6},{8,9},{9,8},{10,11... | collective-permute-start | bytes 516104 | tf_op jit(solution)/shard_map/ppermute | solution.py:406
  (103 other events, 595.2 us)
